TPU v7x, 32 devices: a whole 2x2x4 slice. The times are simulated.
32 devices in a mesh: dp: 2 (over y), blocks: 16 (over z, x, core).
Axes of the slice: x: 2, y: 2, z: 4, core: 2. Of those that a mesh axis runs over, the one named last changes fastest.
Arguments:
- tokens: bfloat16 [4096, 8192], P('blocks', 'dp'), may hold values from -6 to 6
- dec_bias: float32 [8192], P('dp'), may hold values from -3 to 3
- routes: int32 [4096, 2], P('blocks'), may hold values from 0 to 15, all different within a row; in each aligned block of 256 rows (0 to 255, 256 to 511, ...) at most 64 rows name the same one
- latent_picks: int32 [4096, 2, 16], P('blocks'), may hold values from 0 to 1023
- enc_weight: bfloat16 [16, 8192, 1024], P('blocks', 'dp'), may hold values from -0.0625 to 0.0625
- dec_weight: bfloat16 [16, 1024, 8192], P('blocks', None, 'dp'), may hold values from -1 to 1
- enc_bias: float32 [16, 1024], P('blocks'), may hold values from -3 to 3
Outputs:
- reconstruction: bfloat16 [4096, 8192], P('blocks', 'dp')
Inputs may be any that keep to these rules, and one draw needn't show every extreme that they name: `routes`: each row names 2 different blocks; among the rows of one index of blocks no block is named by more than 64 rows, and some block by exactly 64. `latent_picks`: indices within a block; a row may name an index more than once.
All inputs are finite; a program needn't handle non-finite values.
Results may differ from a plain program's by a relative error of at most 0.0059.
Values may be sent and summed in bfloat16 or wider, within the bound.
No kernel may reach another device: no remote copies, remote signals or barrier semaphores. Data moves between devices by JAX's collectives and lax.ppermute only.
A program may use at most 64 MiB of HBM per device.

v0:
```python
import jax
import jax.numpy as jnp
from jax import lax
from jax.sharding import PartitionSpec as P


def on_device(tokens, dec_bias, routes, latent_picks, enc_weight, dec_weight, enc_bias):
    tok_rows, quarter = tokens.shape
    top_blocks = routes.shape[1]
    pick_count = latent_picks.shape[2]
    latents = enc_weight.shape[2]
    blk_count = lax.axis_size("blocks")
    capacity = max(2, 2 * tok_rows * top_blocks // blk_count)
    slot_count = blk_count * capacity
    pair_count = tok_rows * top_blocks
    centered = (tokens.astype(jnp.float32) - dec_bias).astype(jnp.bfloat16)
    owners = routes.reshape(pair_count)
    onehot = (owners[:, None] == jnp.arange(blk_count, dtype=jnp.int32)[None, :]).astype(jnp.int32)
    slot_rank = jnp.sum(jnp.cumsum(onehot, axis=0) * onehot, axis=1) - 1
    target = owners * capacity + slot_rank
    placing = jnp.arange(slot_count, dtype=jnp.int32)[:, None] == target[None, :]
    place_half = placing.astype(jnp.bfloat16)
    paired = jnp.repeat(centered, top_blocks, axis=0)
    outgoing = jnp.dot(place_half, paired, preferred_element_type=jnp.float32).astype(jnp.bfloat16)
    outgoing = outgoing.reshape(blk_count, capacity, quarter)
    sent_picks = jnp.dot(
        placing.astype(jnp.float32),
        latent_picks.reshape(pair_count, pick_count).astype(jnp.float32),
        precision=lax.Precision.HIGHEST,
    ).astype(jnp.int32)
    sent_picks = sent_picks.reshape(blk_count, capacity, pick_count)
    enc_local = enc_weight[0]
    dec_local = dec_weight[0]
    bias_local = enc_bias[0]
    lat_ids = jnp.arange(latents, dtype=jnp.int32)
    arrived = lax.all_to_all(outgoing, "blocks", split_axis=0, concat_axis=0, tiled=True)
    chosen = lax.all_to_all(sent_picks, "blocks", split_axis=0, concat_axis=0, tiled=True)
    item_count = arrived.shape[1]
    flat_rows = arrived.reshape(blk_count * item_count, quarter)
    chosen_ids = chosen.reshape(blk_count * item_count, pick_count)
    partial_value = jnp.dot(flat_rows, enc_local, preferred_element_type=jnp.float32)
    summed = lax.psum(partial_value, "dp") + bias_local[None, :]
    keep_mask = jnp.any(chosen_ids[:, :, None] == lat_ids[None, None, :], axis=1)
    active = jnp.where(keep_mask, jnp.maximum(summed, 0.0), 0.0).astype(jnp.bfloat16)
    partial_out = jnp.dot(active, dec_local, preferred_element_type=jnp.float32).astype(
        jnp.bfloat16
    )
    partial_out = partial_out.reshape(blk_count, item_count, quarter)
    returned = lax.all_to_all(partial_out, "blocks", split_axis=0, concat_axis=0, tiled=True)
    back_rows = returned.reshape(slot_count, quarter)
    per_pair = jnp.einsum("sp,sd->pd", place_half, back_rows, preferred_element_type=jnp.float32)
    summed_out = per_pair.reshape(tok_rows, top_blocks, quarter).sum(axis=1) + dec_bias
    return summed_out.astype(jnp.bfloat16)


def solution(mesh):
    in_specs = (
        P("blocks", "dp"),
        P("dp"),
        P("blocks", None),
        P("blocks", None, None),
        P("blocks", "dp", None),
        P("blocks", None, "dp"),
        P("blocks", None),
    )
    out_specs = P("blocks", "dp")
    return jax.shard_map(
        on_device, mesh=mesh, in_specs=in_specs, out_specs=out_specs, check_vma=False
    )
```

profile of v0, /device:TPU:11, one launch (start us, length us, event | category | flops | bytes accessed | tf_op | source)
XLA Modules:
  0.0 559.7 jit_solution(3788040533072872040)
XLA Ops:
  6.5 0.0 all-reduce.2.cloned.1.call-start
  6.5 0.8 copy.29
  7.4 0.1 eq.70
  7.5 0.1 reshape.77
  7.7 1.2 reduce-window.6
  8.8 0.2 slice_reduce_fusion
  9.1 0.1 fusion.16
  9.2 2.1 subtract_convert_fusion
  11.2 4.7 broadcast_in_dim.3
  15.9 7.2 %reshape.80 = bf16[512,4096]{1,0:T(8,128)(2,1)} reshape(bf16[256,2,4096]{2,1,0:T(2,128)(2,1)} %broadcast_in_dim.3) | data formatting | bytes 8388608 | tf_op jit(solution)/shard_map/reshape | solution.py:23
  23.1 6.9 %convolution_convert_fusion = bf16[1024,4096]{1,0:T(8,128)(2,1)S(1)} fusion(bf16[512,4096]{1,0:T(8,128)(2,1)} %reshape.80, s32[512]{0:T(512)S(1)} %add_add_fusion), kind=kOutput, calls=%fused_computation.7 | convolution fusion | flops 4299685888 | bytes 12584960 | tf_op jit(solution)/shard_map/dot_general | solution.py:24
  30.0 188.5 %all_to_all.15 = bf16[16,64,4096]{2,1,0:T(8,128)(2,1)S(1)} all-to-all(bf16[16,64,4096]{2,1,0:T(8,128)(2,1)S(1)} %bitcast.43), channel_id=1, replica_groups=mesh['dp'=2,'blocks'=16] {'blocks'}, dimensions={0} | all-to-all | bytes 16777216 | tf_op jit(solution)/shard_map/all_to_all | solution.py:36
  218.5 12.5 %fusion.3 = f32[1024,1024]{1,0:T(8,128)} fusion(bf16[1024,4096]{1,0:T(8,128)(2,1)S(1)} %bitcast.44, bf16[1,4096,1024]{2,1,0:T(8,128)(2,1)} %param.11), kind=kOutput, calls=%fused_computation.4 | convolution fusion | flops 8589934592 | bytes 20971520 | tf_op jit(solution)/shard_map/dot_general | solution.py:41
  231.1 0.0 copy-start.1
  231.1 0.0 copy-start.2
  231.1 0.0 all-reduce.2.cloned.1.call-update
  231.1 0.7 copy-done.1
  231.8 0.1 copy.32
  232.0 1.0 fusion.12
  233.0 0.1 reshape.79
  233.2 0.1 reshape.87
  233.3 9.7 %all_to_all.16 = s32[16,1,1024]{2,1,0:T(1,128)S(1)} all-to-all(s32[16,1,1024]{2,1,0:T(1,128)S(1)} %reshape.87), channel_id=1, replica_groups=mesh['dp'=2,'blocks'=16] {'blocks'}, dimensions={0} | all-to-all | bytes 131072 | tf_op jit(solution)/shard_map/all_to_all | solution.py:37
  243.0 0.5 broadcast.47
  243.5 0.8 reduce.2
  244.4 0.1 reshape.88
  244.4 0.2 copy.37
  244.6 13.1 %fusion = pred[1024,1024]{1,0:T(8,128)(4,1)S(1)} fusion(s32[1024,16]{1,0:T(8,128)S(1)} %bitcast.45), kind=kLoop, calls=%fused_computation.1 | loop fusion | flops 32505856 | bytes 1114112 | tf_op jit(solution)/shard_map/reduce_or | solution.py:43
  257.8 81.6 %all-reduce.2.cloned.1.call-done = f32[1024,1024]{1,0:T(8,128)} async-done(((f32[1024,1024]{1,0:T(8,128)}), f32[1024,1024]{1,0:T(8,128)}) %all-reduce.2.cloned.1.call-update) | async-done | bytes 4194320 | tf_op jit(solution)/shard_map/psum | solution.py:42
  339.4 0.0 copy-done.2
  339.4 14.5 %fusion.5 = bf16[1024,4096]{1,0:T(8,128)(2,1)} fusion(bf16[1,1024,4096]{2,1,0:T(8,128)(2,1)} %param.12, pred[1024,1024]{1,0:T(8,128)(4,1)S(1)} %fusion, f32[1024,1024]{1,0:T(8,128)} %all-reduce.2.cloned.1.call-done, f32[1024]{0:T(1024)S(1)} %bitcast.49), kind=kOutput, calls=%fused_computation.6 | convolution fusion | flops 8598323200 | bytes 22024192 | tf_op jit(solution)/shard_map/dot_general | solution.py:45
  353.9 6.4 %all-to-all-start.2 = ((bf16[16,64,4096]{2,1,0:T(8,128)(2,1)}), bf16[16,64,4096]{2,1,0:T(8,128)(2,1)}, u32[]{:S(2)}, u32[]{:S(2)}) async-start(bf16[16,64,4096]{2,1,0:T(8,128)(2,1)} %bitcast.42), calls=%async_computation.2 | async-start | bytes 16777216 | tf_op jit(solution)/shard_map/all_to_all | solution.py:49
  360.3 0.4 iota_compare_fusion.4
  360.6 1.0 eq.76
  361.6 181.0 %all-to-all-done.2 = bf16[16,64,4096]{2,1,0:T(8,128)(2,1)} async-done(((bf16[16,64,4096]{2,1,0:T(8,128)(2,1)}), bf16[16,64,4096]{2,1,0:T(8,128)(2,1)}, u32[]{:S(2)}, u32[]{:S(2)}) %all-to-all-start.2) | async-done | bytes 8388640 | tf_op jit(solution)/shard_map/all_to_all | solution.py:49
  542.6 0.0 copy-start
  542.6 8.6 %convolution_reduce_fusion = f32[256,4096]{1,0:T(8,128)S(1)} fusion(bf16[1024,4096,1]{1,0,2:T(8,128)(2,1)} %bitcast.10, pred[256,2,1024]{2,1,0:T(4,128)(4,1)S(1)} %eq.76), kind=kOutput, calls=%fused_computation.11 | convolution fusion | flops 4296015872 | bytes 13107200 | tf_op jit(solution)/shard_map/sp,sd->pd/dot_general | solution.py:51
  551.2 0.0 copy-done
  551.2 1.7 add_convert_fusion
  (6 shorter events, 0.1 us)
Async XLA Ops:
  6.5 332.9 %all-reduce.2.cloned.1.call-start = ((), (), s32[]{:S(2)}) async-start(), calls=%async_computation.3 | async-start | bytes 8388608 | tf_op jit(solution)/shard_map/psum | solution.py:42
  231.1 0.8 copy-start.1
  231.1 108.3 %copy-start.2 = (f32[1,1024]{1,0:T(1,128)S(1)}, f32[1,1024]{1,0:T(1,128)}, u32[]{:S(2)}) copy-start(f32[1,1024]{1,0:T(1,128)} %param.13) | copy-start | bytes 12292
  353.9 188.7 %all-to-all-start.2 = ((bf16[16,64,4096]{2,1,0:T(8,128)(2,1)}), bf16[16,64,4096]{2,1,0:T(8,128)(2,1)}, u32[]{:S(2)}, u32[]{:S(2)}) async-start(bf16[16,64,4096]{2,1,0:T(8,128)(2,1)} %bitcast.42), calls=%async_computation.2 | async-start | bytes 16777216 | tf_op jit(solution)/shard_map/all_to_all | solution.py:49
  542.6 8.6 %copy-start = (f32[4096]{0:T(1024)S(1)}, f32[4096]{0:T(1024)}, u32[]{:S(2)}) copy-start(f32[4096]{0:T(1024)} %param.8) | copy-start | bytes 49156
Sparse Core Ops, SparseCore 0:
  231.2 108.1 all-reduce.1
where the time goes:
time: 560 us
  waiting for transfers between devices  263 us (47%)
  blocking collectives  198 us (35%)
  matrix products  43.5 us (8%)
  other arithmetic  19.3 us (3%)
  local copies, waits for them, and re-layouts  16.1 us (3%)
  between operations  13.5 us (2%)
  starting transfers between devices  6.38 us (1%)
    all_to_all x1, blocking collectives, on_device(): lax.all_to_all(outgoing, 'blocks', split_axis=0, concat_axis=0, tiled=True)  188 us
    all_to_all x1, waiting for transfers between devices, on_device(): lax.all_to_all(partial_out, 'blocks', split_axis=0, concat_axis=0, tiled=...  181 us
    psum x1, waiting for transfers between devices, on_device(): summed = lax.psum(partial_value, 'dp') + bias_local[None, :]  81.6 us
    dot_general x1, matrix products, on_device(): jnp.dot(active, dec_local, preferred_element_type=jnp.float32)  14.5 us
    reduce_or x1, other arithmetic, on_device(): jnp.any(chosen_ids[:, :, None] == lat_ids[None, None, :], axis=1)  13.1 us
    dot_general x1, matrix products, on_device(): jnp.dot(flat_rows, enc_local, preferred_element_type=jnp.float32)  12.5 us
  transfers between devices with their start and end apart: 2, of which 2 were waited for; matrix products, arithmetic and copies ran while one was open for 3% of the time, Pallas kernels for 0%

commit v1 on v0

v1 whole, which is shorter than its diff:
```python
import functools

import jax
import jax.numpy as jnp
from jax import lax
from jax.experimental import pallas as pl
from jax.experimental.pallas import tpu as pltpu
from jax.sharding import PartitionSpec as P

BACK_CHUNKS = (1, 1, 1, 1)
SUM_CHUNKS = 2
INNER = 4
OUTER = 4
EXTRA = 128
BLOCK = 512
VMEM = 24 * 1024 * 1024
F32 = jnp.float32
BF16 = jnp.bfloat16


def flat_on_device(tokens, dec_bias, routes, latent_picks, enc_weight, dec_weight, enc_bias):
    tok_rows, quarter = tokens.shape
    top_blocks = routes.shape[1]
    pick_count = latent_picks.shape[2]
    latents = enc_weight.shape[2]
    blk_count = lax.axis_size("blocks")
    capacity = max(2, 2 * tok_rows * top_blocks // blk_count)
    slot_count = blk_count * capacity
    pair_count = tok_rows * top_blocks
    centered = (tokens.astype(F32) - dec_bias).astype(BF16)
    owners = routes.reshape(pair_count)
    onehot = (owners[:, None] == jnp.arange(blk_count, dtype=jnp.int32)[None, :]).astype(jnp.int32)
    slot_rank = jnp.sum(jnp.cumsum(onehot, axis=0) * onehot, axis=1) - 1
    target = owners * capacity + slot_rank
    placing = jnp.arange(slot_count, dtype=jnp.int32)[:, None] == target[None, :]
    place_half = placing.astype(BF16)
    paired = jnp.repeat(centered, top_blocks, axis=0)
    outgoing = jnp.dot(place_half, paired, preferred_element_type=F32).astype(BF16)
    outgoing = outgoing.reshape(blk_count, capacity, quarter)
    sent_picks = jnp.dot(
        placing.astype(F32),
        latent_picks.reshape(pair_count, pick_count).astype(F32),
        precision=lax.Precision.HIGHEST,
    ).astype(jnp.int32)
    sent_picks = sent_picks.reshape(blk_count, capacity, pick_count)
    lat_ids = jnp.arange(latents, dtype=jnp.int32)
    arrived = lax.all_to_all(outgoing, "blocks", split_axis=0, concat_axis=0, tiled=True)
    chosen = lax.all_to_all(sent_picks, "blocks", split_axis=0, concat_axis=0, tiled=True)
    flat_rows = arrived.reshape(slot_count, quarter)
    chosen_ids = chosen.reshape(slot_count, pick_count)
    partial_value = jnp.dot(flat_rows, enc_weight[0], preferred_element_type=F32)
    summed = lax.psum(partial_value, "dp") + enc_bias[0][None, :]
    keep_mask = jnp.any(chosen_ids[:, :, None] == lat_ids[None, None, :], axis=1)
    active = jnp.where(keep_mask, jnp.maximum(summed, 0.0), 0.0).astype(BF16)
    partial_out = jnp.dot(active, dec_weight[0], preferred_element_type=F32).astype(BF16)
    partial_out = partial_out.reshape(blk_count, capacity, quarter)
    returned = lax.all_to_all(partial_out, "blocks", split_axis=0, concat_axis=0, tiled=True)
    back_rows = returned.reshape(slot_count, quarter)
    per_pair = jnp.einsum("sp,sd->pd", place_half, back_rows, preferred_element_type=F32)
    summed_out = per_pair.reshape(tok_rows, top_blocks, quarter).sum(axis=1) + dec_bias
    return summed_out.astype(BF16)


def outer_pairs(pairs):
    return [(a * INNER + i, b * INNER + i) for a, b in pairs for i in range(INNER)]


def inner_pairs(flip):
    return [(i, i ^ flip) for i in range(OUTER * INNER)]


ENDS = outer_pairs([(0, 1), (1, 0), (2, 3), (3, 2)])
MIDDLE = outer_pairs([(1, 2), (2, 1)])
OUTWARD = outer_pairs([(1, 0), (2, 3)])
INWARD = outer_pairs([(0, 1), (3, 2)])
FLIPS = {1: inner_pairs(1), 2: inner_pairs(2), 3: inner_pairs(3)}


def move(value, pairs):
    return lax.ppermute(value, "blocks", pairs)


def after(value, *others):
    return lax.optimization_barrier((value, *others))[0]


def call(kernel, name, grid, in_specs, out_specs, out_shape, scratch=()):
    return pl.pallas_call(
        kernel,
        name=name,
        grid=grid,
        in_specs=in_specs,
        out_specs=out_specs,
        out_shape=out_shape,
        scratch_shapes=scratch,
        compiler_params=pltpu.CompilerParams(vmem_limit_bytes=VMEM),
        cost_estimate=pl.CostEstimate(flops=0, bytes_accessed=0, transcendentals=0),
    )


def dispatch_kernel(cap, slots_ref, extra_refs, value_refs, offset_ref, spread_ref, out_refs, place_ref):
    rows = spread_ref.shape[0]

    @pl.when(pl.program_id(0) == 0)
    def _():
        extra = extra_refs[0][...].astype(F32)
        for ref in extra_refs[1:]:
            extra = extra + ref[...].astype(F32)
        hit = (extra[:, 0:1] == slots_ref[0:1, :]) | (extra[:, 1:2] == slots_ref[0:1, :])
        earlier = lax.broadcasted_iota(jnp.int32, (rows, rows), 1) < lax.broadcasted_iota(
            jnp.int32, (rows, rows), 0
        )
        rank = jnp.dot(
            jnp.where(earlier, 1.0, 0.0).astype(BF16),
            jnp.where(hit, 1.0, 0.0).astype(BF16),
            preferred_element_type=F32,
        )
        spread = jnp.where(hit & (rank == slots_ref[1:2, :]), 1.0, 0.0)
        spread_ref[...] = spread.astype(BF16)
        place_ref[...] = spread.T.astype(BF16)

    value = value_refs[0][...]
    for ref in value_refs[1:]:
        value = value + ref[...]
    moved = jnp.dot(place_ref[...], value, preferred_element_type=F32) - offset_ref[...]
    moved = moved.astype(BF16)
    for j, ref in enumerate(out_refs):
        ref[...] = moved[j * cap:(j + 1) * cap]


def dispatch(values, offset, slots, cap):
    rows, wide = values[0].shape
    step = wide // 3
    n = len(values)

    def kernel(slots_ref, *refs):
        dispatch_kernel(
            cap, slots_ref, refs[:n], refs[n:2 * n], refs[2 * n], refs[2 * n + 1], refs[2 * n + 2:-1], refs[-1]
        )

    spread, *pieces = call(
        kernel,
        "dispatch",
        (3,),
        [pl.BlockSpec((8, INNER * cap), lambda j: (0, 0))]
        + [pl.BlockSpec((rows, EXTRA), lambda j: (0, wide // EXTRA - 1))] * n
        + [pl.BlockSpec((rows, step), lambda j: (0, j))] * n
        + [pl.BlockSpec((1, step), lambda j: (0, j))],
        [pl.BlockSpec((rows, INNER * cap), lambda j: (0, 0))]
        + [pl.BlockSpec((cap, step), lambda j: (0, j))] * INNER,
        [jax.ShapeDtypeStruct((rows, INNER * cap), BF16)]
        + [jax.ShapeDtypeStruct((cap, wide), BF16)] * INNER,
        [pltpu.VMEM((INNER * cap, rows), BF16)],
    )(slots, *values, *values, offset)
    return spread, pieces


def encode_kernel(picked, piece_refs, extra_refs, enc_ref, bias_ref, me_ref, chosen_ref, picks_ref, total):
    k = pl.program_id(0)

    @pl.when(k == 0)
    def _():
        total[...] = jnp.broadcast_to(bias_ref[...], total.shape)

    mine = jnp.concatenate([ref[...] for ref in piece_refs], axis=0)
    total[...] += jnp.dot(mine, enc_ref[...], preferred_element_type=F32)

    @pl.when(k == pl.num_programs(0) - 1)
    def _():
        extra = jnp.concatenate([ref[...] for ref in extra_refs], axis=0).astype(F32)
        size = 2 * picked
        both = extra[:, 2:2 + size] * 32.0 + extra[:, 2 + size:2 + 2 * size]
        both = both.astype(jnp.int32)
        picks = jnp.where(extra[:, 0:1] == me_ref[0, 0], both[:, :picked], both[:, picked:])
        slots, latents = total.shape
        lane = lax.broadcasted_iota(jnp.int32, (slots, EXTRA), 1)
        ids = lax.broadcasted_iota(jnp.int32, (slots, latents), 1)
        values = jnp.zeros((slots, EXTRA), F32)
        kept = jnp.zeros((slots, EXTRA), jnp.int32)
        pre = total[...]
        for p in range(picked):
            pick = picks[:, p:p + 1]
            value = jnp.sum(jnp.where(ids == pick, pre, 0.0), axis=1, keepdims=True)
            values = jnp.where(lane == p, value, values)
            kept = jnp.where(lane == p, pick, kept)
        chosen_ref[...] = values.T[:picked]
        picks_ref[...] = kept


def encode(pieces, weight, bias, me, cap, picked):
    width, latents = weight.shape
    slots = INNER * cap
    last = width // EXTRA

    def kernel(*refs):
        encode_kernel(picked, refs[:INNER], refs[INNER:2 * INNER], *refs[2 * INNER:])

    return call(
        kernel,
        "encode",
        (width // BLOCK,),
        [pl.BlockSpec((cap, BLOCK), lambda k: (0, k))] * INNER
        + [pl.BlockSpec((cap, EXTRA), lambda k: (0, last))] * INNER
        + [
            pl.BlockSpec((BLOCK, latents), lambda k: (k, 0)),
            pl.BlockSpec((1, latents), lambda k: (0, 0)),
            pl.BlockSpec(memory_space=pltpu.SMEM),
        ],
        [
            pl.BlockSpec((picked, slots), lambda k: (0, 0)),
            pl.BlockSpec((slots, EXTRA), lambda k: (0, 0)),
        ],
        [
            jax.ShapeDtypeStruct((picked, slots), F32),
            jax.ShapeDtypeStruct((slots, EXTRA), jnp.int32),
        ],
        [pltpu.VMEM((slots, latents), F32)],
    )(*pieces, *pieces, weight, bias, me)


def decode_kernel(cap, chosen_ref, added_ref, picks_ref, dec_ref, *refs):
    active = refs[-1]

    @pl.when(pl.program_id(0) == 0)
    def _():
        picked, slots = chosen_ref.shape
        latents = active.shape[1]
        value = jnp.maximum(chosen_ref[...] + added_ref[...], 0.0)
        value = jnp.concatenate([value, jnp.zeros((EXTRA - picked, slots), F32)], axis=0).T
        ids = lax.broadcasted_iota(jnp.int32, (slots, latents), 1)
        dense = jnp.zeros((slots, latents), F32)
        for p in range(picked):
            dense = jnp.where(ids == picks_ref[:, p:p + 1], value[:, p:p + 1], dense)
        active[...] = dense.astype(BF16)

    part = jnp.dot(active[...], dec_ref[...], preferred_element_type=F32).astype(BF16)
    for j, ref in enumerate(refs[:-1]):
        ref[...] = part[j * cap:(j + 1) * cap]


def decode(chosen, added, picks, weight, cap, first, width):
    picked, slots = chosen.shape
    latents = weight.shape[0]
    skip = first // BLOCK
    return call(
        functools.partial(decode_kernel, cap),
        "decode",
        (width // BLOCK,),
        [
            pl.BlockSpec((picked, slots), lambda j: (0, 0)),
            pl.BlockSpec((picked, slots), lambda j: (0, 0)),
            pl.BlockSpec((slots, EXTRA), lambda j: (0, 0)),
            pl.BlockSpec((latents, BLOCK), lambda j: (0, j + skip)),
        ],
        [pl.BlockSpec((cap, BLOCK), lambda j: (0, j))] * INNER,
        [jax.ShapeDtypeStruct((cap, width), BF16)] * INNER,
        [pltpu.VMEM((slots, latents), BF16)],
    )(chosen, added, picks, weight)


def combine_kernel(spread_ref, *refs):
    parts = jnp.concatenate([ref[...] for ref in refs[:-1]], axis=0)
    refs[-1][...] = jnp.dot(spread_ref[...], parts, preferred_element_type=F32).astype(BF16)


def combine(spread, pieces, first, width):
    cap = pieces[0].shape[0]
    rows, slots = spread.shape
    step = min(width, 1024)
    skip = first // step
    return call(
        combine_kernel,
        "combine",
        (width // step,),
        [pl.BlockSpec((rows, slots), lambda j: (0, 0))]
        + [pl.BlockSpec((cap, step), lambda j: (0, j + skip))] * INNER,
        pl.BlockSpec((rows, step), lambda j: (0, j)),
        jax.ShapeDtypeStruct((rows, width), BF16),
    )(spread, *pieces)


def line_on_device(tokens, dec_bias, routes, latent_picks, enc_weight, dec_weight, enc_bias):
    rows, width = tokens.shape
    top = routes.shape[1]
    picked = latent_picks.shape[2]
    blk_count = lax.axis_size("blocks")
    cap = max(2, 2 * rows * top // blk_count)
    me = lax.axis_index("blocks")
    plane, inner = me // INNER, me % INNER

    flat_picks = latent_picks.reshape(rows, top * picked)
    meta = jnp.concatenate([routes, flat_picks // 32, flat_picks % 32], axis=1).astype(BF16)
    meta = jnp.pad(meta, ((0, 0), (0, EXTRA - meta.shape[1])))
    own = jnp.concatenate([tokens, meta], axis=1)
    offset = jnp.pad(dec_bias, (0, EXTRA))[None, :]
    slot = jnp.arange(INNER * cap, dtype=jnp.int32)
    slots = jnp.stack([plane * INNER + ((slot // cap) ^ inner), slot % cap]).astype(F32)
    slots = jnp.pad(slots, ((0, 6), (0, 0)))
    bias = jnp.where(lax.axis_index("dp") == 0, enc_bias, 0.0)
    me_value = me.astype(F32).reshape(1, 1)
    enc, dec = enc_weight[0], dec_weight[0]

    with jax.named_scope("rows_ends"):
        by_one = move(own, ENDS)
    with jax.named_scope("rows_middle"):
        by_two = move(own, MIDDLE)
    groups = {0: (own,)}

    def exchange(pieces, name):
        moved = [pieces[0]]
        for j in range(1, INNER):
            with jax.named_scope(f"{name}_{j}"):
                moved.append(move(pieces[j], FLIPS[j]))
        return moved

    def all_after(values, *earlier):
        values = tuple(values)
        return lax.optimization_barrier((*values, *earlier))[:len(values)]

    def send_out(t):
        spread, pieces = dispatch(groups[t], offset, slots, cap)
        return spread, exchange(pieces, f"out_{t}")

    def encoded(t, pieces):
        chosen, picks = encode(pieces, enc, bias, me_value, cap, picked)
        with jax.named_scope(f"sums_{t}"):
            added = lax.ppermute(chosen, "dp", [(0, 1), (1, 0)])
        return picks, chosen, added

    def decoded(t, picks, chosen, added):
        each = width // BACK_CHUNKS[t]
        return [
            decode(chosen, added, picks, dec, cap, i * each, each) for i in range(BACK_CHUNKS[t])
        ]

    def leave(t, parts, *earlier):
        if earlier:
            parts = [all_after(pieces, *earlier) for pieces in parts]
        return [exchange(pieces, f"back_{t}_{i}") for i, pieces in enumerate(parts)]

    def combined(spread, parts, count, *earlier):
        sums = []
        for pieces in parts:
            if earlier:
                pieces = all_after(pieces, *earlier)
            wide, each = pieces[0].shape[1], width // count
            for first in range(0, wide, each):
                sums.append(combine(spread, pieces, first, min(each, wide)))
        return sums

    def plus(a, b):
        return (a.astype(F32) + b.astype(F32)).astype(BF16)

    spreads, back = {}, {}
    spreads[0], arrived = send_out(0)
    waiting, returned = {}, {}
    for t in range(OUTER):
        if t > 0:
            arrived = all_after(arrived, *waiting[t - 1][0])
        if t > 1:
            returned[t - 1] = leave(t - 1, waiting[t - 1], *arrived[1:])
        picks, chosen, added = encoded(t, arrived)
        earlier = (chosen,)
        if t == 2:
            pieces = returned[1][0]
            pieces[2] = after(pieces[2], chosen)
            earlier = earlier + (pieces[2],)
        if t == 0:
            by_one, by_two = all_after((by_one, by_two), *earlier)
            with jax.named_scope("rows_outward_two"):
                to_ends_two = move(by_two, OUTWARD)
            with jax.named_scope("rows_middle_far"):
                by_three = move(by_one, MIDDLE)
            groups[1] = (by_one,)
        if t == 1:
            by_three, to_ends_two = all_after((by_three, to_ends_two), *earlier)
            with jax.named_scope("rows_outward_far"):
                to_ends_three = move(by_three, OUTWARD)
            groups[2] = (by_two, to_ends_two)
        if t == 2:
            groups[3] = (by_three, after(to_ends_three, *earlier))
        if t < OUTER - 1:
            spreads[t + 1], arrived = send_out(t + 1)
            added = after(added, spreads[t + 1])
        if t == 2:
            back[1] = combined(spreads[1], returned[1], 1, spreads[3])
            with jax.named_scope("sum_inward_one"):
                from_end = move(back[1][0], INWARD)
            added = after(added, *back[1])
        waiting[t] = decoded(t, picks, chosen, added)
    last = leave(3, waiting[3])
    back[2] = combined(spreads[2], returned[2], SUM_CHUNKS, *waiting[3][0])
    from_end = after(from_end, *back[2])
    back[3] = combined(spreads[3], last, SUM_CHUNKS, from_end)

    count = SUM_CHUNKS
    piece = width // count
    cols = [slice(i * piece, (i + 1) * piece) for i in range(count)]
    from_two, from_far = [], []
    for i in range(count):
        with jax.named_scope(f"sum_inward_two_{i}"):
            from_two.append(move(back[2][i], INWARD))
    for i in range(count):
        with jax.named_scope(f"sum_inward_far_{i}"):
            from_far.append(move(back[3][i], INWARD))
    twos, threes, ones, results = [], [], [], []
    seen = tuple(back[3])
    for i in range(count):
        got = after(from_two[i], *seen)
        with jax.named_scope(f"sum_middle_two_{i}"):
            twos.append(move(plus(back[2][i], got), MIDDLE))
        seen = (got,)
    for i in range(count):
        twos[i] = after(twos[i], *seen)
        got = after(from_far[i], twos[i])
        with jax.named_scope(f"sum_middle_far_{i}"):
            threes.append(move(plus(back[3][i], got), MIDDLE))
        seen = (got,)
    for i in range(count):
        got = after(threes[i], *seen)
        with jax.named_scope(f"sum_outward_far_{i}"):
            ones.append(move(plus(back[1][0][:, cols[i]], got), OUTWARD))
        seen = (ones[i],)
    returned[0] = leave(0, waiting[0], threes[0])
    back[0] = combined(spreads[0], returned[0], 1)
    for i in range(count):
        total = dec_bias[cols[i]]
        for value in (back[0][0][:, cols[i]], from_end[:, cols[i]], twos[i], ones[i]):
            total = total + value.astype(F32)
        results.append(total.astype(BF16))
    return jnp.concatenate(results, axis=1)


def solution(mesh):
    in_specs = (
        P("blocks", "dp"),
        P("dp"),
        P("blocks", None),
        P("blocks", None, None),
        P("blocks", "dp", None),
        P("blocks", None, "dp"),
        P("blocks", None),
    )
    on_device = line_on_device if mesh.shape["blocks"] == OUTER * INNER else flat_on_device
    return jax.shard_map(
        on_device, mesh=mesh, in_specs=in_specs, out_specs=P("blocks", "dp"), check_vma=False
    )
```

time: 560 us -> 382 us (0.68)
  the two profiles are of different devices: /device:TPU:11 before, /device:TPU:0 now
where the time goes in v1:
time: 382 us; the launch traced here: 376 us
  waiting for transfers between devices  220 us (58%)
  Pallas kernels  86.1 us (23%)
  starting transfers between devices  52.8 us (14%)
  other arithmetic  8.61 us (2%)
  local copies, waits for them, and re-layouts  7.82 us (2%)
    ppermute x40, waiting for transfers between devices, move(): return lax.ppermute(value, 'blocks', pairs)  213 us
    ppermute x40, starting transfers between devices, move(): return lax.ppermute(value, 'blocks', pairs)  46.4 us
    pallas_call x4, Pallas kernels, encode(): call(kernel, 'encode', (width // BLOCK,), [pl.BlockSpec((cap, BLOCK), lam...  37.2 us
    pallas_call x4, Pallas kernels, decode(): call(functools.partial(decode_kernel, cap), 'decode', (width // BLOCK,),...  30.6 us
    pallas_call x4, Pallas kernels, dispatch(): call(kernel, 'dispatch', (3,), [pl.BlockSpec((8, INNER * cap), lambda j:...  12.1 us
  transfers between devices with their start and end apart: 44, of which 25 were waited for; matrix products, arithmetic and copies ran while one was open for 1% of the time, Pallas kernels for 23%

profile of v1, /device:TPU:0, one launch (start us, length us, event | category | flops | bytes accessed | tf_op | source)
XLA Modules:
  0.0 376.0 jit_solution(2971104535379562104)
XLA Ops:
  2.0 1.8 pad_maximum_fusion.refs_0_.refs_1_
  3.7 3.1 collective-permute-start.4
  6.8 2.0 collective-permute-start.5
  9.0 2.9 dispatch.4
  11.9 1.5 collective-permute-start.1
  14.0 13.2 %collective-permute-done.1.refs_2_.refs_6_ = bf16[64,4224]{1,0:T(8,128)(2,1)} collective-permute-done((bf16[64,4224]{1,0:T(8,128)(2,1)}, bf16[64,4224]{1,0:T(8,128)(2,1)}, u32[]{:S(2)}, u32[]{:S(2)}) %collective-permute-start.1) | collective-permute-done | bytes 540704 | tf_op jit(solution)/shard_map/out_0_2/ppermute | solution.py:80
  27.3 10.8 %collective-permute-done.2.refs_3_.refs_7_ = bf16[64,4224]{1,0:T(8,128)(2,1)} collective-permute-done((bf16[64,4224]{1,0:T(8,128)(2,1)}, bf16[64,4224]{1,0:T(8,128)(2,1)}, u32[]{:S(2)}, u32[]{:S(2)}) %collective-permute-start.2) | collective-permute-done | bytes 540704 | tf_op jit(solution)/shard_map/out_0_3/ppermute | solution.py:80
  38.1 3.4 copy-done
  41.5 10.3 %encode.4 = (f32[16,256]{1,0:T(8,128)S(1)}, s32[256,128]{1,0:T(8,128)S(1)}) custom-call(bf16[64,4224]{1,0:T(8,128)(2,1)S(1)} %get-tuple-element.105.refs_0_.refs_4_, bf16[64,4224]{1,0:T(8,128)(2,1)S(1)} %collective-permute-done.refs_1_.refs_5_, bf16[64,4224]{1,0:T(8,128)(2,1)} %collective-permute-done.1.refs_2_.refs_6_, ...), custom_call_target="tpu_custom_call" | custom-call | tf_op jit(solution)/shard_map/encode/pallas_call | solution.py:198
  51.8 2.2 collective-permute-done.4.refs_0_.refs_1_
  54.9 1.9 collective-permute-start.7
  56.9 1.7 collective-permute-start.3
  58.6 3.5 dispatch.5
  62.2 1.6 collective-permute-start.8
  64.3 3.4 copy-done.1
  67.7 7.7 %decode.4 = (bf16[64,4096]{1,0:T(8,128)(2,1)S(1)}, bf16[64,4096]{1,0:T(8,128)(2,1)S(1)}, bf16[64,4096]{1,0:T(8,128)(2,1)S(1)}, bf16[64,4096]{1,0:T(8,128)(2,1)S(1)}) custom-call(f32[16,256]{1,0:T(8,128)S(1)} %get-tuple-element.109.chosen_ref, f32[16,256]{1,0:T(8,128)S(1)} %collective-permute-done.3.added_ref, s32[256,128]{1,0:T(8,128)S(1)} %get-tuple-element.113.picks_ref, ...), custom_call_target="tpu_custom_call" | custom-call | tf_op jit(solution)/shard_map/decode/pallas_call | solution.py:245
  75.3 1.3 collective-permute-done.10.refs_3_.refs_7_
  76.7 11.6 %collective-permute-done.9.refs_2_.refs_6_ = bf16[64,4224]{1,0:T(8,128)(2,1)S(1)} collective-permute-done((bf16[64,4224]{1,0:T(8,128)(2,1)S(1)}, bf16[64,4224]{1,0:T(8,128)(2,1)S(1)}, u32[]{:S(2)}, u32[]{:S(2)}) %collective-permute-start.9) | collective-permute-done | bytes 540704 | tf_op jit(solution)/shard_map/out_1_2/ppermute | solution.py:80
  88.3 9.0 %encode.5 = (f32[16,256]{1,0:T(8,128)S(1)}, s32[256,128]{1,0:T(8,128)S(1)}) custom-call(bf16[64,4224]{1,0:T(8,128)(2,1)S(1)} %get-tuple-element.123.refs_0_.refs_4_, bf16[64,4224]{1,0:T(8,128)(2,1)S(1)} %collective-permute-done.8.refs_1_.refs_5_, bf16[64,4224]{1,0:T(8,128)(2,1)S(1)} %collective-permute-done.9.refs_2_.refs_6_, ...), custom_call_target="tpu_custom_call" | custom-call | tf_op jit(solution)/shard_map/encode/pallas_call | solution.py:198
  97.4 12.3 %collective-permute-done.7.refs_1_.refs_3_ = bf16[256,4224]{1,0:T(8,128)(2,1)S(1)} collective-permute-done((bf16[256,4224]{1,0:T(8,128)(2,1)}, bf16[256,4224]{1,0:T(8,128)(2,1)S(1)}, u32[]{:S(2)}, u32[]{:S(2)}) %collective-permute-start.7) | collective-permute-done | bytes 2162720 | tf_op jit(solution)/shard_map/rows_outward_two/ppermute | solution.py:80
  109.7 1.5 collective-permute-start.11
  111.1 3.6 dispatch.6
  114.8 1.6 collective-permute-start.13
  116.6 1.5 collective-permute-start.15
  118.2 2.2 collective-permute-done.15.added_ref
  120.4 7.7 %decode.5 = (bf16[64,4096]{1,0:T(8,128)(2,1)S(1)}, bf16[64,4096]{1,0:T(8,128)(2,1)S(1)}, bf16[64,4096]{1,0:T(8,128)(2,1)S(1)}, bf16[64,4096]{1,0:T(8,128)(2,1)S(1)}) custom-call(f32[16,256]{1,0:T(8,128)S(1)} %get-tuple-element.127.chosen_ref, f32[16,256]{1,0:T(8,128)S(1)} %collective-permute-done.15.added_ref, s32[256,128]{1,0:T(8,128)S(1)} %get-tuple-element.136.picks_ref, ...), custom_call_target="tpu_custom_call" | custom-call | tf_op jit(solution)/shard_map/decode/pallas_call | solution.py:245
  128.1 1.9 collective-permute-done.13.refs_2_.refs_6_
  129.9 10.7 %collective-permute-done.14.refs_3_.refs_7_ = bf16[64,4224]{1,0:T(8,128)(2,1)S(1)} collective-permute-done((bf16[64,4224]{1,0:T(8,128)(2,1)S(1)}, bf16[64,4224]{1,0:T(8,128)(2,1)S(1)}, u32[]{:S(2)}, u32[]{:S(2)}) %collective-permute-start.14) | collective-permute-done | bytes 540704 | tf_op jit(solution)/shard_map/out_2_3/ppermute | solution.py:80
  140.6 1.5 collective-permute-start.16
  142.7 8.9 %encode.6 = (f32[16,256]{1,0:T(8,128)S(1)}, s32[256,128]{1,0:T(8,128)S(1)}) custom-call(bf16[64,4224]{1,0:T(8,128)(2,1)S(1)} %get-tuple-element.141.refs_0_.refs_4_, bf16[64,4224]{1,0:T(8,128)(2,1)S(1)} %collective-permute-done.12.refs_1_.refs_5_, bf16[64,4224]{1,0:T(8,128)(2,1)S(1)} %collective-permute-done.13.refs_2_.refs_6_, ...), custom_call_target="tpu_custom_call" | custom-call | tf_op jit(solution)/shard_map/encode/pallas_call | solution.py:198
  151.7 3.6 collective-permute-done.16.refs_2_
  155.3 2.9 collective-permute-done.11.refs_1_.refs_3_
  158.2 2.1 dispatch.7
  160.4 1.6 collective-permute-start.18
  162.3 3.6 collective-permute-done.22.refs_3_
  165.9 1.5 combine.6
  167.5 4.7 %collective-permute-start.27 = (bf16[256,4096]{1,0:T(8,128)(2,1)S(1)}, bf16[256,4096]{1,0:T(8,128)(2,1)S(1)}, u32[]{:S(2)}, u32[]{:S(2)}) collective-permute-start(bf16[256,4096]{1,0:T(8,128)(2,1)S(1)} %combine.6), channel_id=1, source_target_pairs={{0,4},{1,5},{2,6},{3,7},{12,8},{13,9},{14,10},{15,11},{16,20},{17,... | collective-permute-start | bytes 6291464 | tf_op jit(solution)/shard_map/sum_inward_one/ppermute | solution.py:80
  172.2 1.6 collective-permute-start.20
  173.8 2.2 collective-permute-done.20.added_ref
  176.0 7.7 %decode.6 = (bf16[64,4096]{1,0:T(8,128)(2,1)S(1)}, bf16[64,4096]{1,0:T(8,128)(2,1)S(1)}, bf16[64,4096]{1,0:T(8,128)(2,1)S(1)}, bf16[64,4096]{1,0:T(8,128)(2,1)S(1)}) custom-call(f32[16,256]{1,0:T(8,128)S(1)} %get-tuple-element.145.chosen_ref, f32[16,256]{1,0:T(8,128)S(1)} %collective-permute-done.20.added_ref, s32[256,128]{1,0:T(8,128)S(1)} %get-tuple-element.163.picks_ref, ...), custom_call_target="tpu_custom_call" | custom-call | tf_op jit(solution)/shard_map/decode/pallas_call | solution.py:245
  183.7 5.4 %collective-permute-done.19.refs_3_.refs_7_ = bf16[64,4224]{1,0:T(8,128)(2,1)S(1)} collective-permute-done((bf16[64,4224]{1,0:T(8,128)(2,1)S(1)}, bf16[64,4224]{1,0:T(8,128)(2,1)S(1)}, u32[]{:S(2)}, u32[]{:S(2)}) %collective-permute-start.19) | collective-permute-done | bytes 540704 | tf_op jit(solution)/shard_map/out_3_3/ppermute | solution.py:80
  189.2 1.5 collective-permute-start.29
  191.0 8.9 %encode.7 = (f32[16,256]{1,0:T(8,128)S(1)}, s32[256,128]{1,0:T(8,128)S(1)}) custom-call(bf16[64,4224]{1,0:T(8,128)(2,1)S(1)} %get-tuple-element.168.refs_0_.refs_4_, bf16[64,4224]{1,0:T(8,128)(2,1)S(1)} %collective-permute-done.17.refs_1_.refs_5_, bf16[64,4224]{1,0:T(8,128)(2,1)S(1)} %collective-permute-done.18.refs_2_.refs_6_, ...), custom_call_target="tpu_custom_call" | custom-call | tf_op jit(solution)/shard_map/encode/pallas_call | solution.py:198
  199.9 1.6 collective-permute-start.23
  201.4 2.2 collective-permute-done.23.added_ref
  203.7 7.7 %decode.7 = (bf16[64,4096]{1,0:T(8,128)(2,1)S(1)}, bf16[64,4096]{1,0:T(8,128)(2,1)S(1)}, bf16[64,4096]{1,0:T(8,128)(2,1)S(1)}, bf16[64,4096]{1,0:T(8,128)(2,1)S(1)}) custom-call(f32[16,256]{1,0:T(8,128)S(1)} %get-tuple-element.172.chosen_ref, f32[16,256]{1,0:T(8,128)S(1)} %collective-permute-done.23.added_ref, s32[256,128]{1,0:T(8,128)S(1)} %get-tuple-element.173.picks_ref, ...), custom_call_target="tpu_custom_call" | custom-call | tf_op jit(solution)/shard_map/decode/pallas_call | solution.py:245
  211.4 2.8 collective-permute-done.30.refs_3_
  214.9 4.2 %collective-permute-start.32 = (bf16[256,2048]{1,0:T(8,128)(2,1)S(1)}, bf16[256,2048]{1,0:T(8,128)(2,1)S(1)}, u32[]{:S(2)}, u32[]{:S(2)}) collective-permute-start(bf16[256,2048]{1,0:T(8,128)(2,1)S(1)} %combine.7), channel_id=1, source_target_pairs={{0,4},{1,5},{2,6},{3,7},{12,8},{13,9},{14,10},{15,11},{16,20},{17,... | collective-permute-start | bytes 3145736 | tf_op jit(solution)/shard_map/sum_inward_two_0/ppermute | solution.py:80
  220.0 1.5 collective-permute-start.25
  222.3 1.6 collective-permute-start.34
  223.9 10.9 %collective-permute-done.25.refs_2_ = bf16[64,4096]{1,0:T(8,128)(2,1)S(1)} collective-permute-done((bf16[64,4096]{1,0:T(8,128)(2,1)S(1)}, bf16[64,4096]{1,0:T(8,128)(2,1)S(1)}, u32[]{:S(2)}, u32[]{:S(2)}) %collective-permute-start.25) | collective-permute-done | bytes 524320 | tf_op jit(solution)/shard_map/back_3_0_2/ppermute | solution.py:80
  234.8 9.5 %collective-permute-done.26.refs_3_ = bf16[64,4096]{1,0:T(8,128)(2,1)S(1)} collective-permute-done((bf16[64,4096]{1,0:T(8,128)(2,1)S(1)}, bf16[64,4096]{1,0:T(8,128)(2,1)S(1)}, u32[]{:S(2)}, u32[]{:S(2)}) %collective-permute-start.26) | collective-permute-done | bytes 524320 | tf_op jit(solution)/shard_map/back_3_0_3/ppermute | solution.py:80
  247.1 3.4 collective-permute-start.31
  250.4 1.4 collective-permute-start.39
  251.8 12.9 %collective-permute-done.34 = bf16[256,2048]{1,0:T(8,128)(2,1)S(1)} collective-permute-done((bf16[256,2048]{1,0:T(8,128)(2,1)S(1)}, bf16[256,2048]{1,0:T(8,128)(2,1)S(1)}, u32[]{:S(2)}, u32[]{:S(2)}) %collective-permute-start.34) | collective-permute-done | bytes 1048608 | tf_op jit(solution)/shard_map/sum_inward_two_1/ppermute | solution.py:80
  265.9 21.3 %collective-permute-done.31 = bf16[256,2048]{1,0:T(8,128)(2,1)S(1)} collective-permute-done((bf16[256,2048]{1,0:T(8,128)(2,1)S(1)}, bf16[256,2048]{1,0:T(8,128)(2,1)S(1)}, u32[]{:S(2)}, u32[]{:S(2)}) %collective-permute-start.31) | collective-permute-done | bytes 1048608 | tf_op jit(solution)/shard_map/sum_inward_far_0/ppermute | solution.py:80
  288.3 21.3 %collective-permute-done.39 = bf16[256,2048]{1,0:T(8,128)(2,1)S(1)} collective-permute-done((bf16[256,2048]{1,0:T(8,128)(2,1)S(1)}, bf16[256,2048]{1,0:T(8,128)(2,1)S(1)}, u32[]{:S(2)}, u32[]{:S(2)}) %collective-permute-start.39) | collective-permute-done | bytes 1048608 | tf_op jit(solution)/shard_map/sum_inward_far_1/ppermute | solution.py:80
  312.6 31.4 %collective-permute-done.41 = bf16[256,2048]{1,0:T(8,128)(2,1)S(1)} collective-permute-done((bf16[256,2048]{1,0:T(8,128)(2,1)S(1)}, bf16[256,2048]{1,0:T(8,128)(2,1)S(1)}, u32[]{:S(2)}, u32[]{:S(2)}) %collective-permute-start.41) | collective-permute-done | bytes 1048608 | tf_op jit(solution)/shard_map/sum_outward_far_0/ppermute | solution.py:80
  345.7 1.5 collective-permute-start.37
  347.6 12.9 %collective-permute-done.37.refs_2_ = bf16[64,4096]{1,0:T(8,128)(2,1)S(1)} collective-permute-done((bf16[64,4096]{1,0:T(8,128)(2,1)S(1)}, bf16[64,4096]{1,0:T(8,128)(2,1)S(1)}, u32[]{:S(2)}, u32[]{:S(2)}) %collective-permute-start.37) | collective-permute-done | bytes 524320 | tf_op jit(solution)/shard_map/back_0_0_2/ppermute | solution.py:80
  360.5 10.3 %collective-permute-done.38.refs_3_ = bf16[64,4096]{1,0:T(8,128)(2,1)S(1)} collective-permute-done((bf16[64,4096]{1,0:T(8,128)(2,1)S(1)}, bf16[64,4096]{1,0:T(8,128)(2,1)S(1)}, u32[]{:S(2)}, u32[]{:S(2)}) %collective-permute-start.38) | collective-permute-done | bytes 524320 | tf_op jit(solution)/shard_map/back_0_0_3/ppermute | solution.py:80
  370.8 1.5 combine.11
  372.4 1.8 add_convert_fusion.3
  374.2 1.5 pad_maximum_fusion.1
  (81 shorter events, 18.4 us)
Async XLA Ops:
  1.9 7.0 %copy-start.2 = (f32[4096]{0:T(1024)S(1)}, f32[4096]{0:T(1024)}, u32[]{:S(2)}) copy-start(f32[4096]{0:T(1024)} %param.8) | copy-start | bytes 49156
  3.7 50.2 %collective-permute-start.4 = (bf16[256,4224]{1,0:T(8,128)(2,1)S(1)}, bf16[256,4224]{1,0:T(8,128)(2,1)}, u32[]{:S(2)}, u32[]{:S(2)}) collective-permute-start(bf16[256,4224]{1,0:T(8,128)(2,1)S(1)} %pad_maximum_fusion.refs_0_.refs_1_), channel_id=1, source_target_pairs={{0,4},{1,5},{2,6},{3,7},{4,0},{5,1},{6,2},{7,3},{8,12},{9,13},{10,... | collective-permute-start | bytes 6488072 | tf_op jit(solution)/shard_map/rows_ends/ppermute | solution.py:80
  6.8 47.1 %collective-permute-start.5 = (bf16[256,4224]{1,0:T(8,128)(2,1)S(1)}, bf16[256,4224]{1,0:T(8,128)(2,1)}, u32[]{:S(2)}, u32[]{:S(2)}) collective-permute-start(bf16[256,4224]{1,0:T(8,128)(2,1)S(1)} %pad_maximum_fusion.refs_0_.refs_1_), channel_id=1, source_target_pairs={{4,8},{5,9},{6,10},{7,11},{8,4},{9,5},{10,6},{11,7},{20,24},{21,25... | collective-permute-start | bytes 6488072 | tf_op jit(solution)/shard_map/rows_middle/ppermute | solution.py:80
  8.9 4.8 %copy-start.3 = (f32[1,1024]{1,0:T(1,128)S(1)}, f32[1,1024]{1,0:T(1,128)}, u32[]{:S(2)}) copy-start(f32[1,1024]{1,0:T(1,128)} %param.13) | copy-start | bytes 12292
  11.9 2.1 collective-permute-start
  11.9 15.4 %collective-permute-start.1 = (bf16[64,4224]{1,0:T(8,128)(2,1)}, bf16[64,4224]{1,0:T(8,128)(2,1)}, u32[]{:S(2)}, u32[]{:S(2)}) collective-permute-start(bf16[64,4224]{1,0:T(8,128)(2,1)} %get-tuple-element.107), channel_id=1, source_target_pairs={{0,2},{1,3},{2,0},{3,1},{4,6},{5,7},{6,4},{7,5},{8,10},{9,11},{10,... | collective-permute-start | bytes 1622024 | tf_op jit(solution)/shard_map/out_0_2/ppermute | solution.py:80
  13.4 24.7 %collective-permute-start.2 = (bf16[64,4224]{1,0:T(8,128)(2,1)}, bf16[64,4224]{1,0:T(8,128)(2,1)}, u32[]{:S(2)}, u32[]{:S(2)}) collective-permute-start(bf16[64,4224]{1,0:T(8,128)(2,1)} %get-tuple-element.108), channel_id=1, source_target_pairs={{0,3},{1,2},{2,1},{3,0},{4,7},{5,6},{6,5},{7,4},{8,11},{9,10},{10,... | collective-permute-start | bytes 1622024 | tf_op jit(solution)/shard_map/out_0_3/ppermute | solution.py:80
  38.1 3.4 copy-start
  41.5 46.9 %slice-start = ((s8[8388608]{0:T(1024)(128)(4,1)}), s8[4194304]{0:T(1024)(128)(4,1)S(1)}, s32[]{:S(2)}) async-start(s8[8388608]{0:T(1024)(128)(4,1)} %bitcast.5), calls=%async_computation | async-start | bytes 8388608
  54.0 34.3 %slice-start.1 = ((s8[8388608]{0:T(1024)(128)(4,1)}), s8[4194304]{0:T(1024)(128)(4,1)S(1)}, s32[]{:S(2)}) async-start(s8[8388608]{0:T(1024)(128)(4,1)} %bitcast.5), calls=%async_computation.1 | async-start | bytes 8388608
  54.0 43.4 %collective-permute-start.6 = (bf16[256,4224]{1,0:T(8,128)(2,1)}, bf16[256,4224]{1,0:T(8,128)(2,1)S(1)}, u32[]{:S(2)}, u32[]{:S(2)}) collective-permute-start(bf16[256,4224]{1,0:T(8,128)(2,1)} %collective-permute-done.4.refs_0_.refs_1_), channel_id=1, source_target_pairs={{4,8},{5,9},{6,10},{7,11},{8,4},{9,5},{10,6},{11,7},{20,24},{21,25... | collective-permute-start | bytes 6488072 | tf_op jit(solution)/shard_map/rows_middle_far/ppermute | solution.py:80
  54.9 54.8 %collective-permute-start.7 = (bf16[256,4224]{1,0:T(8,128)(2,1)}, bf16[256,4224]{1,0:T(8,128)(2,1)S(1)}, u32[]{:S(2)}, u32[]{:S(2)}) collective-permute-start(bf16[256,4224]{1,0:T(8,128)(2,1)} %collective-permute-done.5.refs_0_.refs_2_), channel_id=1, source_target_pairs={{4,0},{5,1},{6,2},{7,3},{8,12},{9,13},{10,14},{11,15},{20,16},{21,... | collective-permute-start | bytes 6488072 | tf_op jit(solution)/shard_map/rows_outward_two/ppermute | solution.py:80
  56.9 6.9 %collective-permute-start.3 = (f32[16,256]{1,0:T(8,128)S(1)}, f32[16,256]{1,0:T(8,128)S(1)}, u32[]{:S(2)}, u32[]{:S(2)}) collective-permute-start(f32[16,256]{1,0:T(8,128)S(1)} %get-tuple-element.109.chosen_ref), channel_id=1, source_target_pairs={{0,16},{16,0},{1,17},{17,1},{2,18},{18,2},{3,19},{19,3},{4,20},{20... | collective-permute-start | bytes 49160 | tf_op jit(solution)/shard_map/sums_0/ppermute | solution.py:327
  62.1 14.6 %collective-permute-start.10 = (bf16[64,4224]{1,0:T(8,128)(2,1)S(1)}, bf16[64,4224]{1,0:T(8,128)(2,1)S(1)}, u32[]{:S(2)}, u32[]{:S(2)}) collective-permute-start(bf16[64,4224]{1,0:T(8,128)(2,1)S(1)} %get-tuple-element.122), channel_id=1, source_target_pairs={{0,3},{1,2},{2,1},{3,0},{4,7},{5,6},{6,5},{7,4},{8,11},{9,10},{10,... | collective-permute-start | bytes 1622024 | tf_op jit(solution)/shard_map/out_1_3/ppermute | solution.py:80
  62.2 14.5 %collective-permute-start.8 = (bf16[64,4224]{1,0:T(8,128)(2,1)S(1)}, bf16[64,4224]{1,0:T(8,128)(2,1)S(1)}, u32[]{:S(2)}, u32[]{:S(2)}) collective-permute-start(bf16[64,4224]{1,0:T(8,128)(2,1)S(1)} %get-tuple-element.120), channel_id=1, source_target_pairs={{0,1},{1,0},{2,3},{3,2},{4,5},{5,4},{6,7},{7,6},{8,9},{9,8},{10,11... | collective-permute-start | bytes 1622024 | tf_op jit(solution)/shard_map/out_1_1/ppermute | solution.py:80
  63.8 24.5 %collective-permute-start.9 = (bf16[64,4224]{1,0:T(8,128)(2,1)S(1)}, bf16[64,4224]{1,0:T(8,128)(2,1)S(1)}, u32[]{:S(2)}, u32[]{:S(2)}) collective-permute-start(bf16[64,4224]{1,0:T(8,128)(2,1)S(1)} %get-tuple-element.121), channel_id=1, source_target_pairs={{0,2},{1,3},{2,0},{3,1},{4,6},{5,7},{6,4},{7,5},{8,10},{9,11},{10,... | collective-permute-start | bytes 1622024 | tf_op jit(solution)/shard_map/out_1_2/ppermute | solution.py:80
  64.3 3.4 copy-start.1
  88.3 32.1 %slice-start.2 = ((s8[8388608]{0:T(1024)(128)(4,1)}), s8[4194304]{0:T(1024)(128)(4,1)S(1)}, s32[]{:S(2)}) async-start(s8[8388608]{0:T(1024)(128)(4,1)} %bitcast.11), calls=%async_computation.2 | async-start | bytes 8388608
  88.3 32.1 %slice-start.3 = ((s8[8388608]{0:T(1024)(128)(4,1)}), s8[4194304]{0:T(1024)(128)(4,1)S(1)}, s32[]{:S(2)}) async-start(s8[8388608]{0:T(1024)(128)(4,1)} %bitcast.11), calls=%async_computation.3 | async-start | bytes 8388608
  109.7 48.5 %collective-permute-start.11 = (bf16[256,4224]{1,0:T(8,128)(2,1)S(1)}, bf16[256,4224]{1,0:T(8,128)(2,1)S(1)}, u32[]{:S(2)}, u32[]{:S(2)}) collective-permute-start(bf16[256,4224]{1,0:T(8,128)(2,1)S(1)} %collective-permute-done.6.refs_0_.refs_2_), channel_id=1, source_target_pairs={{4,0},{5,1},{6,2},{7,3},{8,12},{9,13},{10,14},{11,15},{20,16},{21,... | collective-permute-start | bytes 6488072 | tf_op jit(solution)/shard_map/rows_outward_far/ppermute | solution.py:80
  114.7 13.4 %collective-permute-start.12 = (bf16[64,4224]{1,0:T(8,128)(2,1)S(1)}, bf16[64,4224]{1,0:T(8,128)(2,1)S(1)}, u32[]{:S(2)}, u32[]{:S(2)}) collective-permute-start(bf16[64,4224]{1,0:T(8,128)(2,1)S(1)} %get-tuple-element.131), channel_id=1, source_target_pairs={{0,1},{1,0},{2,3},{3,2},{4,5},{5,4},{6,7},{7,6},{8,9},{9,8},{10,11... | collective-permute-start | bytes 1622024 | tf_op jit(solution)/shard_map/out_2_1/ppermute | solution.py:80
  114.8 15.1 %collective-permute-start.13 = (bf16[64,4224]{1,0:T(8,128)(2,1)S(1)}, bf16[64,4224]{1,0:T(8,128)(2,1)S(1)}, u32[]{:S(2)}, u32[]{:S(2)}) collective-permute-start(bf16[64,4224]{1,0:T(8,128)(2,1)S(1)} %get-tuple-element.132), channel_id=1, source_target_pairs={{0,2},{1,3},{2,0},{3,1},{4,6},{5,7},{6,4},{7,5},{8,10},{9,11},{10,... | collective-permute-start | bytes 1622024 | tf_op jit(solution)/shard_map/out_2_2/ppermute | solution.py:80
  116.3 24.3 %collective-permute-start.14 = (bf16[64,4224]{1,0:T(8,128)(2,1)S(1)}, bf16[64,4224]{1,0:T(8,128)(2,1)S(1)}, u32[]{:S(2)}, u32[]{:S(2)}) collective-permute-start(bf16[64,4224]{1,0:T(8,128)(2,1)S(1)} %get-tuple-element.133), channel_id=1, source_target_pairs={{0,3},{1,2},{2,1},{3,0},{4,7},{5,6},{6,5},{7,4},{8,11},{9,10},{10,... | collective-permute-start | bytes 1622024 | tf_op jit(solution)/shard_map/out_2_3/ppermute | solution.py:80
  116.6 3.7 collective-permute-start.15
  140.6 14.7 %collective-permute-start.16 = (bf16[64,4096]{1,0:T(8,128)(2,1)S(1)}, bf16[64,4096]{1,0:T(8,128)(2,1)S(1)}, u32[]{:S(2)}, u32[]{:S(2)}) collective-permute-start(bf16[64,4096]{1,0:T(8,128)(2,1)S(1)} %get-tuple-element.146), channel_id=1, source_target_pairs={{0,2},{1,3},{2,0},{3,1},{4,6},{5,7},{6,4},{7,5},{8,10},{9,11},{10,... | collective-permute-start | bytes 1572872 | tf_op jit(solution)/shard_map/back_1_0_2/ppermute | solution.py:80
  142.1 20.2 %collective-permute-start.21 = (bf16[64,4096]{1,0:T(8,128)(2,1)S(1)}, bf16[64,4096]{1,0:T(8,128)(2,1)S(1)}, u32[]{:S(2)}, u32[]{:S(2)}) collective-permute-start(bf16[64,4096]{1,0:T(8,128)(2,1)S(1)} %get-tuple-element.156), channel_id=1, source_target_pairs={{0,1},{1,0},{2,3},{3,2},{4,5},{5,4},{6,7},{7,6},{8,9},{9,8},{10,11... | collective-permute-start | bytes 1572872 | tf_op jit(solution)/shard_map/back_1_0_1/ppermute | solution.py:80
  142.4 23.5 %collective-permute-start.22 = (bf16[64,4096]{1,0:T(8,128)(2,1)S(1)}, bf16[64,4096]{1,0:T(8,128)(2,1)S(1)}, u32[]{:S(2)}, u32[]{:S(2)}) collective-permute-start(bf16[64,4096]{1,0:T(8,128)(2,1)S(1)} %get-tuple-element.157), channel_id=1, source_target_pairs={{0,3},{1,2},{2,1},{3,0},{4,7},{5,6},{6,5},{7,4},{8,11},{9,10},{10,... | collective-permute-start | bytes 1572872 | tf_op jit(solution)/shard_map/back_1_0_3/ppermute | solution.py:80
  160.4 23.3 %collective-permute-start.17 = (bf16[64,4224]{1,0:T(8,128)(2,1)S(1)}, bf16[64,4224]{1,0:T(8,128)(2,1)S(1)}, u32[]{:S(2)}, u32[]{:S(2)}) collective-permute-start(bf16[64,4224]{1,0:T(8,128)(2,1)S(1)} %get-tuple-element.151), channel_id=1, source_target_pairs={{0,1},{1,0},{2,3},{3,2},{4,5},{5,4},{6,7},{7,6},{8,9},{9,8},{10,11... | collective-permute-start | bytes 1622024 | tf_op jit(solution)/shard_map/out_3_1/ppermute | solution.py:80
  160.4 23.2 %collective-permute-start.18 = (bf16[64,4224]{1,0:T(8,128)(2,1)S(1)}, bf16[64,4224]{1,0:T(8,128)(2,1)S(1)}, u32[]{:S(2)}, u32[]{:S(2)}) collective-permute-start(bf16[64,4224]{1,0:T(8,128)(2,1)S(1)} %get-tuple-element.152), channel_id=1, source_target_pairs={{0,2},{1,3},{2,0},{3,1},{4,6},{5,7},{6,4},{7,5},{8,10},{9,11},{10,... | collective-permute-start | bytes 1622024 | tf_op jit(solution)/shard_map/out_3_2/ppermute | solution.py:80
  162.0 27.1 %collective-permute-start.19 = (bf16[64,4224]{1,0:T(8,128)(2,1)S(1)}, bf16[64,4224]{1,0:T(8,128)(2,1)S(1)}, u32[]{:S(2)}, u32[]{:S(2)}) collective-permute-start(bf16[64,4224]{1,0:T(8,128)(2,1)S(1)} %get-tuple-element.153), channel_id=1, source_target_pairs={{0,3},{1,2},{2,1},{3,0},{4,7},{5,6},{6,5},{7,4},{8,11},{9,10},{10,... | collective-permute-start | bytes 1622024 | tf_op jit(solution)/shard_map/out_3_3/ppermute | solution.py:80
  167.5 54.8 %collective-permute-start.27 = (bf16[256,4096]{1,0:T(8,128)(2,1)S(1)}, bf16[256,4096]{1,0:T(8,128)(2,1)S(1)}, u32[]{:S(2)}, u32[]{:S(2)}) collective-permute-start(bf16[256,4096]{1,0:T(8,128)(2,1)S(1)} %combine.6), channel_id=1, source_target_pairs={{0,4},{1,5},{2,6},{3,7},{12,8},{13,9},{14,10},{15,11},{16,20},{17,... | collective-permute-start | bytes 6291464 | tf_op jit(solution)/shard_map/sum_inward_one/ppermute | solution.py:80
  172.2 3.8 %collective-permute-start.20 = (f32[16,256]{1,0:T(8,128)S(1)}, f32[16,256]{1,0:T(8,128)S(1)}, u32[]{:S(2)}, u32[]{:S(2)}) collective-permute-start(f32[16,256]{1,0:T(8,128)S(1)} %get-tuple-element.145.chosen_ref), channel_id=1, source_target_pairs={{0,16},{16,0},{1,17},{17,1},{2,18},{18,2},{3,19},{19,3},{4,20},{20... | collective-permute-start | bytes 49160 | tf_op jit(solution)/shard_map/sums_2/ppermute | solution.py:327
  189.1 22.2 %collective-permute-start.28 = (bf16[64,4096]{1,0:T(8,128)(2,1)S(1)}, bf16[64,4096]{1,0:T(8,128)(2,1)S(1)}, u32[]{:S(2)}, u32[]{:S(2)}) collective-permute-start(bf16[64,4096]{1,0:T(8,128)(2,1)S(1)} %get-tuple-element.179), channel_id=1, source_target_pairs={{0,1},{1,0},{2,3},{3,2},{4,5},{5,4},{6,7},{7,6},{8,9},{9,8},{10,11... | collective-permute-start | bytes 1572872 | tf_op jit(solution)/shard_map/back_2_0_1/ppermute | solution.py:80
  189.2 22.1 %collective-permute-start.29 = (bf16[64,4096]{1,0:T(8,128)(2,1)S(1)}, bf16[64,4096]{1,0:T(8,128)(2,1)S(1)}, u32[]{:S(2)}, u32[]{:S(2)}) collective-permute-start(bf16[64,4096]{1,0:T(8,128)(2,1)S(1)} %get-tuple-element.180), channel_id=1, source_target_pairs={{0,2},{1,3},{2,0},{3,1},{4,6},{5,7},{6,4},{7,5},{8,10},{9,11},{10,... | collective-permute-start | bytes 1572872 | tf_op jit(solution)/shard_map/back_2_0_2/ppermute | solution.py:80
  190.7 23.4 %collective-permute-start.30 = (bf16[64,4096]{1,0:T(8,128)(2,1)S(1)}, bf16[64,4096]{1,0:T(8,128)(2,1)S(1)}, u32[]{:S(2)}, u32[]{:S(2)}) collective-permute-start(bf16[64,4096]{1,0:T(8,128)(2,1)S(1)} %get-tuple-element.181), channel_id=1, source_target_pairs={{0,3},{1,2},{2,1},{3,0},{4,7},{5,6},{6,5},{7,4},{8,11},{9,10},{10,... | collective-permute-start | bytes 1572872 | tf_op jit(solution)/shard_map/back_2_0_3/ppermute | solution.py:80
  199.9 3.8 %collective-permute-start.23 = (f32[16,256]{1,0:T(8,128)S(1)}, f32[16,256]{1,0:T(8,128)S(1)}, u32[]{:S(2)}, u32[]{:S(2)}) collective-permute-start(f32[16,256]{1,0:T(8,128)S(1)} %get-tuple-element.172.chosen_ref), channel_id=1, source_target_pairs={{0,16},{16,0},{1,17},{17,1},{2,18},{18,2},{3,19},{19,3},{4,20},{20... | collective-permute-start | bytes 49160 | tf_op jit(solution)/shard_map/sums_3/ppermute | solution.py:327
  214.9 30.9 %collective-permute-start.32 = (bf16[256,2048]{1,0:T(8,128)(2,1)S(1)}, bf16[256,2048]{1,0:T(8,128)(2,1)S(1)}, u32[]{:S(2)}, u32[]{:S(2)}) collective-permute-start(bf16[256,2048]{1,0:T(8,128)(2,1)S(1)} %combine.7), channel_id=1, source_target_pairs={{0,4},{1,5},{2,6},{3,7},{12,8},{13,9},{14,10},{15,11},{16,20},{17,... | collective-permute-start | bytes 3145736 | tf_op jit(solution)/shard_map/sum_inward_two_0/ppermute | solution.py:80
  219.1 4.7 %collective-permute-start.24 = (bf16[64,4096]{1,0:T(8,128)(2,1)S(1)}, bf16[64,4096]{1,0:T(8,128)(2,1)S(1)}, u32[]{:S(2)}, u32[]{:S(2)}) collective-permute-start(bf16[64,4096]{1,0:T(8,128)(2,1)S(1)} %get-tuple-element.175), channel_id=1, source_target_pairs={{0,1},{1,0},{2,3},{3,2},{4,5},{5,4},{6,7},{7,6},{8,9},{9,8},{10,11... | collective-permute-start | bytes 1572872 | tf_op jit(solution)/shard_map/back_3_0_1/ppermute | solution.py:80
  220.0 14.8 %collective-permute-start.25 = (bf16[64,4096]{1,0:T(8,128)(2,1)S(1)}, bf16[64,4096]{1,0:T(8,128)(2,1)S(1)}, u32[]{:S(2)}, u32[]{:S(2)}) collective-permute-start(bf16[64,4096]{1,0:T(8,128)(2,1)S(1)} %get-tuple-element.176), channel_id=1, source_target_pairs={{0,2},{1,3},{2,0},{3,1},{4,6},{5,7},{6,4},{7,5},{8,10},{9,11},{10,... | collective-permute-start | bytes 1572872 | tf_op jit(solution)/shard_map/back_3_0_2/ppermute | solution.py:80
  221.5 22.8 %collective-permute-start.26 = (bf16[64,4096]{1,0:T(8,128)(2,1)S(1)}, bf16[64,4096]{1,0:T(8,128)(2,1)S(1)}, u32[]{:S(2)}, u32[]{:S(2)}) collective-permute-start(bf16[64,4096]{1,0:T(8,128)(2,1)S(1)} %get-tuple-element.177), channel_id=1, source_target_pairs={{0,3},{1,2},{2,1},{3,0},{4,7},{5,6},{6,5},{7,4},{8,11},{9,10},{10,... | collective-permute-start | bytes 1572872 | tf_op jit(solution)/shard_map/back_3_0_3/ppermute | solution.py:80
  222.3 42.4 %collective-permute-start.34 = (bf16[256,2048]{1,0:T(8,128)(2,1)S(1)}, bf16[256,2048]{1,0:T(8,128)(2,1)S(1)}, u32[]{:S(2)}, u32[]{:S(2)}) collective-permute-start(bf16[256,2048]{1,0:T(8,128)(2,1)S(1)} %combine.8), channel_id=1, source_target_pairs={{0,4},{1,5},{2,6},{3,7},{12,8},{13,9},{14,10},{15,11},{16,20},{17,... | collective-permute-start | bytes 3145736 | tf_op jit(solution)/shard_map/sum_inward_two_1/ppermute | solution.py:80
  246.3 19.5 %collective-permute-start.33 = (bf16[256,2048]{1,0:T(8,128)(2,1)S(1)}, bf16[256,2048]{1,0:T(8,128)(2,1)S(1)}, u32[]{:S(2)}, u32[]{:S(2)}) collective-permute-start(bf16[256,2048]{1,0:T(8,128)(2,1)S(1)} %add_convert_fusion.7), channel_id=1, source_target_pairs={{4,8},{5,9},{6,10},{7,11},{8,4},{9,5},{10,6},{11,7},{20,24},{21,25... | collective-permute-start | bytes 3145736 | tf_op jit(solution)/shard_map/sum_middle_two_0/ppermute | solution.py:80
  247.1 40.1 %collective-permute-start.31 = (bf16[256,2048]{1,0:T(8,128)(2,1)S(1)}, bf16[256,2048]{1,0:T(8,128)(2,1)S(1)}, u32[]{:S(2)}, u32[]{:S(2)}) collective-permute-start(bf16[256,2048]{1,0:T(8,128)(2,1)S(1)} %combine.9), channel_id=1, source_target_pairs={{0,4},{1,5},{2,6},{3,7},{12,8},{13,9},{14,10},{15,11},{16,20},{17,... | collective-permute-start | bytes 3145736 | tf_op jit(solution)/shard_map/sum_inward_far_0/ppermute | solution.py:80
  250.4 59.2 %collective-permute-start.39 = (bf16[256,2048]{1,0:T(8,128)(2,1)S(1)}, bf16[256,2048]{1,0:T(8,128)(2,1)S(1)}, u32[]{:S(2)}, u32[]{:S(2)}) collective-permute-start(bf16[256,2048]{1,0:T(8,128)(2,1)S(1)} %combine.10), channel_id=1, source_target_pairs={{0,4},{1,5},{2,6},{3,7},{12,8},{13,9},{14,10},{15,11},{16,20},{17,... | collective-permute-start | bytes 3145736 | tf_op jit(solution)/shard_map/sum_inward_far_1/ppermute | solution.py:80
  265.1 23.2 %collective-permute-start.40 = (bf16[256,2048]{1,0:T(8,128)(2,1)S(1)}, bf16[256,2048]{1,0:T(8,128)(2,1)S(1)}, u32[]{:S(2)}, u32[]{:S(2)}) collective-permute-start(bf16[256,2048]{1,0:T(8,128)(2,1)S(1)} %add_convert_fusion.5), channel_id=1, source_target_pairs={{4,8},{5,9},{6,10},{7,11},{8,4},{9,5},{10,6},{11,7},{20,24},{21,25... | collective-permute-start | bytes 3145736 | tf_op jit(solution)/shard_map/sum_middle_two_1/ppermute | solution.py:80
  287.6 23.3 %collective-permute-start.35 = (bf16[256,2048]{1,0:T(8,128)(2,1)S(1)}, bf16[256,2048]{1,0:T(8,128)(2,1)S(1)}, u32[]{:S(2)}, u32[]{:S(2)}) collective-permute-start(bf16[256,2048]{1,0:T(8,128)(2,1)S(1)} %add_convert_fusion.6), channel_id=1, source_target_pairs={{4,8},{5,9},{6,10},{7,11},{8,4},{9,5},{10,6},{11,7},{20,24},{21,25... | collective-permute-start | bytes 3145736 | tf_op jit(solution)/shard_map/sum_middle_far_0/ppermute | solution.py:80
  310.1 2.5 collective-permute-start.42
  311.3 32.7 %collective-permute-start.41 = (bf16[256,2048]{1,0:T(8,128)(2,1)S(1)}, bf16[256,2048]{1,0:T(8,128)(2,1)S(1)}, u32[]{:S(2)}, u32[]{:S(2)}) collective-permute-start(bf16[256,2048]{1,0:T(8,128)(2,1)S(1)} %add_convert_fusion.4), channel_id=1, source_target_pairs={{4,0},{5,1},{6,2},{7,3},{8,12},{9,13},{10,14},{11,15},{20,16},{21,... | collective-permute-start | bytes 3145736 | tf_op jit(solution)/shard_map/sum_outward_far_0/ppermute | solution.py:80
  344.3 28.0 %collective-permute-start.43 = (bf16[256,2048]{1,0:T(8,128)(2,1)S(1)}, bf16[256,2048]{1,0:T(8,128)(2,1)S(1)}, u32[]{:S(2)}, u32[]{:S(2)}) collective-permute-start(bf16[256,2048]{1,0:T(8,128)(2,1)S(1)} %add_convert_fusion.1), channel_id=1, source_target_pairs={{4,0},{5,1},{6,2},{7,3},{8,12},{9,13},{10,14},{11,15},{20,16},{21,... | collective-permute-start | bytes 3145736 | tf_op jit(solution)/shard_map/sum_outward_far_1/ppermute | solution.py:80
  345.6 2.0 collective-permute-start.36
  345.7 14.8 %collective-permute-start.37 = (bf16[64,4096]{1,0:T(8,128)(2,1)S(1)}, bf16[64,4096]{1,0:T(8,128)(2,1)S(1)}, u32[]{:S(2)}, u32[]{:S(2)}) collective-permute-start(bf16[64,4096]{1,0:T(8,128)(2,1)S(1)} %get-tuple-element.197), channel_id=1, source_target_pairs={{0,2},{1,3},{2,0},{3,1},{4,6},{5,7},{6,4},{7,5},{8,10},{9,11},{10,... | collective-permute-start | bytes 1572872 | tf_op jit(solution)/shard_map/back_0_0_2/ppermute | solution.py:80
  347.3 23.6 %collective-permute-start.38 = (bf16[64,4096]{1,0:T(8,128)(2,1)S(1)}, bf16[64,4096]{1,0:T(8,128)(2,1)S(1)}, u32[]{:S(2)}, u32[]{:S(2)}) collective-permute-start(bf16[64,4096]{1,0:T(8,128)(2,1)S(1)} %get-tuple-element.198), channel_id=1, source_target_pairs={{0,3},{1,2},{2,1},{3,0},{4,7},{5,6},{6,5},{7,4},{8,11},{9,10},{10,... | collective-permute-start | bytes 1572872 | tf_op jit(solution)/shard_map/back_0_0_3/ppermute | solution.py:80

commit v2 on v1

--- a/solution.py
+++ b/solution.py
@@ -73,6 +73,7 @@
 MIDDLE = outer_pairs([(1, 2), (2, 1)])
 OUTWARD = outer_pairs([(1, 0), (2, 3)])
 INWARD = outer_pairs([(0, 1), (3, 2)])
+SKIP = outer_pairs([(1, 3), (2, 0)])
 FLIPS = {1: inner_pairs(1), 2: inner_pairs(2), 3: inner_pairs(3)}
 
 
@@ -384,8 +385,8 @@
             added = after(added, spreads[t + 1])
         if t == 2:
             back[1] = combined(spreads[1], returned[1], 1, spreads[3])
-            with jax.named_scope("sum_inward_one"):
-                from_end = move(back[1][0], INWARD)
+            with jax.named_scope("sum_ends"):
+                from_end = move(back[1][0], ENDS)
             added = after(added, *back[1])
         waiting[t] = decoded(t, picks, chosen, added)
     last = leave(3, waiting[3])
@@ -403,7 +404,7 @@
     for i in range(count):
         with jax.named_scope(f"sum_inward_far_{i}"):
             from_far.append(move(back[3][i], INWARD))
-    twos, threes, ones, results = [], [], [], []
+    twos, ones, results = [], [], []
     seen = tuple(back[3])
     for i in range(count):
         got = after(from_two[i], *seen)
@@ -412,17 +413,18 @@
         seen = (got,)
     for i in range(count):
         twos[i] = after(twos[i], *seen)
-        got = after(from_far[i], twos[i])
-        with jax.named_scope(f"sum_middle_far_{i}"):
-            threes.append(move(plus(back[3][i], got), MIDDLE))
+        if i == 0:
+            returned[0] = leave(0, waiting[0], twos[0])
+            got = after(from_far[i], twos[i])
+        else:
+            pieces = returned[0][0]
+            pieces[2] = after(pieces[2], twos[i])
+            got = after(from_far[i], pieces[2], ones[i - 1])
+        with jax.named_scope(f"sum_skip_far_{i}"):
+            ones.append(move(plus(back[3][i], got), SKIP))
         seen = (got,)
-    for i in range(count):
-        got = after(threes[i], *seen)
-        with jax.named_scope(f"sum_outward_far_{i}"):
-            ones.append(move(plus(back[1][0][:, cols[i]], got), OUTWARD))
-        seen = (ones[i],)
-    returned[0] = leave(0, waiting[0], threes[0])
-    back[0] = combined(spreads[0], returned[0], 1)
+    back[0] = combined(spreads[0], returned[0], 1, *seen)
+    ones[-1] = after(ones[-1], *back[0])
     for i in range(count):
         total = dec_bias[cols[i]]
         for value in (back[0][0][:, cols[i]], from_end[:, cols[i]], twos[i], ones[i]):

time: 382 us -> 355 us (0.929)
  waiting for transfers between devices: 220 us -> 197 us
    ppermute x40 -> x38, waiting for transfers between devices: 213 us -> 190 us  [move(): return lax.ppermute(value, 'blocks', pairs)]
    ppermute x40 -> x38, starting transfers between devices: 46.4 us -> 44.1 us  [move(): return lax.ppermute(value, 'blocks', pairs)]
  transfers between devices with their start and end apart: 44 -> 42, of which waited for: 25 -> 27; matrix products, arithmetic and copies ran while one was open for 1% -> 0% of each run, Pallas kernels for 23% -> 25%
where the time goes in v2:
time: 355 us; the launch traced here: 350 us
  waiting for transfers between devices  197 us (55%)
  Pallas kernels  86.1 us (24%)
  starting transfers between devices  50.5 us (14%)
  local copies, waits for them, and re-layouts  7.82 us (2%)
  other arithmetic  7.63 us (2%)
    ppermute x38, waiting for transfers between devices, move(): return lax.ppermute(value, 'blocks', pairs)  190 us
    ppermute x38, starting transfers between devices, move(): return lax.ppermute(value, 'blocks', pairs)  44.1 us
    pallas_call x4, Pallas kernels, encode(): call(kernel, 'encode', (width // BLOCK,), [pl.BlockSpec((cap, BLOCK), lam...  36.8 us
    pallas_call x4, Pallas kernels, decode(): call(functools.partial(decode_kernel, cap), 'decode', (width // BLOCK,),...  30.8 us
    pallas_call x4, Pallas kernels, dispatch(): call(kernel, 'dispatch', (3,), [pl.BlockSpec((8, INNER * cap), lambda j:...  12.1 us
  transfers between devices with their start and end apart: 42, of which 27 were waited for; matrix products, arithmetic and copies ran while one was open for 0% of the time, Pallas kernels for 25%

profile of v2, /device:TPU:0, one launch (start us, length us, event | category | flops | bytes accessed | tf_op | source)
XLA Modules:
  0.0 349.9 jit_solution(8600614685534783147)
XLA Ops:
  2.0 1.8 pad_maximum_fusion.refs_0_.refs_1_
  3.7 3.1 collective-permute-start.4
  6.8 2.0 collective-permute-start.5
  8.9 2.9 dispatch.4
  11.9 1.5 collective-permute-start.1
  14.0 13.2 %collective-permute-done.1.refs_2_.refs_6_ = bf16[64,4224]{1,0:T(8,128)(2,1)} collective-permute-done((bf16[64,4224]{1,0:T(8,128)(2,1)}, bf16[64,4224]{1,0:T(8,128)(2,1)}, u32[]{:S(2)}, u32[]{:S(2)}) %collective-permute-start.1) | collective-permute-done | bytes 540704 | tf_op jit(solution)/shard_map/out_0_2/ppermute | solution.py:81
  27.3 10.8 %collective-permute-done.2.refs_3_.refs_7_ = bf16[64,4224]{1,0:T(8,128)(2,1)} collective-permute-done((bf16[64,4224]{1,0:T(8,128)(2,1)}, bf16[64,4224]{1,0:T(8,128)(2,1)}, u32[]{:S(2)}, u32[]{:S(2)}) %collective-permute-start.2) | collective-permute-done | bytes 540704 | tf_op jit(solution)/shard_map/out_0_3/ppermute | solution.py:81
  38.1 3.4 copy-done
  41.5 10.3 %encode.4 = (f32[16,256]{1,0:T(8,128)S(1)}, s32[256,128]{1,0:T(8,128)S(1)}) custom-call(bf16[64,4224]{1,0:T(8,128)(2,1)S(1)} %get-tuple-element.109.refs_0_.refs_4_, bf16[64,4224]{1,0:T(8,128)(2,1)S(1)} %collective-permute-done.refs_1_.refs_5_, bf16[64,4224]{1,0:T(8,128)(2,1)} %collective-permute-done.1.refs_2_.refs_6_, ...), custom_call_target="tpu_custom_call" | custom-call | tf_op jit(solution)/shard_map/encode/pallas_call | solution.py:199
  51.7 2.2 collective-permute-done.4.refs_0_.refs_1_
  54.9 1.9 collective-permute-start.7
  56.9 1.7 collective-permute-start.3
  58.6 3.5 dispatch.5
  62.2 1.6 collective-permute-start.8
  64.3 3.4 copy-done.1
  67.7 7.6 %decode.4 = (bf16[64,4096]{1,0:T(8,128)(2,1)S(1)}, bf16[64,4096]{1,0:T(8,128)(2,1)S(1)}, bf16[64,4096]{1,0:T(8,128)(2,1)S(1)}, bf16[64,4096]{1,0:T(8,128)(2,1)S(1)}) custom-call(f32[16,256]{1,0:T(8,128)S(1)} %get-tuple-element.113.chosen_ref, f32[16,256]{1,0:T(8,128)S(1)} %collective-permute-done.3.added_ref, s32[256,128]{1,0:T(8,128)S(1)} %get-tuple-element.117.picks_ref, ...), custom_call_target="tpu_custom_call" | custom-call | tf_op jit(solution)/shard_map/decode/pallas_call | solution.py:246
  76.7 11.6 %collective-permute-done.9.refs_2_.refs_6_ = bf16[64,4224]{1,0:T(8,128)(2,1)S(1)} collective-permute-done((bf16[64,4224]{1,0:T(8,128)(2,1)S(1)}, bf16[64,4224]{1,0:T(8,128)(2,1)S(1)}, u32[]{:S(2)}, u32[]{:S(2)}) %collective-permute-start.9) | collective-permute-done | bytes 540704 | tf_op jit(solution)/shard_map/out_1_2/ppermute | solution.py:81
  88.3 8.9 %encode.5 = (f32[16,256]{1,0:T(8,128)S(1)}, s32[256,128]{1,0:T(8,128)S(1)}) custom-call(bf16[64,4224]{1,0:T(8,128)(2,1)S(1)} %get-tuple-element.127.refs_0_.refs_4_, bf16[64,4224]{1,0:T(8,128)(2,1)S(1)} %collective-permute-done.8.refs_1_.refs_5_, bf16[64,4224]{1,0:T(8,128)(2,1)S(1)} %collective-permute-done.9.refs_2_.refs_6_, ...), custom_call_target="tpu_custom_call" | custom-call | tf_op jit(solution)/shard_map/encode/pallas_call | solution.py:199
  97.2 12.4 %collective-permute-done.7.refs_1_.refs_3_ = bf16[256,4224]{1,0:T(8,128)(2,1)S(1)} collective-permute-done((bf16[256,4224]{1,0:T(8,128)(2,1)}, bf16[256,4224]{1,0:T(8,128)(2,1)S(1)}, u32[]{:S(2)}, u32[]{:S(2)}) %collective-permute-start.7) | collective-permute-done | bytes 2162720 | tf_op jit(solution)/shard_map/rows_outward_two/ppermute | solution.py:81
  109.7 1.5 collective-permute-start.16
  111.1 3.6 %dispatch.6 = (bf16[256,256]{1,0:T(8,128)(2,1)S(1)}, bf16[64,4224]{1,0:T(8,128)(2,1)S(1)}, bf16[64,4224]{1,0:T(8,128)(2,1)S(1)}, bf16[64,4224]{1,0:T(8,128)(2,1)S(1)}, bf16[64,4224]{1,0:T(8,128)(2,1)S(1)}) custom-call(f32[8,256]{1,0:T(8,128)S(1)} %pad.12.slots_ref, bf16[256,4224]{1,0:T(8,128)(2,1)} %collective-permute-done.5.refs_0_.refs_2_, ...), custom_call_target="tpu_custom_call" | custom-call | tf_op jit(solution)/shard_map/dispatch/pallas_call | solution.py:142
  114.8 1.6 collective-permute-start.12
  116.6 1.5 collective-permute-start.14
  118.2 2.2 collective-permute-done.14.added_ref
  120.4 7.6 %decode.5 = (bf16[64,4096]{1,0:T(8,128)(2,1)S(1)}, bf16[64,4096]{1,0:T(8,128)(2,1)S(1)}, bf16[64,4096]{1,0:T(8,128)(2,1)S(1)}, bf16[64,4096]{1,0:T(8,128)(2,1)S(1)}) custom-call(f32[16,256]{1,0:T(8,128)S(1)} %get-tuple-element.131.chosen_ref, f32[16,256]{1,0:T(8,128)S(1)} %collective-permute-done.14.added_ref, s32[256,128]{1,0:T(8,128)S(1)} %get-tuple-element.139.picks_ref, ...), custom_call_target="tpu_custom_call" | custom-call | tf_op jit(solution)/shard_map/decode/pallas_call | solution.py:246
  128.1 1.9 collective-permute-done.12.refs_2_.refs_6_
  129.9 10.7 %collective-permute-done.13.refs_3_.refs_7_ = bf16[64,4224]{1,0:T(8,128)(2,1)S(1)} collective-permute-done((bf16[64,4224]{1,0:T(8,128)(2,1)S(1)}, bf16[64,4224]{1,0:T(8,128)(2,1)S(1)}, u32[]{:S(2)}, u32[]{:S(2)}) %collective-permute-start.13) | collective-permute-done | bytes 540704 | tf_op jit(solution)/shard_map/out_2_3/ppermute | solution.py:81
  140.6 1.5 collective-permute-start.17
  142.7 8.8 %encode.6 = (f32[16,256]{1,0:T(8,128)S(1)}, s32[256,128]{1,0:T(8,128)S(1)}) custom-call(bf16[64,4224]{1,0:T(8,128)(2,1)S(1)} %get-tuple-element.144.refs_0_.refs_4_, bf16[64,4224]{1,0:T(8,128)(2,1)S(1)} %collective-permute-done.11.refs_1_.refs_5_, bf16[64,4224]{1,0:T(8,128)(2,1)S(1)} %collective-permute-done.12.refs_2_.refs_6_, ...), custom_call_target="tpu_custom_call" | custom-call | tf_op jit(solution)/shard_map/encode/pallas_call | solution.py:199
  151.6 3.7 %collective-permute-done.17.refs_2_ = bf16[64,4096]{1,0:T(8,128)(2,1)S(1)} collective-permute-done((bf16[64,4096]{1,0:T(8,128)(2,1)S(1)}, bf16[64,4096]{1,0:T(8,128)(2,1)S(1)}, u32[]{:S(2)}, u32[]{:S(2)}) %collective-permute-start.17) | collective-permute-done | bytes 524320 | tf_op jit(solution)/shard_map/back_1_0_2/ppermute | solution.py:81
  155.3 2.9 collective-permute-done.16.refs_1_.refs_3_
  158.2 2.1 dispatch.7
  160.4 1.6 collective-permute-start.21
  162.3 3.6 %collective-permute-done.19.refs_3_ = bf16[64,4096]{1,0:T(8,128)(2,1)S(1)} collective-permute-done((bf16[64,4096]{1,0:T(8,128)(2,1)S(1)}, bf16[64,4096]{1,0:T(8,128)(2,1)S(1)}, u32[]{:S(2)}, u32[]{:S(2)}) %collective-permute-start.19) | collective-permute-done | bytes 524320 | tf_op jit(solution)/shard_map/back_1_0_3/ppermute | solution.py:81
  165.9 1.5 combine.6
  167.5 2.5 collective-permute-start.31
  170.0 1.5 collective-permute-start.15
  171.5 2.2 collective-permute-done.15.added_ref
  173.7 7.8 %decode.6 = (bf16[64,4096]{1,0:T(8,128)(2,1)S(1)}, bf16[64,4096]{1,0:T(8,128)(2,1)S(1)}, bf16[64,4096]{1,0:T(8,128)(2,1)S(1)}, bf16[64,4096]{1,0:T(8,128)(2,1)S(1)}) custom-call(f32[16,256]{1,0:T(8,128)S(1)} %get-tuple-element.148.chosen_ref, f32[16,256]{1,0:T(8,128)S(1)} %collective-permute-done.15.added_ref, s32[256,128]{1,0:T(8,128)S(1)} %get-tuple-element.163.picks_ref, ...), custom_call_target="tpu_custom_call" | custom-call | tf_op jit(solution)/shard_map/decode/pallas_call | solution.py:246
  181.6 7.5 %collective-permute-done.22.refs_3_.refs_7_ = bf16[64,4224]{1,0:T(8,128)(2,1)S(1)} collective-permute-done((bf16[64,4224]{1,0:T(8,128)(2,1)S(1)}, bf16[64,4224]{1,0:T(8,128)(2,1)S(1)}, u32[]{:S(2)}, u32[]{:S(2)}) %collective-permute-start.22) | collective-permute-done | bytes 540704 | tf_op jit(solution)/shard_map/out_3_3/ppermute | solution.py:81
  189.5 1.5 collective-permute-start.24
  191.0 8.8 %encode.7 = (f32[16,256]{1,0:T(8,128)S(1)}, s32[256,128]{1,0:T(8,128)S(1)}) custom-call(bf16[64,4224]{1,0:T(8,128)(2,1)S(1)} %get-tuple-element.179.refs_0_.refs_4_, bf16[64,4224]{1,0:T(8,128)(2,1)S(1)} %collective-permute-done.20.refs_1_.refs_5_, bf16[64,4224]{1,0:T(8,128)(2,1)S(1)} %collective-permute-done.21.refs_2_.refs_6_, ...), custom_call_target="tpu_custom_call" | custom-call | tf_op jit(solution)/shard_map/encode/pallas_call | solution.py:199
  199.9 1.6 collective-permute-start.26
  201.5 2.2 collective-permute-done.26.added_ref
  203.7 7.6 %decode.7 = (bf16[64,4096]{1,0:T(8,128)(2,1)S(1)}, bf16[64,4096]{1,0:T(8,128)(2,1)S(1)}, bf16[64,4096]{1,0:T(8,128)(2,1)S(1)}, bf16[64,4096]{1,0:T(8,128)(2,1)S(1)}) custom-call(f32[16,256]{1,0:T(8,128)S(1)} %get-tuple-element.180.chosen_ref, f32[16,256]{1,0:T(8,128)S(1)} %collective-permute-done.26.added_ref, s32[256,128]{1,0:T(8,128)S(1)} %get-tuple-element.181.picks_ref, ...), custom_call_target="tpu_custom_call" | custom-call | tf_op jit(solution)/shard_map/decode/pallas_call | solution.py:246
  211.3 2.5 collective-permute-done.25.refs_3_
  214.6 4.3 %collective-permute-start.27 = (bf16[256,2048]{1,0:T(8,128)(2,1)S(1)}, bf16[256,2048]{1,0:T(8,128)(2,1)S(1)}, u32[]{:S(2)}, u32[]{:S(2)}) collective-permute-start(bf16[256,2048]{1,0:T(8,128)(2,1)S(1)} %combine.7), channel_id=1, source_target_pairs={{0,4},{1,5},{2,6},{3,7},{12,8},{13,9},{14,10},{15,11},{16,20},{17,... | collective-permute-start | bytes 3145736 | tf_op jit(solution)/shard_map/sum_inward_two_0/ppermute | solution.py:81
  219.8 1.5 collective-permute-start.29
  222.3 1.6 collective-permute-start.33
  223.9 10.6 %collective-permute-done.29.refs_2_ = bf16[64,4096]{1,0:T(8,128)(2,1)S(1)} collective-permute-done((bf16[64,4096]{1,0:T(8,128)(2,1)S(1)}, bf16[64,4096]{1,0:T(8,128)(2,1)S(1)}, u32[]{:S(2)}, u32[]{:S(2)}) %collective-permute-start.29) | collective-permute-done | bytes 524320 | tf_op jit(solution)/shard_map/back_3_0_2/ppermute | solution.py:81
  234.5 9.5 %collective-permute-done.30.refs_3_ = bf16[64,4096]{1,0:T(8,128)(2,1)S(1)} collective-permute-done((bf16[64,4096]{1,0:T(8,128)(2,1)S(1)}, bf16[64,4096]{1,0:T(8,128)(2,1)S(1)}, u32[]{:S(2)}, u32[]{:S(2)}) %collective-permute-start.30) | collective-permute-done | bytes 524320 | tf_op jit(solution)/shard_map/back_3_0_3/ppermute | solution.py:81
  246.8 3.4 collective-permute-start.37
  251.5 13.2 %collective-permute-done.33 = bf16[256,2048]{1,0:T(8,128)(2,1)S(1)} collective-permute-done((bf16[256,2048]{1,0:T(8,128)(2,1)S(1)}, bf16[256,2048]{1,0:T(8,128)(2,1)S(1)}, u32[]{:S(2)}, u32[]{:S(2)}) %collective-permute-start.33) | collective-permute-done | bytes 1048608 | tf_op jit(solution)/shard_map/sum_inward_two_1/ppermute | solution.py:81
  265.9 21.3 %collective-permute-done.37 = bf16[256,2048]{1,0:T(8,128)(2,1)S(1)} collective-permute-done((bf16[256,2048]{1,0:T(8,128)(2,1)S(1)}, bf16[256,2048]{1,0:T(8,128)(2,1)S(1)}, u32[]{:S(2)}, u32[]{:S(2)}) %collective-permute-start.37) | collective-permute-done | bytes 1048608 | tf_op jit(solution)/shard_map/sum_inward_far_0/ppermute | solution.py:81
  288.9 1.6 collective-permute-start.35
  290.4 12.7 %collective-permute-done.35.refs_2_ = bf16[64,4096]{1,0:T(8,128)(2,1)S(1)} collective-permute-done((bf16[64,4096]{1,0:T(8,128)(2,1)S(1)}, bf16[64,4096]{1,0:T(8,128)(2,1)S(1)}, u32[]{:S(2)}, u32[]{:S(2)}) %collective-permute-start.35) | collective-permute-done | bytes 524320 | tf_op jit(solution)/shard_map/back_0_0_2/ppermute | solution.py:81
  303.1 6.5 %collective-permute-done.39 = bf16[256,2048]{1,0:T(8,128)(2,1)S(1)} collective-permute-done((bf16[256,2048]{1,0:T(8,128)(2,1)S(1)}, bf16[256,2048]{1,0:T(8,128)(2,1)S(1)}, u32[]{:S(2)}, u32[]{:S(2)}) %collective-permute-start.39) | collective-permute-done | bytes 1048608 | tf_op jit(solution)/shard_map/sum_inward_far_1/ppermute | solution.py:81
  309.7 8.2 %collective-permute-done.40 = bf16[256,2048]{1,0:T(8,128)(2,1)S(1)} collective-permute-done((bf16[256,2048]{1,0:T(8,128)(2,1)S(1)}, bf16[256,2048]{1,0:T(8,128)(2,1)S(1)}, u32[]{:S(2)}, u32[]{:S(2)}) %collective-permute-start.40) | collective-permute-done | bytes 1048608 | tf_op jit(solution)/shard_map/sum_skip_far_0/ppermute | solution.py:81
  319.8 1.5 collective-permute-start.38
  321.6 12.0 %collective-permute-done.38.refs_3_ = bf16[64,4096]{1,0:T(8,128)(2,1)S(1)} collective-permute-done((bf16[64,4096]{1,0:T(8,128)(2,1)S(1)}, bf16[64,4096]{1,0:T(8,128)(2,1)S(1)}, u32[]{:S(2)}, u32[]{:S(2)}) %collective-permute-start.38) | collective-permute-done | bytes 524320 | tf_op jit(solution)/shard_map/back_0_0_3/ppermute | solution.py:81
  333.6 1.5 combine.11
  335.1 11.2 %collective-permute-done.41 = bf16[256,2048]{1,0:T(8,128)(2,1)S(1)} collective-permute-done((bf16[256,2048]{1,0:T(8,128)(2,1)S(1)}, bf16[256,2048]{1,0:T(8,128)(2,1)S(1)}, u32[]{:S(2)}, u32[]{:S(2)}) %collective-permute-start.41) | collective-permute-done | bytes 1048608 | tf_op jit(solution)/shard_map/sum_skip_far_1/ppermute | solution.py:81
  346.3 1.9 add_convert_fusion.2
  348.2 1.5 pad_maximum_fusion.1
  (75 shorter events, 19.1 us)
Async XLA Ops:
  1.9 6.9 %copy-start.2 = (f32[4096]{0:T(1024)S(1)}, f32[4096]{0:T(1024)}, u32[]{:S(2)}) copy-start(f32[4096]{0:T(1024)} %param.8) | copy-start | bytes 49156
  3.7 50.2 %collective-permute-start.4 = (bf16[256,4224]{1,0:T(8,128)(2,1)S(1)}, bf16[256,4224]{1,0:T(8,128)(2,1)}, u32[]{:S(2)}, u32[]{:S(2)}) collective-permute-start(bf16[256,4224]{1,0:T(8,128)(2,1)S(1)} %pad_maximum_fusion.refs_0_.refs_1_), channel_id=1, source_target_pairs={{0,4},{1,5},{2,6},{3,7},{4,0},{5,1},{6,2},{7,3},{8,12},{9,13},{10,... | collective-permute-start | bytes 6488072 | tf_op jit(solution)/shard_map/rows_ends/ppermute | solution.py:81
  6.8 47.1 %collective-permute-start.5 = (bf16[256,4224]{1,0:T(8,128)(2,1)S(1)}, bf16[256,4224]{1,0:T(8,128)(2,1)}, u32[]{:S(2)}, u32[]{:S(2)}) collective-permute-start(bf16[256,4224]{1,0:T(8,128)(2,1)S(1)} %pad_maximum_fusion.refs_0_.refs_1_), channel_id=1, source_target_pairs={{4,8},{5,9},{6,10},{7,11},{8,4},{9,5},{10,6},{11,7},{20,24},{21,25... | collective-permute-start | bytes 6488072 | tf_op jit(solution)/shard_map/rows_middle/ppermute | solution.py:81
  8.9 4.8 %copy-start.3 = (f32[1,1024]{1,0:T(1,128)S(1)}, f32[1,1024]{1,0:T(1,128)}, u32[]{:S(2)}) copy-start(f32[1,1024]{1,0:T(1,128)} %param.13) | copy-start | bytes 12292
  11.9 2.1 collective-permute-start
  11.9 15.4 %collective-permute-start.1 = (bf16[64,4224]{1,0:T(8,128)(2,1)}, bf16[64,4224]{1,0:T(8,128)(2,1)}, u32[]{:S(2)}, u32[]{:S(2)}) collective-permute-start(bf16[64,4224]{1,0:T(8,128)(2,1)} %get-tuple-element.111), channel_id=1, source_target_pairs={{0,2},{1,3},{2,0},{3,1},{4,6},{5,7},{6,4},{7,5},{8,10},{9,11},{10,... | collective-permute-start | bytes 1622024 | tf_op jit(solution)/shard_map/out_0_2/ppermute | solution.py:81
  13.4 24.7 %collective-permute-start.2 = (bf16[64,4224]{1,0:T(8,128)(2,1)}, bf16[64,4224]{1,0:T(8,128)(2,1)}, u32[]{:S(2)}, u32[]{:S(2)}) collective-permute-start(bf16[64,4224]{1,0:T(8,128)(2,1)} %get-tuple-element.112), channel_id=1, source_target_pairs={{0,3},{1,2},{2,1},{3,0},{4,7},{5,6},{6,5},{7,4},{8,11},{9,10},{10,... | collective-permute-start | bytes 1622024 | tf_op jit(solution)/shard_map/out_0_3/ppermute | solution.py:81
  38.1 3.4 copy-start
  41.5 46.9 %slice-start = ((s8[8388608]{0:T(1024)(128)(4,1)}), s8[4194304]{0:T(1024)(128)(4,1)S(1)}, s32[]{:S(2)}) async-start(s8[8388608]{0:T(1024)(128)(4,1)} %bitcast.5), calls=%async_computation | async-start | bytes 8388608
  54.0 34.3 %slice-start.1 = ((s8[8388608]{0:T(1024)(128)(4,1)}), s8[4194304]{0:T(1024)(128)(4,1)S(1)}, s32[]{:S(2)}) async-start(s8[8388608]{0:T(1024)(128)(4,1)} %bitcast.5), calls=%async_computation.1 | async-start | bytes 8388608
  54.0 43.3 %collective-permute-start.6 = (bf16[256,4224]{1,0:T(8,128)(2,1)}, bf16[256,4224]{1,0:T(8,128)(2,1)S(1)}, u32[]{:S(2)}, u32[]{:S(2)}) collective-permute-start(bf16[256,4224]{1,0:T(8,128)(2,1)} %collective-permute-done.4.refs_0_.refs_1_), channel_id=1, source_target_pairs={{4,8},{5,9},{6,10},{7,11},{8,4},{9,5},{10,6},{11,7},{20,24},{21,25... | collective-permute-start | bytes 6488072 | tf_op jit(solution)/shard_map/rows_middle_far/ppermute | solution.py:81
  54.9 54.8 %collective-permute-start.7 = (bf16[256,4224]{1,0:T(8,128)(2,1)}, bf16[256,4224]{1,0:T(8,128)(2,1)S(1)}, u32[]{:S(2)}, u32[]{:S(2)}) collective-permute-start(bf16[256,4224]{1,0:T(8,128)(2,1)} %collective-permute-done.5.refs_0_.refs_2_), channel_id=1, source_target_pairs={{4,0},{5,1},{6,2},{7,3},{8,12},{9,13},{10,14},{11,15},{20,16},{21,... | collective-permute-start | bytes 6488072 | tf_op jit(solution)/shard_map/rows_outward_two/ppermute | solution.py:81
  56.9 6.9 %collective-permute-start.3 = (f32[16,256]{1,0:T(8,128)S(1)}, f32[16,256]{1,0:T(8,128)S(1)}, u32[]{:S(2)}, u32[]{:S(2)}) collective-permute-start(f32[16,256]{1,0:T(8,128)S(1)} %get-tuple-element.113.chosen_ref), channel_id=1, source_target_pairs={{0,16},{16,0},{1,17},{17,1},{2,18},{18,2},{3,19},{19,3},{4,20},{20... | collective-permute-start | bytes 49160 | tf_op jit(solution)/shard_map/sums_0/ppermute | solution.py:328
  62.1 14.6 %collective-permute-start.10 = (bf16[64,4224]{1,0:T(8,128)(2,1)S(1)}, bf16[64,4224]{1,0:T(8,128)(2,1)S(1)}, u32[]{:S(2)}, u32[]{:S(2)}) collective-permute-start(bf16[64,4224]{1,0:T(8,128)(2,1)S(1)} %get-tuple-element.126), channel_id=1, source_target_pairs={{0,3},{1,2},{2,1},{3,0},{4,7},{5,6},{6,5},{7,4},{8,11},{9,10},{10,... | collective-permute-start | bytes 1622024 | tf_op jit(solution)/shard_map/out_1_3/ppermute | solution.py:81
  62.2 14.5 %collective-permute-start.8 = (bf16[64,4224]{1,0:T(8,128)(2,1)S(1)}, bf16[64,4224]{1,0:T(8,128)(2,1)S(1)}, u32[]{:S(2)}, u32[]{:S(2)}) collective-permute-start(bf16[64,4224]{1,0:T(8,128)(2,1)S(1)} %get-tuple-element.124), channel_id=1, source_target_pairs={{0,1},{1,0},{2,3},{3,2},{4,5},{5,4},{6,7},{7,6},{8,9},{9,8},{10,11... | collective-permute-start | bytes 1622024 | tf_op jit(solution)/shard_map/out_1_1/ppermute | solution.py:81
  63.8 24.5 %collective-permute-start.9 = (bf16[64,4224]{1,0:T(8,128)(2,1)S(1)}, bf16[64,4224]{1,0:T(8,128)(2,1)S(1)}, u32[]{:S(2)}, u32[]{:S(2)}) collective-permute-start(bf16[64,4224]{1,0:T(8,128)(2,1)S(1)} %get-tuple-element.125), channel_id=1, source_target_pairs={{0,2},{1,3},{2,0},{3,1},{4,6},{5,7},{6,4},{7,5},{8,10},{9,11},{10,... | collective-permute-start | bytes 1622024 | tf_op jit(solution)/shard_map/out_1_2/ppermute | solution.py:81
  64.3 3.4 copy-start.1
  88.3 32.1 %slice-start.2 = ((s8[8388608]{0:T(1024)(128)(4,1)}), s8[4194304]{0:T(1024)(128)(4,1)S(1)}, s32[]{:S(2)}) async-start(s8[8388608]{0:T(1024)(128)(4,1)} %bitcast.11), calls=%async_computation.2 | async-start | bytes 8388608
  88.3 32.1 %slice-start.3 = ((s8[8388608]{0:T(1024)(128)(4,1)}), s8[4194304]{0:T(1024)(128)(4,1)S(1)}, s32[]{:S(2)}) async-start(s8[8388608]{0:T(1024)(128)(4,1)} %bitcast.11), calls=%async_computation.3 | async-start | bytes 8388608
  109.7 48.5 %collective-permute-start.16 = (bf16[256,4224]{1,0:T(8,128)(2,1)S(1)}, bf16[256,4224]{1,0:T(8,128)(2,1)S(1)}, u32[]{:S(2)}, u32[]{:S(2)}) collective-permute-start(bf16[256,4224]{1,0:T(8,128)(2,1)S(1)} %collective-permute-done.6.refs_0_.refs_2_), channel_id=1, source_target_pairs={{4,0},{5,1},{6,2},{7,3},{8,12},{9,13},{10,14},{11,15},{20,16},{21,... | collective-permute-start | bytes 6488072 | tf_op jit(solution)/shard_map/rows_outward_far/ppermute | solution.py:81
  114.7 13.3 %collective-permute-start.11 = (bf16[64,4224]{1,0:T(8,128)(2,1)S(1)}, bf16[64,4224]{1,0:T(8,128)(2,1)S(1)}, u32[]{:S(2)}, u32[]{:S(2)}) collective-permute-start(bf16[64,4224]{1,0:T(8,128)(2,1)S(1)} %get-tuple-element.135), channel_id=1, source_target_pairs={{0,1},{1,0},{2,3},{3,2},{4,5},{5,4},{6,7},{7,6},{8,9},{9,8},{10,11... | collective-permute-start | bytes 1622024 | tf_op jit(solution)/shard_map/out_2_1/ppermute | solution.py:81
  114.8 15.1 %collective-permute-start.12 = (bf16[64,4224]{1,0:T(8,128)(2,1)S(1)}, bf16[64,4224]{1,0:T(8,128)(2,1)S(1)}, u32[]{:S(2)}, u32[]{:S(2)}) collective-permute-start(bf16[64,4224]{1,0:T(8,128)(2,1)S(1)} %get-tuple-element.136), channel_id=1, source_target_pairs={{0,2},{1,3},{2,0},{3,1},{4,6},{5,7},{6,4},{7,5},{8,10},{9,11},{10,... | collective-permute-start | bytes 1622024 | tf_op jit(solution)/shard_map/out_2_2/ppermute | solution.py:81
  116.3 24.3 %collective-permute-start.13 = (bf16[64,4224]{1,0:T(8,128)(2,1)S(1)}, bf16[64,4224]{1,0:T(8,128)(2,1)S(1)}, u32[]{:S(2)}, u32[]{:S(2)}) collective-permute-start(bf16[64,4224]{1,0:T(8,128)(2,1)S(1)} %get-tuple-element.137), channel_id=1, source_target_pairs={{0,3},{1,2},{2,1},{3,0},{4,7},{5,6},{6,5},{7,4},{8,11},{9,10},{10,... | collective-permute-start | bytes 1622024 | tf_op jit(solution)/shard_map/out_2_3/ppermute | solution.py:81
  116.6 3.7 %collective-permute-start.14 = (f32[16,256]{1,0:T(8,128)S(1)}, f32[16,256]{1,0:T(8,128)S(1)}, u32[]{:S(2)}, u32[]{:S(2)}) collective-permute-start(f32[16,256]{1,0:T(8,128)S(1)} %get-tuple-element.131.chosen_ref), channel_id=1, source_target_pairs={{0,16},{16,0},{1,17},{17,1},{2,18},{18,2},{3,19},{19,3},{4,20},{20... | collective-permute-start | bytes 49160 | tf_op jit(solution)/shard_map/sums_1/ppermute | solution.py:328
  140.6 14.7 %collective-permute-start.17 = (bf16[64,4096]{1,0:T(8,128)(2,1)S(1)}, bf16[64,4096]{1,0:T(8,128)(2,1)S(1)}, u32[]{:S(2)}, u32[]{:S(2)}) collective-permute-start(bf16[64,4096]{1,0:T(8,128)(2,1)S(1)} %get-tuple-element.150), channel_id=1, source_target_pairs={{0,2},{1,3},{2,0},{3,1},{4,6},{5,7},{6,4},{7,5},{8,10},{9,11},{10,... | collective-permute-start | bytes 1572872 | tf_op jit(solution)/shard_map/back_1_0_2/ppermute | solution.py:81
  142.1 20.2 %collective-permute-start.18 = (bf16[64,4096]{1,0:T(8,128)(2,1)S(1)}, bf16[64,4096]{1,0:T(8,128)(2,1)S(1)}, u32[]{:S(2)}, u32[]{:S(2)}) collective-permute-start(bf16[64,4096]{1,0:T(8,128)(2,1)S(1)} %get-tuple-element.156), channel_id=1, source_target_pairs={{0,1},{1,0},{2,3},{3,2},{4,5},{5,4},{6,7},{7,6},{8,9},{9,8},{10,11... | collective-permute-start | bytes 1572872 | tf_op jit(solution)/shard_map/back_1_0_1/ppermute | solution.py:81
  142.4 23.5 %collective-permute-start.19 = (bf16[64,4096]{1,0:T(8,128)(2,1)S(1)}, bf16[64,4096]{1,0:T(8,128)(2,1)S(1)}, u32[]{:S(2)}, u32[]{:S(2)}) collective-permute-start(bf16[64,4096]{1,0:T(8,128)(2,1)S(1)} %get-tuple-element.157), channel_id=1, source_target_pairs={{0,3},{1,2},{2,1},{3,0},{4,7},{5,6},{6,5},{7,4},{8,11},{9,10},{10,... | collective-permute-start | bytes 1572872 | tf_op jit(solution)/shard_map/back_1_0_3/ppermute | solution.py:81
  160.4 21.2 %collective-permute-start.20 = (bf16[64,4224]{1,0:T(8,128)(2,1)S(1)}, bf16[64,4224]{1,0:T(8,128)(2,1)S(1)}, u32[]{:S(2)}, u32[]{:S(2)}) collective-permute-start(bf16[64,4224]{1,0:T(8,128)(2,1)S(1)} %get-tuple-element.169), channel_id=1, source_target_pairs={{0,1},{1,0},{2,3},{3,2},{4,5},{5,4},{6,7},{7,6},{8,9},{9,8},{10,11... | collective-permute-start | bytes 1622024 | tf_op jit(solution)/shard_map/out_3_1/ppermute | solution.py:81
  160.4 21.1 %collective-permute-start.21 = (bf16[64,4224]{1,0:T(8,128)(2,1)S(1)}, bf16[64,4224]{1,0:T(8,128)(2,1)S(1)}, u32[]{:S(2)}, u32[]{:S(2)}) collective-permute-start(bf16[64,4224]{1,0:T(8,128)(2,1)S(1)} %get-tuple-element.170), channel_id=1, source_target_pairs={{0,2},{1,3},{2,0},{3,1},{4,6},{5,7},{6,4},{7,5},{8,10},{9,11},{10,... | collective-permute-start | bytes 1622024 | tf_op jit(solution)/shard_map/out_3_2/ppermute | solution.py:81
  162.0 27.1 %collective-permute-start.22 = (bf16[64,4224]{1,0:T(8,128)(2,1)S(1)}, bf16[64,4224]{1,0:T(8,128)(2,1)S(1)}, u32[]{:S(2)}, u32[]{:S(2)}) collective-permute-start(bf16[64,4224]{1,0:T(8,128)(2,1)S(1)} %get-tuple-element.171), channel_id=1, source_target_pairs={{0,3},{1,2},{2,1},{3,0},{4,7},{5,6},{6,5},{7,4},{8,11},{9,10},{10,... | collective-permute-start | bytes 1622024 | tf_op jit(solution)/shard_map/out_3_3/ppermute | solution.py:81
  167.5 54.9 %collective-permute-start.31 = (bf16[256,4096]{1,0:T(8,128)(2,1)S(1)}, bf16[256,4096]{1,0:T(8,128)(2,1)S(1)}, u32[]{:S(2)}, u32[]{:S(2)}) collective-permute-start(bf16[256,4096]{1,0:T(8,128)(2,1)S(1)} %combine.6), channel_id=1, source_target_pairs={{0,4},{1,5},{2,6},{3,7},{4,0},{5,1},{6,2},{7,3},{8,12},{9,13},{10,... | collective-permute-start | bytes 6291464 | tf_op jit(solution)/shard_map/sum_ends/ppermute | solution.py:81
  170.0 3.7 %collective-permute-start.15 = (f32[16,256]{1,0:T(8,128)S(1)}, f32[16,256]{1,0:T(8,128)S(1)}, u32[]{:S(2)}, u32[]{:S(2)}) collective-permute-start(f32[16,256]{1,0:T(8,128)S(1)} %get-tuple-element.148.chosen_ref), channel_id=1, source_target_pairs={{0,16},{16,0},{1,17},{17,1},{2,18},{18,2},{3,19},{19,3},{4,20},{20... | collective-permute-start | bytes 49160 | tf_op jit(solution)/shard_map/sums_2/ppermute | solution.py:328
  189.1 22.2 %collective-permute-start.23 = (bf16[64,4096]{1,0:T(8,128)(2,1)S(1)}, bf16[64,4096]{1,0:T(8,128)(2,1)S(1)}, u32[]{:S(2)}, u32[]{:S(2)}) collective-permute-start(bf16[64,4096]{1,0:T(8,128)(2,1)S(1)} %get-tuple-element.176), channel_id=1, source_target_pairs={{0,1},{1,0},{2,3},{3,2},{4,5},{5,4},{6,7},{7,6},{8,9},{9,8},{10,11... | collective-permute-start | bytes 1572872 | tf_op jit(solution)/shard_map/back_2_0_1/ppermute | solution.py:81
  189.5 21.8 %collective-permute-start.24 = (bf16[64,4096]{1,0:T(8,128)(2,1)S(1)}, bf16[64,4096]{1,0:T(8,128)(2,1)S(1)}, u32[]{:S(2)}, u32[]{:S(2)}) collective-permute-start(bf16[64,4096]{1,0:T(8,128)(2,1)S(1)} %get-tuple-element.177), channel_id=1, source_target_pairs={{0,2},{1,3},{2,0},{3,1},{4,6},{5,7},{6,4},{7,5},{8,10},{9,11},{10,... | collective-permute-start | bytes 1572872 | tf_op jit(solution)/shard_map/back_2_0_2/ppermute | solution.py:81
  191.0 22.8 %collective-permute-start.25 = (bf16[64,4096]{1,0:T(8,128)(2,1)S(1)}, bf16[64,4096]{1,0:T(8,128)(2,1)S(1)}, u32[]{:S(2)}, u32[]{:S(2)}) collective-permute-start(bf16[64,4096]{1,0:T(8,128)(2,1)S(1)} %get-tuple-element.178), channel_id=1, source_target_pairs={{0,3},{1,2},{2,1},{3,0},{4,7},{5,6},{6,5},{7,4},{8,11},{9,10},{10,... | collective-permute-start | bytes 1572872 | tf_op jit(solution)/shard_map/back_2_0_3/ppermute | solution.py:81
  199.9 3.8 %collective-permute-start.26 = (f32[16,256]{1,0:T(8,128)S(1)}, f32[16,256]{1,0:T(8,128)S(1)}, u32[]{:S(2)}, u32[]{:S(2)}) collective-permute-start(f32[16,256]{1,0:T(8,128)S(1)} %get-tuple-element.180.chosen_ref), channel_id=1, source_target_pairs={{0,16},{16,0},{1,17},{17,1},{2,18},{18,2},{3,19},{19,3},{4,20},{20... | collective-permute-start | bytes 49160 | tf_op jit(solution)/shard_map/sums_3/ppermute | solution.py:328
  214.6 31.0 %collective-permute-start.27 = (bf16[256,2048]{1,0:T(8,128)(2,1)S(1)}, bf16[256,2048]{1,0:T(8,128)(2,1)S(1)}, u32[]{:S(2)}, u32[]{:S(2)}) collective-permute-start(bf16[256,2048]{1,0:T(8,128)(2,1)S(1)} %combine.7), channel_id=1, source_target_pairs={{0,4},{1,5},{2,6},{3,7},{12,8},{13,9},{14,10},{15,11},{16,20},{17,... | collective-permute-start | bytes 3145736 | tf_op jit(solution)/shard_map/sum_inward_two_0/ppermute | solution.py:81
  218.9 5.0 %collective-permute-start.28 = (bf16[64,4096]{1,0:T(8,128)(2,1)S(1)}, bf16[64,4096]{1,0:T(8,128)(2,1)S(1)}, u32[]{:S(2)}, u32[]{:S(2)}) collective-permute-start(bf16[64,4096]{1,0:T(8,128)(2,1)S(1)} %get-tuple-element.183), channel_id=1, source_target_pairs={{0,1},{1,0},{2,3},{3,2},{4,5},{5,4},{6,7},{7,6},{8,9},{9,8},{10,11... | collective-permute-start | bytes 1572872 | tf_op jit(solution)/shard_map/back_3_0_1/ppermute | solution.py:81
  219.8 14.8 %collective-permute-start.29 = (bf16[64,4096]{1,0:T(8,128)(2,1)S(1)}, bf16[64,4096]{1,0:T(8,128)(2,1)S(1)}, u32[]{:S(2)}, u32[]{:S(2)}) collective-permute-start(bf16[64,4096]{1,0:T(8,128)(2,1)S(1)} %get-tuple-element.184), channel_id=1, source_target_pairs={{0,2},{1,3},{2,0},{3,1},{4,6},{5,7},{6,4},{7,5},{8,10},{9,11},{10,... | collective-permute-start | bytes 1572872 | tf_op jit(solution)/shard_map/back_3_0_2/ppermute | solution.py:81
  221.3 22.8 %collective-permute-start.30 = (bf16[64,4096]{1,0:T(8,128)(2,1)S(1)}, bf16[64,4096]{1,0:T(8,128)(2,1)S(1)}, u32[]{:S(2)}, u32[]{:S(2)}) collective-permute-start(bf16[64,4096]{1,0:T(8,128)(2,1)S(1)} %get-tuple-element.185), channel_id=1, source_target_pairs={{0,3},{1,2},{2,1},{3,0},{4,7},{5,6},{6,5},{7,4},{8,11},{9,10},{10,... | collective-permute-start | bytes 1572872 | tf_op jit(solution)/shard_map/back_3_0_3/ppermute | solution.py:81
  222.3 42.4 %collective-permute-start.33 = (bf16[256,2048]{1,0:T(8,128)(2,1)S(1)}, bf16[256,2048]{1,0:T(8,128)(2,1)S(1)}, u32[]{:S(2)}, u32[]{:S(2)}) collective-permute-start(bf16[256,2048]{1,0:T(8,128)(2,1)S(1)} %combine.8), channel_id=1, source_target_pairs={{0,4},{1,5},{2,6},{3,7},{12,8},{13,9},{14,10},{15,11},{16,20},{17,... | collective-permute-start | bytes 3145736 | tf_op jit(solution)/shard_map/sum_inward_two_1/ppermute | solution.py:81
  246.0 19.8 %collective-permute-start.32 = (bf16[256,2048]{1,0:T(8,128)(2,1)S(1)}, bf16[256,2048]{1,0:T(8,128)(2,1)S(1)}, u32[]{:S(2)}, u32[]{:S(2)}) collective-permute-start(bf16[256,2048]{1,0:T(8,128)(2,1)S(1)} %add_convert_fusion.5), channel_id=1, source_target_pairs={{4,8},{5,9},{6,10},{7,11},{8,4},{9,5},{10,6},{11,7},{20,24},{21,25... | collective-permute-start | bytes 3145736 | tf_op jit(solution)/shard_map/sum_middle_two_0/ppermute | solution.py:81
  246.8 40.4 %collective-permute-start.37 = (bf16[256,2048]{1,0:T(8,128)(2,1)S(1)}, bf16[256,2048]{1,0:T(8,128)(2,1)S(1)}, u32[]{:S(2)}, u32[]{:S(2)}) collective-permute-start(bf16[256,2048]{1,0:T(8,128)(2,1)S(1)} %combine.9), channel_id=1, source_target_pairs={{0,4},{1,5},{2,6},{3,7},{12,8},{13,9},{14,10},{15,11},{16,20},{17,... | collective-permute-start | bytes 3145736 | tf_op jit(solution)/shard_map/sum_inward_far_0/ppermute | solution.py:81
  250.1 59.5 %collective-permute-start.39 = (bf16[256,2048]{1,0:T(8,128)(2,1)S(1)}, bf16[256,2048]{1,0:T(8,128)(2,1)S(1)}, u32[]{:S(2)}, u32[]{:S(2)}) collective-permute-start(bf16[256,2048]{1,0:T(8,128)(2,1)S(1)} %combine.10), channel_id=1, source_target_pairs={{0,4},{1,5},{2,6},{3,7},{12,8},{13,9},{14,10},{15,11},{16,20},{17,... | collective-permute-start | bytes 3145736 | tf_op jit(solution)/shard_map/sum_inward_far_1/ppermute | solution.py:81
  265.1 25.3 %collective-permute-start.36 = (bf16[256,2048]{1,0:T(8,128)(2,1)S(1)}, bf16[256,2048]{1,0:T(8,128)(2,1)S(1)}, u32[]{:S(2)}, u32[]{:S(2)}) collective-permute-start(bf16[256,2048]{1,0:T(8,128)(2,1)S(1)} %add_convert_fusion.4), channel_id=1, source_target_pairs={{4,8},{5,9},{6,10},{7,11},{8,4},{9,5},{10,6},{11,7},{20,24},{21,25... | collective-permute-start | bytes 3145736 | tf_op jit(solution)/shard_map/sum_middle_two_1/ppermute | solution.py:81
  287.6 30.3 %collective-permute-start.40 = (bf16[256,2048]{1,0:T(8,128)(2,1)S(1)}, bf16[256,2048]{1,0:T(8,128)(2,1)S(1)}, u32[]{:S(2)}, u32[]{:S(2)}) collective-permute-start(bf16[256,2048]{1,0:T(8,128)(2,1)S(1)} %add_convert_fusion.3), channel_id=1, source_target_pairs={{4,12},{5,13},{6,14},{7,15},{8,0},{9,1},{10,2},{11,3},{20,28},{21,... | collective-permute-start | bytes 3145736 | tf_op jit(solution)/shard_map/sum_skip_far_0/ppermute | solution.py:81
  288.9 14.2 %collective-permute-start.35 = (bf16[64,4096]{1,0:T(8,128)(2,1)S(1)}, bf16[64,4096]{1,0:T(8,128)(2,1)S(1)}, u32[]{:S(2)}, u32[]{:S(2)}) collective-permute-start(bf16[64,4096]{1,0:T(8,128)(2,1)S(1)} %get-tuple-element.200), channel_id=1, source_target_pairs={{0,2},{1,3},{2,0},{3,1},{4,6},{5,7},{6,4},{7,5},{8,10},{9,11},{10,... | collective-permute-start | bytes 1572872 | tf_op jit(solution)/shard_map/back_0_0_2/ppermute | solution.py:81
  318.3 28.0 %collective-permute-start.41 = (bf16[256,2048]{1,0:T(8,128)(2,1)S(1)}, bf16[256,2048]{1,0:T(8,128)(2,1)S(1)}, u32[]{:S(2)}, u32[]{:S(2)}) collective-permute-start(bf16[256,2048]{1,0:T(8,128)(2,1)S(1)} %add_convert_fusion.1), channel_id=1, source_target_pairs={{4,12},{5,13},{6,14},{7,15},{8,0},{9,1},{10,2},{11,3},{20,28},{21,... | collective-permute-start | bytes 3145736 | tf_op jit(solution)/shard_map/sum_skip_far_1/ppermute | solution.py:81
  319.6 2.0 collective-permute-start.34
  319.8 13.8 %collective-permute-start.38 = (bf16[64,4096]{1,0:T(8,128)(2,1)S(1)}, bf16[64,4096]{1,0:T(8,128)(2,1)S(1)}, u32[]{:S(2)}, u32[]{:S(2)}) collective-permute-start(bf16[64,4096]{1,0:T(8,128)(2,1)S(1)} %get-tuple-element.204), channel_id=1, source_target_pairs={{0,3},{1,2},{2,1},{3,0},{4,7},{5,6},{6,5},{7,4},{8,11},{9,10},{10,... | collective-permute-start | bytes 1572872 | tf_op jit(solution)/shard_map/back_0_0_3/ppermute | solution.py:81

commit v3 on v2

--- a/solution.py
+++ b/solution.py
@@ -1,4 +1,5 @@
 import functools
+import math
 
 import jax
 import jax.numpy as jnp
@@ -8,11 +9,12 @@
 from jax.sharding import PartitionSpec as P
 
 BACK_CHUNKS = (1, 1, 1, 1)
-SUM_CHUNKS = 2
+TWO_SHARES = (1, 1)
+FAR_SHARES = (1, 1)
 INNER = 4
 OUTER = 4
 EXTRA = 128
-BLOCK = 512
+BLOCK = 1024
 VMEM = 24 * 1024 * 1024
 F32 = jnp.float32
 BF16 = jnp.bfloat16
@@ -174,18 +176,14 @@
         both = both.astype(jnp.int32)
         picks = jnp.where(extra[:, 0:1] == me_ref[0, 0], both[:, :picked], both[:, picked:])
         slots, latents = total.shape
-        lane = lax.broadcasted_iota(jnp.int32, (slots, EXTRA), 1)
-        ids = lax.broadcasted_iota(jnp.int32, (slots, latents), 1)
+        picks = jnp.concatenate([picks, jnp.zeros((slots, EXTRA - picked), jnp.int32)], axis=1)
+        group, lane = picks // EXTRA, picks % EXTRA
         values = jnp.zeros((slots, EXTRA), F32)
-        kept = jnp.zeros((slots, EXTRA), jnp.int32)
-        pre = total[...]
-        for p in range(picked):
-            pick = picks[:, p:p + 1]
-            value = jnp.sum(jnp.where(ids == pick, pre, 0.0), axis=1, keepdims=True)
-            values = jnp.where(lane == p, value, values)
-            kept = jnp.where(lane == p, pick, kept)
+        for g in range(latents // EXTRA):
+            here = total[:, g * EXTRA:(g + 1) * EXTRA]
+            values = jnp.where(group == g, jnp.take_along_axis(here, lane, axis=1), values)
         chosen_ref[...] = values.T[:picked]
-        picks_ref[...] = kept
+        picks_ref[...] = picks.astype(F32).T[:picked].astype(jnp.int32)
 
 
 def encode(pieces, weight, bias, me, cap, picked):
@@ -209,17 +207,17 @@
         ],
         [
             pl.BlockSpec((picked, slots), lambda k: (0, 0)),
-            pl.BlockSpec((slots, EXTRA), lambda k: (0, 0)),
+            pl.BlockSpec((picked, slots), lambda k: (0, 0)),
         ],
         [
             jax.ShapeDtypeStruct((picked, slots), F32),
-            jax.ShapeDtypeStruct((slots, EXTRA), jnp.int32),
+            jax.ShapeDtypeStruct((picked, slots), jnp.int32),
         ],
         [pltpu.VMEM((slots, latents), F32)],
     )(*pieces, *pieces, weight, bias, me)
 
 
-def decode_kernel(cap, chosen_ref, added_ref, picks_ref, dec_ref, *refs):
+def decode_kernel(chosen_ref, added_ref, picks_ref, dec_ref, *refs):
     active = refs[-1]
 
     @pl.when(pl.program_id(0) == 0)
@@ -227,57 +225,84 @@
         picked, slots = chosen_ref.shape
         latents = active.shape[1]
         value = jnp.maximum(chosen_ref[...] + added_ref[...], 0.0)
-        value = jnp.concatenate([value, jnp.zeros((EXTRA - picked, slots), F32)], axis=0).T
-        ids = lax.broadcasted_iota(jnp.int32, (slots, latents), 1)
-        dense = jnp.zeros((slots, latents), F32)
+        ids = lax.broadcasted_iota(jnp.int32, (latents, slots), 0)
+        dense = jnp.zeros((latents, slots), F32)
         for p in range(picked):
-            dense = jnp.where(ids == picks_ref[:, p:p + 1], value[:, p:p + 1], dense)
-        active[...] = dense.astype(BF16)
+            dense = jnp.where(ids == picks_ref[p:p + 1, :], value[p:p + 1, :], dense)
+        active[...] = dense.T.astype(BF16)
 
     part = jnp.dot(active[...], dec_ref[...], preferred_element_type=F32).astype(BF16)
-    for j, ref in enumerate(refs[:-1]):
-        ref[...] = part[j * cap:(j + 1) * cap]
-
-
-def decode(chosen, added, picks, weight, cap, first, width):
+    first = 0
+    for ref in refs[:-1]:
+        ref[...] = part[first:first + ref.shape[0]]
+        first += ref.shape[0]
+
+
+def decode(chosen, added, picks, weight, sizes):
     picked, slots = chosen.shape
-    latents = weight.shape[0]
-    skip = first // BLOCK
+    latents, width = weight.shape
     return call(
-        functools.partial(decode_kernel, cap),
+        decode_kernel,
         "decode",
         (width // BLOCK,),
         [
             pl.BlockSpec((picked, slots), lambda j: (0, 0)),
             pl.BlockSpec((picked, slots), lambda j: (0, 0)),
-            pl.BlockSpec((slots, EXTRA), lambda j: (0, 0)),
-            pl.BlockSpec((latents, BLOCK), lambda j: (0, j + skip)),
+            pl.BlockSpec((picked, slots), lambda j: (0, 0)),
+            pl.BlockSpec((latents, BLOCK), lambda j: (0, j)),
         ],
-        [pl.BlockSpec((cap, BLOCK), lambda j: (0, j))] * INNER,
-        [jax.ShapeDtypeStruct((cap, width), BF16)] * INNER,
+        [pl.BlockSpec((size, BLOCK), lambda j: (0, j)) for size in sizes],
+        [jax.ShapeDtypeStruct((size, width), BF16) for size in sizes],
         [pltpu.VMEM((slots, latents), BF16)],
     )(chosen, added, picks, weight)
 
 
 def combine_kernel(spread_ref, *refs):
     parts = jnp.concatenate([ref[...] for ref in refs[:-1]], axis=0)
-    refs[-1][...] = jnp.dot(spread_ref[...], parts, preferred_element_type=F32).astype(BF16)
-
-
-def combine(spread, pieces, first, width):
-    cap = pieces[0].shape[0]
+    total = jnp.dot(spread_ref[...], parts, preferred_element_type=F32)
+    refs[-1][...] = total.astype(refs[-1].dtype)
+
+
+def combine(spread, blocks, cap, first, width, dtype=BF16):
     rows, slots = spread.shape
-    step = min(width, 1024)
+    step = math.gcd(math.gcd(first, width), 1024)
     skip = first // step
     return call(
         combine_kernel,
         "combine",
         (width // step,),
         [pl.BlockSpec((rows, slots), lambda j: (0, 0))]
-        + [pl.BlockSpec((cap, step), lambda j: (0, j + skip))] * INNER,
+        + [pl.BlockSpec((cap, step), lambda j, at=at: (at, j + skip)) for _, at in blocks],
         pl.BlockSpec((rows, step), lambda j: (0, j)),
-        jax.ShapeDtypeStruct((rows, width), BF16),
-    )(spread, *pieces)
+        jax.ShapeDtypeStruct((rows, width), dtype),
+    )(spread, *(array for array, _ in blocks))
+
+
+def spread_kernel(slots_ref, meta_ref, spread_ref):
+    rows = spread_ref.shape[0]
+    extra = meta_ref[...].astype(F32)
+    hit = (extra[:, 0:1] == slots_ref[0:1, :]) | (extra[:, 1:2] == slots_ref[0:1, :])
+    earlier = lax.broadcasted_iota(jnp.int32, (rows, rows), 1) < lax.broadcasted_iota(
+        jnp.int32, (rows, rows), 0
+    )
+    rank = jnp.dot(
+        jnp.where(earlier, 1.0, 0.0).astype(BF16),
+        jnp.where(hit, 1.0, 0.0).astype(BF16),
+        preferred_element_type=F32,
+    )
+    spread = jnp.where(hit & (rank == slots_ref[1:2, :]), 1.0, 0.0)
+    spread_ref[...] = spread.astype(BF16)
+
+
+def spread_of(slots, meta):
+    return call(
+        spread_kernel,
+        "spread",
+        (),
+        [pl.BlockSpec(memory_space=pltpu.VMEM)] * 2,
+        pl.BlockSpec(memory_space=pltpu.VMEM),
+        jax.ShapeDtypeStruct((meta.shape[0], slots.shape[1]), BF16),
+    )(slots, meta)
 
 
 def line_on_device(tokens, dec_bias, routes, latent_picks, enc_weight, dec_weight, enc_bias):
@@ -295,8 +320,12 @@
     own = jnp.concatenate([tokens, meta], axis=1)
     offset = jnp.pad(dec_bias, (0, EXTRA))[None, :]
     slot = jnp.arange(INNER * cap, dtype=jnp.int32)
-    slots = jnp.stack([plane * INNER + ((slot // cap) ^ inner), slot % cap]).astype(F32)
-    slots = jnp.pad(slots, ((0, 6), (0, 0)))
+
+    def slots_in(which):
+        named = jnp.stack([which * INNER + ((slot // cap) ^ inner), slot % cap]).astype(F32)
+        return jnp.pad(named, ((0, 6), (0, 0)))
+
+    slots = slots_in(plane)
     bias = jnp.where(lax.axis_index("dp") == 0, enc_bias, 0.0)
     me_value = me.astype(F32).reshape(1, 1)
     enc, dec = enc_weight[0], dec_weight[0]
@@ -328,109 +357,114 @@
             added = lax.ppermute(chosen, "dp", [(0, 1), (1, 0)])
         return picks, chosen, added
 
-    def decoded(t, picks, chosen, added):
-        each = width // BACK_CHUNKS[t]
-        return [
-            decode(chosen, added, picks, dec, cap, i * each, each) for i in range(BACK_CHUNKS[t])
-        ]
-
-    def leave(t, parts, *earlier):
-        if earlier:
-            parts = [all_after(pieces, *earlier) for pieces in parts]
-        return [exchange(pieces, f"back_{t}_{i}") for i, pieces in enumerate(parts)]
-
-    def combined(spread, parts, count, *earlier):
-        sums = []
-        for pieces in parts:
-            if earlier:
-                pieces = all_after(pieces, *earlier)
-            wide, each = pieces[0].shape[1], width // count
-            for first in range(0, wide, each):
-                sums.append(combine(spread, pieces, first, min(each, wide)))
+    def decoded(picks, chosen, added, sizes=(cap,) * INNER):
+        return decode(chosen, added, picks, dec, sizes)
+
+    def leave(t, pieces):
+        return exchange(pieces, f"back_{t}")
+
+    def combined(spread, pieces, shares):
+        sums, first = [], 0
+        for share in shares:
+            size = width * share // sum(shares)
+            sums.append(combine(spread, [(piece, 0) for piece in pieces], cap, first, size))
+            first += size
         return sums
 
     def plus(a, b):
         return (a.astype(F32) + b.astype(F32)).astype(BF16)
 
-    spreads, back = {}, {}
+    spreads, parts = {}, {}
     spreads[0], arrived = send_out(0)
-    waiting, returned = {}, {}
-    for t in range(OUTER):
-        if t > 0:
-            arrived = all_after(arrived, *waiting[t - 1][0])
-        if t > 1:
-            returned[t - 1] = leave(t - 1, waiting[t - 1], *arrived[1:])
-        picks, chosen, added = encoded(t, arrived)
-        earlier = (chosen,)
-        if t == 2:
-            pieces = returned[1][0]
-            pieces[2] = after(pieces[2], chosen)
-            earlier = earlier + (pieces[2],)
-        if t == 0:
-            by_one, by_two = all_after((by_one, by_two), *earlier)
-            with jax.named_scope("rows_outward_two"):
-                to_ends_two = move(by_two, OUTWARD)
-            with jax.named_scope("rows_middle_far"):
-                by_three = move(by_one, MIDDLE)
-            groups[1] = (by_one,)
-        if t == 1:
-            by_three, to_ends_two = all_after((by_three, to_ends_two), *earlier)
-            with jax.named_scope("rows_outward_far"):
-                to_ends_three = move(by_three, OUTWARD)
-            groups[2] = (by_two, to_ends_two)
-        if t == 2:
-            groups[3] = (by_three, after(to_ends_three, *earlier))
-        if t < OUTER - 1:
-            spreads[t + 1], arrived = send_out(t + 1)
-            added = after(added, spreads[t + 1])
-        if t == 2:
-            back[1] = combined(spreads[1], returned[1], 1, spreads[3])
-            with jax.named_scope("sum_ends"):
-                from_end = move(back[1][0], ENDS)
-            added = after(added, *back[1])
-        waiting[t] = decoded(t, picks, chosen, added)
-    last = leave(3, waiting[3])
-    back[2] = combined(spreads[2], returned[2], SUM_CHUNKS, *waiting[3][0])
-    from_end = after(from_end, *back[2])
-    back[3] = combined(spreads[3], last, SUM_CHUNKS, from_end)
-
-    count = SUM_CHUNKS
-    piece = width // count
-    cols = [slice(i * piece, (i + 1) * piece) for i in range(count)]
-    from_two, from_far = [], []
-    for i in range(count):
+    spread_next = spread_of(slots_in(plane ^ 1), meta)
+
+    picks, chosen, added = encoded(0, arrived)
+    added = after(added, chosen)
+    by_one, by_two = all_after((by_one, by_two), added)
+    with jax.named_scope("rows_outward_two"):
+        to_ends_two = move(by_two, OUTWARD)
+    with jax.named_scope("rows_middle_far"):
+        by_three = move(by_one, MIDDLE)
+    groups[1] = (by_one,)
+    spreads[1], arrived = send_out(1)
+    parts[0] = decoded(picks, chosen, after(added, spreads[1]))
+
+    picks, chosen, added = encoded(1, all_after(arrived, *parts[0]))
+    (parts1,) = decoded(picks, chosen, added, (INNER * cap,))
+    with jax.named_scope("parts_inward"):
+        inward = move(parts1, INWARD)
+    to_ends_two = after(to_ends_two, parts1)
+    by_three = after(by_three, to_ends_two)
+    with jax.named_scope("rows_outward_far"):
+        to_ends_three = move(by_three, OUTWARD)
+    groups[2] = (by_two, to_ends_two)
+    spreads[2], arrived = send_out(2)
+
+    picks, chosen, added = encoded(2, arrived)
+    parts[2] = decoded(picks, chosen, added)
+    returned2 = leave(2, parts[2])
+    to_ends_three = after(to_ends_three, *parts[2])
+    returned2[1] = after(returned2[1], to_ends_three)
+    with jax.named_scope("parts_outward"):
+        outward = move(after(parts1, to_ends_three), OUTWARD)
+    groups[3] = (by_three, after(to_ends_three, returned2[1]))
+    spreads[3], arrived = send_out(3)
+    arrived[1] = after(arrived[1], spreads[3])
+    arrived[2] = after(arrived[2], arrived[1])
+    inward = after(inward, arrived[2])
+    arrived[3] = after(arrived[3], inward)
+
+    picks, chosen, added = encoded(3, arrived)
+    parts[3] = decoded(picks, chosen, added)
+    returned3 = leave(3, parts[3])
+    back2 = combined(spreads[2], all_after(returned2, *parts[3]), TWO_SHARES)
+    from_two = []
+    for i, value in enumerate(back2):
         with jax.named_scope(f"sum_inward_two_{i}"):
-            from_two.append(move(back[2][i], INWARD))
-    for i in range(count):
+            from_two.append(move(value, INWARD))
+    twos, ones = [], []
+
+    def two_on(i, *earlier):
+        from_two[i] = after(from_two[i], *earlier)
+        with jax.named_scope(f"sum_middle_two_{i}"):
+            twos.append(move(plus(back2[i], from_two[i]), MIDDLE))
+
+    returned3[2] = after(returned3[2], *back2)
+    two_on(0, returned3[2])
+    returned3 = all_after(returned3, from_two[0])
+    back3 = combined(spreads[3], returned3, FAR_SHARES)
+    two_on(1, *back3)
+    twos[0] = after(twos[0], from_two[1])
+    outward = after(outward, from_two[1])
+    from_far = []
+    for i, value in enumerate(back3):
         with jax.named_scope(f"sum_inward_far_{i}"):
-            from_far.append(move(back[3][i], INWARD))
-    twos, ones, results = [], [], []
-    seen = tuple(back[3])
-    for i in range(count):
-        got = after(from_two[i], *seen)
-        with jax.named_scope(f"sum_middle_two_{i}"):
-            twos.append(move(plus(back[2][i], got), MIDDLE))
-        seen = (got,)
-    for i in range(count):
-        twos[i] = after(twos[i], *seen)
-        if i == 0:
-            returned[0] = leave(0, waiting[0], twos[0])
-            got = after(from_far[i], twos[i])
-        else:
-            pieces = returned[0][0]
-            pieces[2] = after(pieces[2], twos[i])
-            got = after(from_far[i], pieces[2], ones[i - 1])
+            from_far.append(move(value, INWARD))
+
+    near = inward + outward
+    pieces = []
+    for j in range(1, INNER):
+        pieces.append(jnp.concatenate([parts[0][j], near[j * cap:(j + 1) * cap]], axis=0))
+    pieces = exchange([None, *all_after(pieces, *returned3)], "back_near")
+
+    def skip_on(i, *earlier):
+        from_far[i] = after(from_far[i], *earlier)
         with jax.named_scope(f"sum_skip_far_{i}"):
-            ones.append(move(plus(back[3][i], got), SKIP))
-        seen = (got,)
-    back[0] = combined(spreads[0], returned[0], 1, *seen)
-    ones[-1] = after(ones[-1], *back[0])
-    for i in range(count):
-        total = dec_bias[cols[i]]
-        for value in (back[0][0][:, cols[i]], from_end[:, cols[i]], twos[i], ones[i]):
-            total = total + value.astype(F32)
-        results.append(total.astype(BF16))
-    return jnp.concatenate(results, axis=1)
+            ones.append(move(plus(back3[i], from_far[i]), SKIP))
+
+    skip_on(0, pieces[2], twos[0])
+    twos[1] = after(twos[1], from_far[0])
+    pieces[3] = after(pieces[3], twos[1])
+    skip_on(1, pieces[3], ones[0])
+    pieces[1] = after(pieces[1], from_far[1])
+    blocks = [(parts[0][0], 0)] + [(piece, 0) for piece in pieces[1:]]
+    blocks += [(near, 0)] + [(piece, 1) for piece in pieces[1:]]
+    near = combine(
+        jnp.concatenate([spreads[0], spread_next], axis=1), blocks, cap, 0, width, F32
+    )
+    ones = all_after(ones, near)
+    near = near + dec_bias + jnp.concatenate(twos, axis=1).astype(F32)
+    return (near + jnp.concatenate(ones, axis=1).astype(F32)).astype(BF16)
 
 
 def solution(mesh):

time: 355 us -> 339 us (0.955); the launches traced: 350 us -> 338 us
  Pallas kernels: 86.1 us -> 59.2 us
  waiting for transfers between devices: 197 us -> 210 us
    pallas_call x4, Pallas kernels: 36.8 us -> 20.7 us  [encode(): call(kernel, 'encode', (width // BLOCK,), [pl.BlockSpec((cap, BLOCK), lam...]
    ppermute x38 -> x36, waiting for transfers between devices: 190 us -> 201 us  [move(): return lax.ppermute(value, 'blocks', pairs)]
    pallas_call x4 -> x5, Pallas kernels: 30.8 us -> 20.5 us  [the longest x4 20.2 us: decode(): call(decode_kernel, 'decode', (width // BLOCK,), [pl.BlockSpec((picked, s...]
    ppermute x38 -> x36, starting transfers between devices: 44.1 us -> 47.4 us  [move(): return lax.ppermute(value, 'blocks', pairs)]
  transfers between devices with their start and end apart: 42 -> 40, of which waited for: 27 -> 26; matrix products, arithmetic and copies ran while one was open for 0% -> 1% of each run, Pallas kernels for 25% -> 18%
where the time goes in v3:
time: 339 us; the launch traced here: 338 us
  waiting for transfers between devices  210 us (62%)
  Pallas kernels  59.2 us (17%)
  starting transfers between devices  53.9 us (16%)
  local copies, waits for them, and re-layouts  7.97 us (2%)
  other arithmetic  7.13 us (2%)
    ppermute x36, waiting for transfers between devices, move(): return lax.ppermute(value, 'blocks', pairs)  201 us
    ppermute x36, starting transfers between devices, move(): return lax.ppermute(value, 'blocks', pairs)  47.4 us
    pallas_call x4, Pallas kernels, encode(): call(kernel, 'encode', (width // BLOCK,), [pl.BlockSpec((cap, BLOCK), lam...  20.7 us
    pallas_call x4, Pallas kernels, decode(): call(decode_kernel, 'decode', (width // BLOCK,), [pl.BlockSpec((picked, s...  20.2 us
    pallas_call x4, Pallas kernels, dispatch(): call(kernel, 'dispatch', (3,), [pl.BlockSpec((8, INNER * cap), lambda j:...  12.5 us
    ppermute x4, waiting for transfers between devices, encoded(): added = lax.ppermute(chosen, 'dp', [(0, 1), (1, 0)])  8.83 us
    unnamed x16, local copies, waits for them, and re-layouts  6.79 us
  transfers between devices with their start and end apart: 40, of which 26 were waited for; matrix products, arithmetic and copies ran while one was open for 1% of the time, Pallas kernels for 18%

profile of v3, /device:TPU:0, one launch (start us, length us, event | category | flops | bytes accessed | tf_op | source)
XLA Modules:
  0.0 338.3 jit_solution(10174027741733507648)
XLA Ops:
  2.0 1.8 pad_maximum_fusion.refs_0_.refs_1_
  3.7 3.1 collective-permute-start.4
  6.8 2.0 collective-permute-start.5
  8.9 2.9 dispatch.4
  11.9 1.5 collective-permute-start.1
  14.0 13.2 %collective-permute-done.1.refs_2_.refs_6_ = bf16[64,4224]{1,0:T(8,128)(2,1)} collective-permute-done((bf16[64,4224]{1,0:T(8,128)(2,1)}, bf16[64,4224]{1,0:T(8,128)(2,1)}, u32[]{:S(2)}, u32[]{:S(2)}) %collective-permute-start.1) | collective-permute-done | bytes 540704 | tf_op jit(solution)/shard_map/out_0_2/ppermute | solution.py:83
  27.2 10.8 %collective-permute-done.2.refs_3_.refs_7_ = bf16[64,4224]{1,0:T(8,128)(2,1)} collective-permute-done((bf16[64,4224]{1,0:T(8,128)(2,1)}, bf16[64,4224]{1,0:T(8,128)(2,1)}, u32[]{:S(2)}, u32[]{:S(2)}) %collective-permute-start.2) | collective-permute-done | bytes 540704 | tf_op jit(solution)/shard_map/out_0_3/ppermute | solution.py:83
  38.1 3.4 copy-done
  41.4 5.8 %encode.4 = (f32[16,256]{1,0:T(8,128)S(1)}, s32[16,256]{1,0:T(8,128)S(1)}) custom-call(bf16[64,4224]{1,0:T(8,128)(2,1)S(1)} %get-tuple-element.85.refs_0_.refs_4_, bf16[64,4224]{1,0:T(8,128)(2,1)S(1)} %collective-permute-done.refs_1_.refs_5_, bf16[64,4224]{1,0:T(8,128)(2,1)} %collective-permute-done.1.refs_2_.refs_6_, ...), custom_call_target="tpu_custom_call" | custom-call | tf_op jit(solution)/shard_map/encode/pallas_call | solution.py:197
  47.3 1.6 collective-permute-start.3
  48.9 2.2 collective-permute-done.3.added_ref
  51.1 2.9 collective-permute-done.4.refs_0_.refs_1_
  54.0 1.3 collective-permute-start.12
  56.1 3.9 %dispatch.5 = (bf16[256,256]{1,0:T(8,128)(2,1)}, bf16[64,4224]{1,0:T(8,128)(2,1)S(1)}, bf16[64,4224]{1,0:T(8,128)(2,1)S(1)}, bf16[64,4224]{1,0:T(8,128)(2,1)S(1)}, bf16[64,4224]{1,0:T(8,128)(2,1)S(1)}) custom-call(f32[8,256]{1,0:T(8,128)S(1)} %pad.15.slots_ref, bf16[256,4224]{1,0:T(8,128)(2,1)} %collective-permute-done.4.refs_0_.refs_1_, ...), custom_call_target="tpu_custom_call" | custom-call | tf_op jit(solution)/shard_map/dispatch/pallas_call | solution.py:144
  59.9 1.7 collective-permute-start.7
  61.8 3.4 copy-done.1
  65.2 5.1 %decode.4 = (bf16[64,4096]{1,0:T(8,128)(2,1)S(1)}, bf16[64,4096]{1,0:T(8,128)(2,1)S(1)}, bf16[64,4096]{1,0:T(8,128)(2,1)S(1)}, bf16[64,4096]{1,0:T(8,128)(2,1)S(1)}) custom-call(f32[16,256]{1,0:T(8,128)S(1)} %get-tuple-element.89.chosen_ref, f32[16,256]{1,0:T(8,128)S(1)} %collective-permute-done.3.added_ref, s32[16,256]{1,0:T(8,128)S(1)} %get-tuple-element.91.picks_ref, ...), custom_call_target="tpu_custom_call" | custom-call | tf_op jit(solution)/shard_map/decode/pallas_call | solution.py:244
  70.3 4.7 %collective-permute-done.7.refs_2_.refs_6_ = bf16[64,4224]{1,0:T(8,128)(2,1)S(1)} collective-permute-done((bf16[64,4224]{1,0:T(8,128)(2,1)S(1)}, bf16[64,4224]{1,0:T(8,128)(2,1)S(1)}, u32[]{:S(2)}, u32[]{:S(2)}) %collective-permute-start.7) | collective-permute-done | bytes 540704 | tf_op jit(solution)/shard_map/out_1_2/ppermute | solution.py:83
  75.0 10.8 %collective-permute-done.8.refs_3_.refs_7_ = bf16[64,4224]{1,0:T(8,128)(2,1)S(1)} collective-permute-done((bf16[64,4224]{1,0:T(8,128)(2,1)S(1)}, bf16[64,4224]{1,0:T(8,128)(2,1)S(1)}, u32[]{:S(2)}, u32[]{:S(2)}) %collective-permute-start.8) | collective-permute-done | bytes 540704 | tf_op jit(solution)/shard_map/out_1_3/ppermute | solution.py:83
  85.8 5.0 %encode.5 = (f32[16,256]{1,0:T(8,128)S(1)}, s32[16,256]{1,0:T(8,128)S(1)}) custom-call(bf16[64,4224]{1,0:T(8,128)(2,1)S(1)} %get-tuple-element.101.refs_0_.refs_4_, bf16[64,4224]{1,0:T(8,128)(2,1)S(1)} %collective-permute-done.6.refs_1_.refs_5_, bf16[64,4224]{1,0:T(8,128)(2,1)S(1)} %collective-permute-done.7.refs_2_.refs_6_, ...), custom_call_target="tpu_custom_call" | custom-call | tf_op jit(solution)/shard_map/encode/pallas_call | solution.py:197
  90.8 1.7 collective-permute-start.9
  92.6 2.1 collective-permute-done.9.added_ref
  94.6 5.0 %decode.5 = bf16[256,4096]{1,0:T(8,128)(2,1)S(1)} custom-call(f32[16,256]{1,0:T(8,128)S(1)} %get-tuple-element.105.chosen_ref, f32[16,256]{1,0:T(8,128)S(1)} %collective-permute-done.9.added_ref, s32[16,256]{1,0:T(8,128)S(1)} %get-tuple-element.106.picks_ref, bf16[1024,4096]{1,0:T(8,128)(2,1)S(1)} %bitcast.13), custom_call_target="tpu_custom_call" | custom-call | tf_op jit(solution)/shard_map/decode/pallas_call | solution.py:244
  99.6 6.7 %collective-permute-done.12.refs_1_.refs_3_ = bf16[256,4224]{1,0:T(8,128)(2,1)S(1)} collective-permute-done((bf16[256,4224]{1,0:T(8,128)(2,1)}, bf16[256,4224]{1,0:T(8,128)(2,1)S(1)}, u32[]{:S(2)}, u32[]{:S(2)}) %collective-permute-start.12) | collective-permute-done | bytes 2162720 | tf_op jit(solution)/shard_map/rows_outward_two/ppermute | solution.py:83
  106.4 1.3 collective-permute-start.13
  107.7 3.6 %dispatch.6 = (bf16[256,256]{1,0:T(8,128)(2,1)S(1)}, bf16[64,4224]{1,0:T(8,128)(2,1)S(1)}, bf16[64,4224]{1,0:T(8,128)(2,1)S(1)}, bf16[64,4224]{1,0:T(8,128)(2,1)S(1)}, bf16[64,4224]{1,0:T(8,128)(2,1)S(1)}) custom-call(f32[8,256]{1,0:T(8,128)S(1)} %pad.15.slots_ref, bf16[256,4224]{1,0:T(8,128)(2,1)} %collective-permute-done.5.refs_0_.refs_2_, ...), custom_call_target="tpu_custom_call" | custom-call | tf_op jit(solution)/shard_map/dispatch/pallas_call | solution.py:144
  111.3 1.6 collective-permute-start.15
  113.2 6.1 %collective-permute-start.10 = (bf16[256,4096]{1,0:T(8,128)(2,1)S(1)}, bf16[256,4096]{1,0:T(8,128)(2,1)S(1)}, u32[]{:S(2)}, u32[]{:S(2)}) collective-permute-start(bf16[256,4096]{1,0:T(8,128)(2,1)S(1)} %decode.5), channel_id=1, source_target_pairs={{0,4},{1,5},{2,6},{3,7},{12,8},{13,9},{14,10},{15,11},{16,20},{17,... | collective-permute-start | bytes 6291464 | tf_op jit(solution)/shard_map/parts_inward/ppermute | solution.py:83
  119.3 7.1 %collective-permute-done.15.refs_2_.refs_6_ = bf16[64,4224]{1,0:T(8,128)(2,1)S(1)} collective-permute-done((bf16[64,4224]{1,0:T(8,128)(2,1)S(1)}, bf16[64,4224]{1,0:T(8,128)(2,1)S(1)}, u32[]{:S(2)}, u32[]{:S(2)}) %collective-permute-start.15) | collective-permute-done | bytes 540704 | tf_op jit(solution)/shard_map/out_2_2/ppermute | solution.py:83
  126.4 10.7 %collective-permute-done.16.refs_3_.refs_7_ = bf16[64,4224]{1,0:T(8,128)(2,1)S(1)} collective-permute-done((bf16[64,4224]{1,0:T(8,128)(2,1)S(1)}, bf16[64,4224]{1,0:T(8,128)(2,1)S(1)}, u32[]{:S(2)}, u32[]{:S(2)}) %collective-permute-start.16) | collective-permute-done | bytes 540704 | tf_op jit(solution)/shard_map/out_2_3/ppermute | solution.py:83
  137.1 5.0 %encode.6 = (f32[16,256]{1,0:T(8,128)S(1)}, s32[16,256]{1,0:T(8,128)S(1)}) custom-call(bf16[64,4224]{1,0:T(8,128)(2,1)S(1)} %get-tuple-element.110.refs_0_.refs_4_, bf16[64,4224]{1,0:T(8,128)(2,1)S(1)} %collective-permute-done.14.refs_1_.refs_5_, bf16[64,4224]{1,0:T(8,128)(2,1)S(1)} %collective-permute-done.15.refs_2_.refs_6_, ...), custom_call_target="tpu_custom_call" | custom-call | tf_op jit(solution)/shard_map/encode/pallas_call | solution.py:197
  142.1 1.6 collective-permute-start.17
  143.7 2.2 collective-permute-done.17.added_ref
  145.9 5.0 %decode.6 = (bf16[64,4096]{1,0:T(8,128)(2,1)S(1)}, bf16[64,4096]{1,0:T(8,128)(2,1)S(1)}, bf16[64,4096]{1,0:T(8,128)(2,1)S(1)}, bf16[64,4096]{1,0:T(8,128)(2,1)S(1)}) custom-call(f32[16,256]{1,0:T(8,128)S(1)} %get-tuple-element.114.chosen_ref, f32[16,256]{1,0:T(8,128)S(1)} %collective-permute-done.17.added_ref, s32[16,256]{1,0:T(8,128)S(1)} %get-tuple-element.115.picks_ref, ...), custom_call_target="tpu_custom_call" | custom-call | tf_op jit(solution)/shard_map/decode/pallas_call | solution.py:244
  151.0 5.6 %collective-permute-done.13.refs_1_.refs_3_ = bf16[256,4224]{1,0:T(8,128)(2,1)S(1)} collective-permute-done((bf16[256,4224]{1,0:T(8,128)(2,1)S(1)}, bf16[256,4224]{1,0:T(8,128)(2,1)S(1)}, u32[]{:S(2)}, u32[]{:S(2)}) %collective-permute-start.13) | collective-permute-done | bytes 2162720 | tf_op jit(solution)/shard_map/rows_outward_far/ppermute | solution.py:83
  156.7 2.1 dispatch.7
  158.9 1.6 collective-permute-start.19
  160.8 1.5 collective-permute-start.22
  162.5 11.6 %collective-permute-done.19.refs_2_.refs_6_ = bf16[64,4224]{1,0:T(8,128)(2,1)S(1)} collective-permute-done((bf16[64,4224]{1,0:T(8,128)(2,1)S(1)}, bf16[64,4224]{1,0:T(8,128)(2,1)S(1)}, u32[]{:S(2)}, u32[]{:S(2)}) %collective-permute-start.19) | collective-permute-done | bytes 540704 | tf_op jit(solution)/shard_map/out_3_2/ppermute | solution.py:83
  174.0 1.3 collective-permute-start.21
  175.3 9.4 %collective-permute-done.24.refs_3_.refs_7_ = bf16[64,4224]{1,0:T(8,128)(2,1)S(1)} collective-permute-done((bf16[64,4224]{1,0:T(8,128)(2,1)S(1)}, bf16[64,4224]{1,0:T(8,128)(2,1)S(1)}, u32[]{:S(2)}, u32[]{:S(2)}) %collective-permute-start.24) | collective-permute-done | bytes 540704 | tf_op jit(solution)/shard_map/out_3_3/ppermute | solution.py:83
  184.7 5.0 %encode.7 = (f32[16,256]{1,0:T(8,128)S(1)}, s32[16,256]{1,0:T(8,128)S(1)}) custom-call(bf16[64,4224]{1,0:T(8,128)(2,1)S(1)} %get-tuple-element.131.refs_0_.refs_4_, bf16[64,4224]{1,0:T(8,128)(2,1)S(1)} %collective-permute-done.20.refs_1_.refs_5_, bf16[64,4224]{1,0:T(8,128)(2,1)S(1)} %collective-permute-done.19.refs_2_.refs_6_, ...), custom_call_target="tpu_custom_call" | custom-call | tf_op jit(solution)/shard_map/encode/pallas_call | solution.py:197
  189.7 1.6 collective-permute-start.25
  191.3 2.3 collective-permute-done.25.added_ref
  193.6 5.0 %decode.7 = (bf16[64,4096]{1,0:T(8,128)(2,1)S(1)}, bf16[64,4096]{1,0:T(8,128)(2,1)S(1)}, bf16[64,4096]{1,0:T(8,128)(2,1)S(1)}, bf16[64,4096]{1,0:T(8,128)(2,1)S(1)}) custom-call(f32[16,256]{1,0:T(8,128)S(1)} %get-tuple-element.134.chosen_ref, f32[16,256]{1,0:T(8,128)S(1)} %collective-permute-done.25.added_ref, s32[16,256]{1,0:T(8,128)S(1)} %get-tuple-element.135.picks_ref, ...), custom_call_target="tpu_custom_call" | custom-call | tf_op jit(solution)/shard_map/decode/pallas_call | solution.py:244
  198.7 8.5 %collective-permute-done.23.refs_3_ = bf16[64,4096]{1,0:T(8,128)(2,1)S(1)} collective-permute-done((bf16[64,4096]{1,0:T(8,128)(2,1)S(1)}, bf16[64,4096]{1,0:T(8,128)(2,1)S(1)}, u32[]{:S(2)}, u32[]{:S(2)}) %collective-permute-start.23) | collective-permute-done | bytes 524320 | tf_op jit(solution)/shard_map/back_2_3/ppermute | solution.py:83
  208.0 2.0 collective-permute-start.30
  210.0 1.6 collective-permute-start.28
  213.0 11.8 %collective-permute-done.28.refs_2_ = bf16[64,4096]{1,0:T(8,128)(2,1)S(1)} collective-permute-done((bf16[64,4096]{1,0:T(8,128)(2,1)S(1)}, bf16[64,4096]{1,0:T(8,128)(2,1)S(1)}, u32[]{:S(2)}, u32[]{:S(2)}) %collective-permute-start.28) | collective-permute-done | bytes 524320 | tf_op jit(solution)/shard_map/back_3_2/ppermute | solution.py:83
  224.9 1.3 collective-permute-start.26
  226.2 7.2 %collective-permute-done.30 = bf16[256,2048]{1,0:T(8,128)(2,1)S(1)} collective-permute-done((bf16[256,2048]{1,0:T(8,128)(2,1)S(1)}, bf16[256,2048]{1,0:T(8,128)(2,1)S(1)}, u32[]{:S(2)}, u32[]{:S(2)}) %collective-permute-start.30) | collective-permute-done | bytes 1048608 | tf_op jit(solution)/shard_map/sum_inward_two_0/ppermute | solution.py:83
  237.1 6.4 %collective-permute-start.35 = (bf16[256,2048]{1,0:T(8,128)(2,1)S(1)}, bf16[256,2048]{1,0:T(8,128)(2,1)S(1)}, u32[]{:S(2)}, u32[]{:S(2)}) collective-permute-start(bf16[256,2048]{1,0:T(8,128)(2,1)S(1)} %combine.7), channel_id=1, source_target_pairs={{0,4},{1,5},{2,6},{3,7},{12,8},{13,9},{14,10},{15,11},{16,20},{17,... | collective-permute-start | bytes 3145736 | tf_op jit(solution)/shard_map/sum_inward_far_0/ppermute | solution.py:83
  243.4 12.5 %collective-permute-done.26 = bf16[256,2048]{1,0:T(8,128)(2,1)S(1)} collective-permute-done((bf16[256,2048]{1,0:T(8,128)(2,1)S(1)}, bf16[256,2048]{1,0:T(8,128)(2,1)S(1)}, u32[]{:S(2)}, u32[]{:S(2)}) %collective-permute-start.26) | collective-permute-done | bytes 1048608 | tf_op jit(solution)/shard_map/sum_inward_two_1/ppermute | solution.py:83
  257.1 1.6 collective-permute-start.36
  258.7 4.4 %collective-permute-start.32 = (bf16[256,2048]{1,0:T(8,128)(2,1)S(1)}, bf16[256,2048]{1,0:T(8,128)(2,1)S(1)}, u32[]{:S(2)}, u32[]{:S(2)}) collective-permute-start(bf16[256,2048]{1,0:T(8,128)(2,1)S(1)} %combine.8), channel_id=1, source_target_pairs={{0,4},{1,5},{2,6},{3,7},{12,8},{13,9},{14,10},{15,11},{16,20},{17,... | collective-permute-start | bytes 3145736 | tf_op jit(solution)/shard_map/sum_inward_far_1/ppermute | solution.py:83
  264.4 14.0 %collective-permute-done.35 = bf16[256,2048]{1,0:T(8,128)(2,1)S(1)} collective-permute-done((bf16[256,2048]{1,0:T(8,128)(2,1)S(1)}, bf16[256,2048]{1,0:T(8,128)(2,1)S(1)}, u32[]{:S(2)}, u32[]{:S(2)}) %collective-permute-start.35) | collective-permute-done | bytes 1048608 | tf_op jit(solution)/shard_map/sum_inward_far_0/ppermute | solution.py:83
  278.4 4.9 %collective-permute-done.36.refs_2_.refs_6_ = bf16[128,4096]{1,0:T(8,128)(2,1)S(1)} collective-permute-done((bf16[128,4096]{1,0:T(8,128)(2,1)S(1)}, bf16[128,4096]{1,0:T(8,128)(2,1)S(1)}, u32[]{:S(2)}, u32[]{:S(2)}) %collective-permute-start.36) | collective-permute-done | bytes 1048608 | tf_op jit(solution)/shard_map/back_near_2/ppermute | solution.py:83
  283.7 1.3 collective-permute-start.38
  285.1 17.7 %collective-permute-done.33.refs_3_.refs_7_ = bf16[128,4096]{1,0:T(8,128)(2,1)S(1)} collective-permute-done((bf16[128,4096]{1,0:T(8,128)(2,1)S(1)}, bf16[128,4096]{1,0:T(8,128)(2,1)S(1)}, u32[]{:S(2)}, u32[]{:S(2)}) %collective-permute-start.33) | collective-permute-done | bytes 1048608 | tf_op jit(solution)/shard_map/back_near_3/ppermute | solution.py:83
  302.8 7.7 %collective-permute-done.38 = bf16[256,2048]{1,0:T(8,128)(2,1)S(1)} collective-permute-done((bf16[256,2048]{1,0:T(8,128)(2,1)S(1)}, bf16[256,2048]{1,0:T(8,128)(2,1)S(1)}, u32[]{:S(2)}, u32[]{:S(2)}) %collective-permute-start.38) | collective-permute-done | bytes 1048608 | tf_op jit(solution)/shard_map/sum_skip_far_0/ppermute | solution.py:83
  310.8 1.3 collective-permute-start.39
  312.5 2.4 combine.9
  314.9 21.6 %collective-permute-done.39 = bf16[256,2048]{1,0:T(8,128)(2,1)S(1)} collective-permute-done((bf16[256,2048]{1,0:T(8,128)(2,1)S(1)}, bf16[256,2048]{1,0:T(8,128)(2,1)S(1)}, u32[]{:S(2)}, u32[]{:S(2)}) %collective-permute-start.39) | collective-permute-done | bytes 1048608 | tf_op jit(solution)/shard_map/sum_skip_far_1/ppermute | solution.py:83
  336.5 1.8 add_convert_fusion
  (77 shorter events, 14.1 us)
Async XLA Ops:
  1.9 6.9 %copy-start.2 = (f32[4096]{0:T(1024)S(1)}, f32[4096]{0:T(1024)}, u32[]{:S(2)}) copy-start(f32[4096]{0:T(1024)} %param.8) | copy-start | bytes 49156
  3.7 50.2 %collective-permute-start.4 = (bf16[256,4224]{1,0:T(8,128)(2,1)S(1)}, bf16[256,4224]{1,0:T(8,128)(2,1)}, u32[]{:S(2)}, u32[]{:S(2)}) collective-permute-start(bf16[256,4224]{1,0:T(8,128)(2,1)S(1)} %pad_maximum_fusion.refs_0_.refs_1_), channel_id=1, source_target_pairs={{0,4},{1,5},{2,6},{3,7},{4,0},{5,1},{6,2},{7,3},{8,12},{9,13},{10,... | collective-permute-start | bytes 6488072 | tf_op jit(solution)/shard_map/rows_ends/ppermute | solution.py:83
  6.8 47.1 %collective-permute-start.5 = (bf16[256,4224]{1,0:T(8,128)(2,1)S(1)}, bf16[256,4224]{1,0:T(8,128)(2,1)}, u32[]{:S(2)}, u32[]{:S(2)}) collective-permute-start(bf16[256,4224]{1,0:T(8,128)(2,1)S(1)} %pad_maximum_fusion.refs_0_.refs_1_), channel_id=1, source_target_pairs={{4,8},{5,9},{6,10},{7,11},{8,4},{9,5},{10,6},{11,7},{20,24},{21,25... | collective-permute-start | bytes 6488072 | tf_op jit(solution)/shard_map/rows_middle/ppermute | solution.py:83
  8.9 4.8 %copy-start.3 = (f32[1,1024]{1,0:T(1,128)S(1)}, f32[1,1024]{1,0:T(1,128)}, u32[]{:S(2)}) copy-start(f32[1,1024]{1,0:T(1,128)} %param.13) | copy-start | bytes 12292
  11.9 2.1 collective-permute-start
  11.9 15.4 %collective-permute-start.1 = (bf16[64,4224]{1,0:T(8,128)(2,1)}, bf16[64,4224]{1,0:T(8,128)(2,1)}, u32[]{:S(2)}, u32[]{:S(2)}) collective-permute-start(bf16[64,4224]{1,0:T(8,128)(2,1)} %get-tuple-element.87), channel_id=1, source_target_pairs={{0,2},{1,3},{2,0},{3,1},{4,6},{5,7},{6,4},{7,5},{8,10},{9,11},{10,... | collective-permute-start | bytes 1622024 | tf_op jit(solution)/shard_map/out_0_2/ppermute | solution.py:83
  13.4 24.7 %collective-permute-start.2 = (bf16[64,4224]{1,0:T(8,128)(2,1)}, bf16[64,4224]{1,0:T(8,128)(2,1)}, u32[]{:S(2)}, u32[]{:S(2)}) collective-permute-start(bf16[64,4224]{1,0:T(8,128)(2,1)} %get-tuple-element.88), channel_id=1, source_target_pairs={{0,3},{1,2},{2,1},{3,0},{4,7},{5,6},{6,5},{7,4},{8,11},{9,10},{10,... | collective-permute-start | bytes 1622024 | tf_op jit(solution)/shard_map/out_0_3/ppermute | solution.py:83
  38.1 3.4 copy-start
  41.4 44.4 %slice-start = ((s8[8388608]{0:T(1024)(128)(4,1)}), s8[4194304]{0:T(1024)(128)(4,1)S(1)}, s32[]{:S(2)}) async-start(s8[8388608]{0:T(1024)(128)(4,1)} %bitcast.5), calls=%async_computation | async-start | bytes 8388608
  47.3 38.5 %slice-start.1 = ((s8[8388608]{0:T(1024)(128)(4,1)}), s8[4194304]{0:T(1024)(128)(4,1)S(1)}, s32[]{:S(2)}) async-start(s8[8388608]{0:T(1024)(128)(4,1)} %bitcast.5), calls=%async_computation.1 | async-start | bytes 8388608
  47.3 3.8 %collective-permute-start.3 = (f32[16,256]{1,0:T(8,128)S(1)}, f32[16,256]{1,0:T(8,128)S(1)}, u32[]{:S(2)}, u32[]{:S(2)}) collective-permute-start(f32[16,256]{1,0:T(8,128)S(1)} %get-tuple-element.89.chosen_ref), channel_id=1, source_target_pairs={{0,16},{16,0},{1,17},{17,1},{2,18},{18,2},{3,19},{19,3},{4,20},{20... | collective-permute-start | bytes 49160 | tf_op jit(solution)/shard_map/sums_0/ppermute | solution.py:357
  54.0 52.4 %collective-permute-start.12 = (bf16[256,4224]{1,0:T(8,128)(2,1)}, bf16[256,4224]{1,0:T(8,128)(2,1)S(1)}, u32[]{:S(2)}, u32[]{:S(2)}) collective-permute-start(bf16[256,4224]{1,0:T(8,128)(2,1)} %collective-permute-done.5.refs_0_.refs_2_), channel_id=1, source_target_pairs={{4,0},{5,1},{6,2},{7,3},{8,12},{9,13},{10,14},{11,15},{20,16},{21,... | collective-permute-start | bytes 6488072 | tf_op jit(solution)/shard_map/rows_outward_two/ppermute | solution.py:83
  55.3 51.1 %collective-permute-start.11 = (bf16[256,4224]{1,0:T(8,128)(2,1)}, bf16[256,4224]{1,0:T(8,128)(2,1)S(1)}, u32[]{:S(2)}, u32[]{:S(2)}) collective-permute-start(bf16[256,4224]{1,0:T(8,128)(2,1)} %collective-permute-done.4.refs_0_.refs_1_), channel_id=1, source_target_pairs={{4,8},{5,9},{6,10},{7,11},{8,4},{9,5},{10,6},{11,7},{20,24},{21,25... | collective-permute-start | bytes 6488072 | tf_op jit(solution)/shard_map/rows_middle_far/ppermute | solution.py:83
  59.9 10.3 %collective-permute-start.6 = (bf16[64,4224]{1,0:T(8,128)(2,1)S(1)}, bf16[64,4224]{1,0:T(8,128)(2,1)S(1)}, u32[]{:S(2)}, u32[]{:S(2)}) collective-permute-start(bf16[64,4224]{1,0:T(8,128)(2,1)S(1)} %get-tuple-element.96), channel_id=1, source_target_pairs={{0,1},{1,0},{2,3},{3,2},{4,5},{5,4},{6,7},{7,6},{8,9},{9,8},{10,11... | collective-permute-start | bytes 1622024 | tf_op jit(solution)/shard_map/out_1_1/ppermute | solution.py:83
  59.9 15.1 %collective-permute-start.7 = (bf16[64,4224]{1,0:T(8,128)(2,1)S(1)}, bf16[64,4224]{1,0:T(8,128)(2,1)S(1)}, u32[]{:S(2)}, u32[]{:S(2)}) collective-permute-start(bf16[64,4224]{1,0:T(8,128)(2,1)S(1)} %get-tuple-element.97), channel_id=1, source_target_pairs={{0,2},{1,3},{2,0},{3,1},{4,6},{5,7},{6,4},{7,5},{8,10},{9,11},{10,... | collective-permute-start | bytes 1622024 | tf_op jit(solution)/shard_map/out_1_2/ppermute | solution.py:83
  61.6 24.2 %collective-permute-start.8 = (bf16[64,4224]{1,0:T(8,128)(2,1)S(1)}, bf16[64,4224]{1,0:T(8,128)(2,1)S(1)}, u32[]{:S(2)}, u32[]{:S(2)}) collective-permute-start(bf16[64,4224]{1,0:T(8,128)(2,1)S(1)} %get-tuple-element.98), channel_id=1, source_target_pairs={{0,3},{1,2},{2,1},{3,0},{4,7},{5,6},{6,5},{7,4},{8,11},{9,10},{10,... | collective-permute-start | bytes 1622024 | tf_op jit(solution)/shard_map/out_1_3/ppermute | solution.py:83
  61.8 3.4 copy-start.1
  65.2 29.5 %slice-start.2 = ((s8[8388608]{0:T(1024)(128)(4,1)}), s8[4194304]{0:T(1024)(128)(4,1)S(1)}, s32[]{:S(2)}) async-start(s8[8388608]{0:T(1024)(128)(4,1)} %bitcast.11), calls=%async_computation.2 | async-start | bytes 8388608
  85.8 8.8 %slice-start.3 = ((s8[8388608]{0:T(1024)(128)(4,1)}), s8[4194304]{0:T(1024)(128)(4,1)S(1)}, s32[]{:S(2)}) async-start(s8[8388608]{0:T(1024)(128)(4,1)} %bitcast.11), calls=%async_computation.3 | async-start | bytes 8388608
  90.8 3.8 %collective-permute-start.9 = (f32[16,256]{1,0:T(8,128)S(1)}, f32[16,256]{1,0:T(8,128)S(1)}, u32[]{:S(2)}, u32[]{:S(2)}) collective-permute-start(f32[16,256]{1,0:T(8,128)S(1)} %get-tuple-element.105.chosen_ref), channel_id=1, source_target_pairs={{0,16},{16,0},{1,17},{17,1},{2,18},{18,2},{3,19},{19,3},{4,20},{20... | collective-permute-start | bytes 49160 | tf_op jit(solution)/shard_map/sums_1/ppermute | solution.py:357
  106.4 50.3 %collective-permute-start.13 = (bf16[256,4224]{1,0:T(8,128)(2,1)S(1)}, bf16[256,4224]{1,0:T(8,128)(2,1)S(1)}, u32[]{:S(2)}, u32[]{:S(2)}) collective-permute-start(bf16[256,4224]{1,0:T(8,128)(2,1)S(1)} %collective-permute-done.11.refs_0_.refs_2_), channel_id=1, source_target_pairs={{4,0},{5,1},{6,2},{7,3},{8,12},{9,13},{10,14},{11,15},{20,16},{21,... | collective-permute-start | bytes 6488072 | tf_op jit(solution)/shard_map/rows_outward_far/ppermute | solution.py:83
  111.2 8.1 %collective-permute-start.14 = (bf16[64,4224]{1,0:T(8,128)(2,1)S(1)}, bf16[64,4224]{1,0:T(8,128)(2,1)S(1)}, u32[]{:S(2)}, u32[]{:S(2)}) collective-permute-start(bf16[64,4224]{1,0:T(8,128)(2,1)S(1)} %get-tuple-element.111), channel_id=1, source_target_pairs={{0,1},{1,0},{2,3},{3,2},{4,5},{5,4},{6,7},{7,6},{8,9},{9,8},{10,11... | collective-permute-start | bytes 1622024 | tf_op jit(solution)/shard_map/out_2_1/ppermute | solution.py:83
  111.3 15.1 %collective-permute-start.15 = (bf16[64,4224]{1,0:T(8,128)(2,1)S(1)}, bf16[64,4224]{1,0:T(8,128)(2,1)S(1)}, u32[]{:S(2)}, u32[]{:S(2)}) collective-permute-start(bf16[64,4224]{1,0:T(8,128)(2,1)S(1)} %get-tuple-element.112), channel_id=1, source_target_pairs={{0,2},{1,3},{2,0},{3,1},{4,6},{5,7},{6,4},{7,5},{8,10},{9,11},{10,... | collective-permute-start | bytes 1622024 | tf_op jit(solution)/shard_map/out_2_2/ppermute | solution.py:83
  112.9 24.3 %collective-permute-start.16 = (bf16[64,4224]{1,0:T(8,128)(2,1)S(1)}, bf16[64,4224]{1,0:T(8,128)(2,1)S(1)}, u32[]{:S(2)}, u32[]{:S(2)}) collective-permute-start(bf16[64,4224]{1,0:T(8,128)(2,1)S(1)} %get-tuple-element.113), channel_id=1, source_target_pairs={{0,3},{1,2},{2,1},{3,0},{4,7},{5,6},{6,5},{7,4},{8,11},{9,10},{10,... | collective-permute-start | bytes 1622024 | tf_op jit(solution)/shard_map/out_2_3/ppermute | solution.py:83
  113.2 62.2 %collective-permute-start.10 = (bf16[256,4096]{1,0:T(8,128)(2,1)S(1)}, bf16[256,4096]{1,0:T(8,128)(2,1)S(1)}, u32[]{:S(2)}, u32[]{:S(2)}) collective-permute-start(bf16[256,4096]{1,0:T(8,128)(2,1)S(1)} %decode.5), channel_id=1, source_target_pairs={{0,4},{1,5},{2,6},{3,7},{12,8},{13,9},{14,10},{15,11},{16,20},{17,... | collective-permute-start | bytes 6291464 | tf_op jit(solution)/shard_map/parts_inward/ppermute | solution.py:83
  142.1 3.8 %collective-permute-start.17 = (f32[16,256]{1,0:T(8,128)S(1)}, f32[16,256]{1,0:T(8,128)S(1)}, u32[]{:S(2)}, u32[]{:S(2)}) collective-permute-start(f32[16,256]{1,0:T(8,128)S(1)} %get-tuple-element.114.chosen_ref), channel_id=1, source_target_pairs={{0,16},{16,0},{1,17},{17,1},{2,18},{18,2},{3,19},{19,3},{4,20},{20... | collective-permute-start | bytes 49160 | tf_op jit(solution)/shard_map/sums_2/ppermute | solution.py:357
  150.9 5.7 %collective-permute-start.18 = (bf16[64,4096]{1,0:T(8,128)(2,1)S(1)}, bf16[64,4096]{1,0:T(8,128)(2,1)S(1)}, u32[]{:S(2)}, u32[]{:S(2)}) collective-permute-start(bf16[64,4096]{1,0:T(8,128)(2,1)S(1)} %get-tuple-element.117), channel_id=1, source_target_pairs={{0,1},{1,0},{2,3},{3,2},{4,5},{5,4},{6,7},{7,6},{8,9},{9,8},{10,11... | collective-permute-start | bytes 1572872 | tf_op jit(solution)/shard_map/back_2_1/ppermute | solution.py:83
  158.8 3.4 %collective-permute-start.20 = (bf16[64,4224]{1,0:T(8,128)(2,1)S(1)}, bf16[64,4224]{1,0:T(8,128)(2,1)S(1)}, u32[]{:S(2)}, u32[]{:S(2)}) collective-permute-start(bf16[64,4224]{1,0:T(8,128)(2,1)S(1)} %get-tuple-element.124), channel_id=1, source_target_pairs={{0,1},{1,0},{2,3},{3,2},{4,5},{5,4},{6,7},{7,6},{8,9},{9,8},{10,11... | collective-permute-start | bytes 1622024 | tf_op jit(solution)/shard_map/out_3_1/ppermute | solution.py:83
  158.9 15.1 %collective-permute-start.19 = (bf16[64,4224]{1,0:T(8,128)(2,1)S(1)}, bf16[64,4224]{1,0:T(8,128)(2,1)S(1)}, u32[]{:S(2)}, u32[]{:S(2)}) collective-permute-start(bf16[64,4224]{1,0:T(8,128)(2,1)S(1)} %get-tuple-element.123), channel_id=1, source_target_pairs={{0,2},{1,3},{2,0},{3,1},{4,6},{5,7},{6,4},{7,5},{8,10},{9,11},{10,... | collective-permute-start | bytes 1622024 | tf_op jit(solution)/shard_map/out_3_2/ppermute | solution.py:83
  160.4 24.3 %collective-permute-start.24 = (bf16[64,4224]{1,0:T(8,128)(2,1)S(1)}, bf16[64,4224]{1,0:T(8,128)(2,1)S(1)}, u32[]{:S(2)}, u32[]{:S(2)}) collective-permute-start(bf16[64,4224]{1,0:T(8,128)(2,1)S(1)} %get-tuple-element.132), channel_id=1, source_target_pairs={{0,3},{1,2},{2,1},{3,0},{4,7},{5,6},{6,5},{7,4},{8,11},{9,10},{10,... | collective-permute-start | bytes 1622024 | tf_op jit(solution)/shard_map/out_3_3/ppermute | solution.py:83
  160.8 37.9 %collective-permute-start.22 = (bf16[64,4096]{1,0:T(8,128)(2,1)S(1)}, bf16[64,4096]{1,0:T(8,128)(2,1)S(1)}, u32[]{:S(2)}, u32[]{:S(2)}) collective-permute-start(bf16[64,4096]{1,0:T(8,128)(2,1)S(1)} %get-tuple-element.118), channel_id=1, source_target_pairs={{0,2},{1,3},{2,0},{3,1},{4,6},{5,7},{6,4},{7,5},{8,10},{9,11},{10,... | collective-permute-start | bytes 1572872 | tf_op jit(solution)/shard_map/back_2_2/ppermute | solution.py:83
  162.2 44.9 %collective-permute-start.23 = (bf16[64,4096]{1,0:T(8,128)(2,1)S(1)}, bf16[64,4096]{1,0:T(8,128)(2,1)S(1)}, u32[]{:S(2)}, u32[]{:S(2)}) collective-permute-start(bf16[64,4096]{1,0:T(8,128)(2,1)S(1)} %get-tuple-element.119), channel_id=1, source_target_pairs={{0,3},{1,2},{2,1},{3,0},{4,7},{5,6},{6,5},{7,4},{8,11},{9,10},{10,... | collective-permute-start | bytes 1572872 | tf_op jit(solution)/shard_map/back_2_3/ppermute | solution.py:83
  174.0 81.9 %collective-permute-start.21 = (bf16[256,4096]{1,0:T(8,128)(2,1)S(1)}, bf16[256,4096]{1,0:T(8,128)(2,1)S(1)}, u32[]{:S(2)}, u32[]{:S(2)}) collective-permute-start(bf16[256,4096]{1,0:T(8,128)(2,1)S(1)} %decode.5), channel_id=1, source_target_pairs={{4,0},{5,1},{6,2},{7,3},{8,12},{9,13},{10,14},{11,15},{20,16},{21,... | collective-permute-start | bytes 6291464 | tf_op jit(solution)/shard_map/parts_outward/ppermute | solution.py:83
  189.7 3.9 %collective-permute-start.25 = (f32[16,256]{1,0:T(8,128)S(1)}, f32[16,256]{1,0:T(8,128)S(1)}, u32[]{:S(2)}, u32[]{:S(2)}) collective-permute-start(f32[16,256]{1,0:T(8,128)S(1)} %get-tuple-element.134.chosen_ref), channel_id=1, source_target_pairs={{0,16},{16,0},{1,17},{17,1},{2,18},{18,2},{3,19},{19,3},{4,20},{20... | collective-permute-start | bytes 49160 | tf_op jit(solution)/shard_map/sums_3/ppermute | solution.py:357
  208.0 25.5 %collective-permute-start.30 = (bf16[256,2048]{1,0:T(8,128)(2,1)S(1)}, bf16[256,2048]{1,0:T(8,128)(2,1)S(1)}, u32[]{:S(2)}, u32[]{:S(2)}) collective-permute-start(bf16[256,2048]{1,0:T(8,128)(2,1)S(1)} %combine.6), channel_id=1, source_target_pairs={{0,4},{1,5},{2,6},{3,7},{12,8},{13,9},{14,10},{15,11},{16,20},{17,... | collective-permute-start | bytes 3145736 | tf_op jit(solution)/shard_map/sum_inward_two_0/ppermute | solution.py:83
  210.0 14.8 %collective-permute-start.28 = (bf16[64,4096]{1,0:T(8,128)(2,1)S(1)}, bf16[64,4096]{1,0:T(8,128)(2,1)S(1)}, u32[]{:S(2)}, u32[]{:S(2)}) collective-permute-start(bf16[64,4096]{1,0:T(8,128)(2,1)S(1)} %get-tuple-element.138), channel_id=1, source_target_pairs={{0,2},{1,3},{2,0},{3,1},{4,6},{5,7},{6,4},{7,5},{8,10},{9,11},{10,... | collective-permute-start | bytes 1572872 | tf_op jit(solution)/shard_map/back_3_2/ppermute | solution.py:83
  211.6 21.9 %collective-permute-start.27 = (bf16[64,4096]{1,0:T(8,128)(2,1)S(1)}, bf16[64,4096]{1,0:T(8,128)(2,1)S(1)}, u32[]{:S(2)}, u32[]{:S(2)}) collective-permute-start(bf16[64,4096]{1,0:T(8,128)(2,1)S(1)} %get-tuple-element.137), channel_id=1, source_target_pairs={{0,1},{1,0},{2,3},{3,2},{4,5},{5,4},{6,7},{7,6},{8,9},{9,8},{10,11... | collective-permute-start | bytes 1572872 | tf_op jit(solution)/shard_map/back_3_1/ppermute | solution.py:83
  211.6 22.8 %collective-permute-start.29 = (bf16[64,4096]{1,0:T(8,128)(2,1)S(1)}, bf16[64,4096]{1,0:T(8,128)(2,1)S(1)}, u32[]{:S(2)}, u32[]{:S(2)}) collective-permute-start(bf16[64,4096]{1,0:T(8,128)(2,1)S(1)} %get-tuple-element.139), channel_id=1, source_target_pairs={{0,3},{1,2},{2,1},{3,0},{4,7},{5,6},{6,5},{7,4},{8,11},{9,10},{10,... | collective-permute-start | bytes 1572872 | tf_op jit(solution)/shard_map/back_3_3/ppermute | solution.py:83
  224.9 31.0 %collective-permute-start.26 = (bf16[256,2048]{1,0:T(8,128)(2,1)S(1)}, bf16[256,2048]{1,0:T(8,128)(2,1)S(1)}, u32[]{:S(2)}, u32[]{:S(2)}) collective-permute-start(bf16[256,2048]{1,0:T(8,128)(2,1)S(1)} %combine.5), channel_id=1, source_target_pairs={{0,4},{1,5},{2,6},{3,7},{12,8},{13,9},{14,10},{15,11},{16,20},{17,... | collective-permute-start | bytes 3145736 | tf_op jit(solution)/shard_map/sum_inward_two_1/ppermute | solution.py:83
  236.3 27.9 %collective-permute-start.37 = (bf16[256,2048]{1,0:T(8,128)(2,1)S(1)}, bf16[256,2048]{1,0:T(8,128)(2,1)S(1)}, u32[]{:S(2)}, u32[]{:S(2)}) collective-permute-start(bf16[256,2048]{1,0:T(8,128)(2,1)S(1)} %add_convert_fusion.3), channel_id=1, source_target_pairs={{4,8},{5,9},{6,10},{7,11},{8,4},{9,5},{10,6},{11,7},{20,24},{21,25... | collective-permute-start | bytes 3145736 | tf_op jit(solution)/shard_map/sum_middle_two_0/ppermute | solution.py:83
  237.1 41.3 %collective-permute-start.35 = (bf16[256,2048]{1,0:T(8,128)(2,1)S(1)}, bf16[256,2048]{1,0:T(8,128)(2,1)S(1)}, u32[]{:S(2)}, u32[]{:S(2)}) collective-permute-start(bf16[256,2048]{1,0:T(8,128)(2,1)S(1)} %combine.7), channel_id=1, source_target_pairs={{0,4},{1,5},{2,6},{3,7},{12,8},{13,9},{14,10},{15,11},{16,20},{17,... | collective-permute-start | bytes 3145736 | tf_op jit(solution)/shard_map/sum_inward_far_0/ppermute | solution.py:83
  257.1 26.2 %collective-permute-start.36 = (bf16[128,4096]{1,0:T(8,128)(2,1)S(1)}, bf16[128,4096]{1,0:T(8,128)(2,1)S(1)}, u32[]{:S(2)}, u32[]{:S(2)}) collective-permute-start(bf16[128,4096]{1,0:T(8,128)(2,1)S(1)} %pad_maximum_fusion.2), channel_id=1, source_target_pairs={{0,2},{1,3},{2,0},{3,1},{4,6},{5,7},{6,4},{7,5},{8,10},{9,11},{10,... | collective-permute-start | bytes 3145736 | tf_op jit(solution)/shard_map/back_near_2/ppermute | solution.py:83
  258.7 44.1 %collective-permute-start.32 = (bf16[256,2048]{1,0:T(8,128)(2,1)S(1)}, bf16[256,2048]{1,0:T(8,128)(2,1)S(1)}, u32[]{:S(2)}, u32[]{:S(2)}) collective-permute-start(bf16[256,2048]{1,0:T(8,128)(2,1)S(1)} %combine.8), channel_id=1, source_target_pairs={{0,4},{1,5},{2,6},{3,7},{12,8},{13,9},{14,10},{15,11},{16,20},{17,... | collective-permute-start | bytes 3145736 | tf_op jit(solution)/shard_map/sum_inward_far_1/ppermute | solution.py:83
  263.5 21.5 %collective-permute-start.34 = (bf16[256,2048]{1,0:T(8,128)(2,1)S(1)}, bf16[256,2048]{1,0:T(8,128)(2,1)S(1)}, u32[]{:S(2)}, u32[]{:S(2)}) collective-permute-start(bf16[256,2048]{1,0:T(8,128)(2,1)S(1)} %add_convert_fusion.4), channel_id=1, source_target_pairs={{4,8},{5,9},{6,10},{7,11},{8,4},{9,5},{10,6},{11,7},{20,24},{21,25... | collective-permute-start | bytes 3145736 | tf_op jit(solution)/shard_map/sum_middle_two_1/ppermute | solution.py:83
  264.3 38.5 %collective-permute-start.33 = (bf16[128,4096]{1,0:T(8,128)(2,1)S(1)}, bf16[128,4096]{1,0:T(8,128)(2,1)S(1)}, u32[]{:S(2)}, u32[]{:S(2)}) collective-permute-start(bf16[128,4096]{1,0:T(8,128)(2,1)S(1)} %pad_maximum_fusion.3), channel_id=1, source_target_pairs={{0,3},{1,2},{2,1},{3,0},{4,7},{5,6},{6,5},{7,4},{8,11},{9,10},{10,... | collective-permute-start | bytes 3145736 | tf_op jit(solution)/shard_map/back_near_3/ppermute | solution.py:83
  283.7 26.8 %collective-permute-start.38 = (bf16[256,2048]{1,0:T(8,128)(2,1)S(1)}, bf16[256,2048]{1,0:T(8,128)(2,1)S(1)}, u32[]{:S(2)}, u32[]{:S(2)}) collective-permute-start(bf16[256,2048]{1,0:T(8,128)(2,1)S(1)} %add_convert_fusion.2), channel_id=1, source_target_pairs={{4,12},{5,13},{6,14},{7,15},{8,0},{9,1},{10,2},{11,3},{20,28},{21,... | collective-permute-start | bytes 3145736 | tf_op jit(solution)/shard_map/sum_skip_far_0/ppermute | solution.py:83
  285.0 27.5 %collective-permute-start.31 = (bf16[128,4096]{1,0:T(8,128)(2,1)S(1)}, bf16[128,4096]{1,0:T(8,128)(2,1)S(1)}, u32[]{:S(2)}, u32[]{:S(2)}) collective-permute-start(bf16[128,4096]{1,0:T(8,128)(2,1)S(1)} %pad_maximum_fusion.1), channel_id=1, source_target_pairs={{0,1},{1,0},{2,3},{3,2},{4,5},{5,4},{6,7},{7,6},{8,9},{9,8},{10,11... | collective-permute-start | bytes 3145736 | tf_op jit(solution)/shard_map/back_near_1/ppermute | solution.py:83
  310.8 25.7 %collective-permute-start.39 = (bf16[256,2048]{1,0:T(8,128)(2,1)S(1)}, bf16[256,2048]{1,0:T(8,128)(2,1)S(1)}, u32[]{:S(2)}, u32[]{:S(2)}) collective-permute-start(bf16[256,2048]{1,0:T(8,128)(2,1)S(1)} %add_convert_fusion.1), channel_id=1, source_target_pairs={{4,12},{5,13},{6,14},{7,15},{8,0},{9,1},{10,2},{11,3},{20,28},{21,... | collective-permute-start | bytes 3145736 | tf_op jit(solution)/shard_map/sum_skip_far_1/ppermute | solution.py:83

commit v4 on v3

--- a/solution.py
+++ b/solution.py
@@ -101,60 +101,43 @@
     )
 
 
-def dispatch_kernel(cap, slots_ref, extra_refs, value_refs, offset_ref, spread_ref, out_refs, place_ref):
-    rows = spread_ref.shape[0]
-
-    @pl.when(pl.program_id(0) == 0)
-    def _():
-        extra = extra_refs[0][...].astype(F32)
-        for ref in extra_refs[1:]:
-            extra = extra + ref[...].astype(F32)
-        hit = (extra[:, 0:1] == slots_ref[0:1, :]) | (extra[:, 1:2] == slots_ref[0:1, :])
-        earlier = lax.broadcasted_iota(jnp.int32, (rows, rows), 1) < lax.broadcasted_iota(
-            jnp.int32, (rows, rows), 0
-        )
-        rank = jnp.dot(
-            jnp.where(earlier, 1.0, 0.0).astype(BF16),
-            jnp.where(hit, 1.0, 0.0).astype(BF16),
-            preferred_element_type=F32,
-        )
-        spread = jnp.where(hit & (rank == slots_ref[1:2, :]), 1.0, 0.0)
-        spread_ref[...] = spread.astype(BF16)
-        place_ref[...] = spread.T.astype(BF16)
-
+def dispatch_kernel(cap, n, slots_ref, offset_ref, *refs):
+    value_refs, (spread_ref, *out_refs) = refs[:n], refs[n:]
+    rows, wide = value_refs[0].shape
+    extra = value_refs[0][:, wide - EXTRA:].astype(F32)
+    for ref in value_refs[1:]:
+        extra = extra + ref[:, wide - EXTRA:].astype(F32)
+    hit = (extra[:, 0:1] == slots_ref[0:1, :]) | (extra[:, 1:2] == slots_ref[0:1, :])
+    earlier = lax.broadcasted_iota(jnp.int32, (rows, rows), 1) < lax.broadcasted_iota(
+        jnp.int32, (rows, rows), 0
+    )
+    rank = jnp.dot(
+        jnp.where(earlier, 1.0, 0.0).astype(BF16),
+        jnp.where(hit, 1.0, 0.0).astype(BF16),
+        preferred_element_type=F32,
+    )
+    spread = jnp.where(hit & (rank == slots_ref[1:2, :]), 1.0, 0.0)
+    spread_ref[...] = spread.astype(BF16)
     value = value_refs[0][...]
     for ref in value_refs[1:]:
         value = value + ref[...]
-    moved = jnp.dot(place_ref[...], value, preferred_element_type=F32) - offset_ref[...]
-    moved = moved.astype(BF16)
+    place = spread.T.astype(BF16)
+    moved = (jnp.dot(place, value, preferred_element_type=F32) - offset_ref[...]).astype(BF16)
     for j, ref in enumerate(out_refs):
         ref[...] = moved[j * cap:(j + 1) * cap]
 
 
 def dispatch(values, offset, slots, cap):
     rows, wide = values[0].shape
-    step = wide // 3
-    n = len(values)
-
-    def kernel(slots_ref, *refs):
-        dispatch_kernel(
-            cap, slots_ref, refs[:n], refs[n:2 * n], refs[2 * n], refs[2 * n + 1], refs[2 * n + 2:-1], refs[-1]
-        )
-
     spread, *pieces = call(
-        kernel,
+        functools.partial(dispatch_kernel, cap, len(values)),
         "dispatch",
-        (3,),
-        [pl.BlockSpec((8, INNER * cap), lambda j: (0, 0))]
-        + [pl.BlockSpec((rows, EXTRA), lambda j: (0, wide // EXTRA - 1))] * n
-        + [pl.BlockSpec((rows, step), lambda j: (0, j))] * n
-        + [pl.BlockSpec((1, step), lambda j: (0, j))],
-        [pl.BlockSpec((rows, INNER * cap), lambda j: (0, 0))]
-        + [pl.BlockSpec((cap, step), lambda j: (0, j))] * INNER,
+        (),
+        [pl.BlockSpec(memory_space=pltpu.VMEM)] * (2 + len(values)),
+        [pl.BlockSpec(memory_space=pltpu.VMEM)] * (1 + INNER),
         [jax.ShapeDtypeStruct((rows, INNER * cap), BF16)]
         + [jax.ShapeDtypeStruct((cap, wide), BF16)] * INNER,
-        [pltpu.VMEM((INNER * cap, rows), BF16)],
-    )(slots, *values, *values, offset)
+    )(slots, offset, *values)
     return spread, pieces
 
 
@@ -430,12 +413,12 @@
             twos.append(move(plus(back2[i], from_two[i]), MIDDLE))
 
     returned3[2] = after(returned3[2], *back2)
-    two_on(0, returned3[2])
+    outward = after(outward, returned3[2])
+    two_on(0, outward)
     returned3 = all_after(returned3, from_two[0])
     back3 = combined(spreads[3], returned3, FAR_SHARES)
     two_on(1, *back3)
     twos[0] = after(twos[0], from_two[1])
-    outward = after(outward, from_two[1])
     from_far = []
     for i, value in enumerate(back3):
         with jax.named_scope(f"sum_inward_far_{i}"):

time: 339 us -> 337 us (level)
    pallas_call x4, Pallas kernels: 12.5 us -> 8.85 us  [dispatch(): call(functools.partial(dispatch_kernel, cap, len(values)), 'dispatch', ()...]
    unnamed x16 -> x10, local copies, waits for them, and re-layouts: 6.79 us -> 3.4 us
  transfers between devices with their start and end apart: 40 -> 40, of which waited for: 26 -> 26; matrix products, arithmetic and copies ran while one was open for 1% -> 1% of each run, Pallas kernels for 18% -> 17%
where the time goes in v4:
time: 337 us; the launch traced here: 336 us
  waiting for transfers between devices  212 us (63%)
  Pallas kernels  55.9 us (17%)
  starting transfers between devices  55.8 us (17%)
  other arithmetic  7.14 us (2%)
  local copies, waits for them, and re-layouts  4.58 us (1%)
    ppermute x36, waiting for transfers between devices, move(): return lax.ppermute(value, 'blocks', pairs)  203 us
    ppermute x36, starting transfers between devices, move(): return lax.ppermute(value, 'blocks', pairs)  49.5 us
    pallas_call x4, Pallas kernels, encode(): call(kernel, 'encode', (width // BLOCK,), [pl.BlockSpec((cap, BLOCK), lam...  21.1 us
    pallas_call x4, Pallas kernels, decode(): call(decode_kernel, 'decode', (width // BLOCK,), [pl.BlockSpec((picked, s...  20.1 us
    ppermute x4, waiting for transfers between devices, encoded(): added = lax.ppermute(chosen, 'dp', [(0, 1), (1, 0)])  8.91 us
    pallas_call x4, Pallas kernels, dispatch(): call(functools.partial(dispatch_kernel, cap, len(values)), 'dispatch', ()...  8.85 us
  transfers between devices with their start and end apart: 40, of which 26 were waited for; matrix products, arithmetic and copies ran while one was open for 1% of the time, Pallas kernels for 17%

profile of v4, /device:TPU:0, one launch (start us, length us, event | category | flops | bytes accessed | tf_op | source)
XLA Modules:
  0.0 336.4 jit_solution(2460976549935058466)
XLA Ops:
  2.0 1.8 pad_maximum_fusion.refs_0_
  3.7 2.0 collective-permute-start.5
  5.8 4.5 %collective-permute-start.4 = (bf16[256,4224]{1,0:T(8,128)(2,1)S(1)}, bf16[256,4224]{1,0:T(8,128)(2,1)}, u32[]{:S(2)}, u32[]{:S(2)}) collective-permute-start(bf16[256,4224]{1,0:T(8,128)(2,1)S(1)} %pad_maximum_fusion.refs_0_), channel_id=1, source_target_pairs={{0,4},{1,5},{2,6},{3,7},{4,0},{5,1},{6,2},{7,3},{8,12},{9,13},{10,... | collective-permute-start | bytes 6488072 | tf_op jit(solution)/shard_map/rows_ends/ppermute | solution.py:83
  10.4 2.2 dispatch.4
  12.7 1.5 collective-permute-start.1
  14.8 13.2 %collective-permute-done.1.refs_2_.refs_6_ = bf16[64,4224]{1,0:T(8,128)(2,1)} collective-permute-done((bf16[64,4224]{1,0:T(8,128)(2,1)}, bf16[64,4224]{1,0:T(8,128)(2,1)}, u32[]{:S(2)}, u32[]{:S(2)}) %collective-permute-start.1) | collective-permute-done | bytes 540704 | tf_op jit(solution)/shard_map/out_0_2/ppermute | solution.py:83
  28.0 10.8 %collective-permute-done.2.refs_3_.refs_7_ = bf16[64,4224]{1,0:T(8,128)(2,1)} collective-permute-done((bf16[64,4224]{1,0:T(8,128)(2,1)}, bf16[64,4224]{1,0:T(8,128)(2,1)}, u32[]{:S(2)}, u32[]{:S(2)}) %collective-permute-start.2) | collective-permute-done | bytes 540704 | tf_op jit(solution)/shard_map/out_0_3/ppermute | solution.py:83
  38.9 3.4 %copy-done = bf16[1,4096,1024]{2,1,0:T(8,128)(2,1)S(1)} copy-done((bf16[1,4096,1024]{2,1,0:T(8,128)(2,1)S(1)}, bf16[1,4096,1024]{2,1,0:T(8,128)(2,1)}, u32[]{:S(2)}) %copy-start) | copy-done | bytes 8388632
  42.2 6.2 %encode.4 = (f32[16,256]{1,0:T(8,128)S(1)}, s32[16,256]{1,0:T(8,128)S(1)}) custom-call(bf16[64,4224]{1,0:T(8,128)(2,1)S(1)} %get-tuple-element.85.refs_0_.refs_4_, bf16[64,4224]{1,0:T(8,128)(2,1)S(1)} %collective-permute-done.refs_1_.refs_5_, bf16[64,4224]{1,0:T(8,128)(2,1)} %collective-permute-done.1.refs_2_.refs_6_, ...), custom_call_target="tpu_custom_call" | custom-call | tf_op jit(solution)/shard_map/encode/pallas_call | solution.py:180
  48.5 1.6 collective-permute-start.3
  50.0 2.2 collective-permute-done.3.added_ref
  52.3 4.9 %collective-permute-done.4.refs_0_ = bf16[256,4224]{1,0:T(8,128)(2,1)} collective-permute-done((bf16[256,4224]{1,0:T(8,128)(2,1)S(1)}, bf16[256,4224]{1,0:T(8,128)(2,1)}, u32[]{:S(2)}, u32[]{:S(2)}) %collective-permute-start.4) | collective-permute-done | bytes 2162720 | tf_op jit(solution)/shard_map/rows_ends/ppermute | solution.py:83
  57.2 1.3 collective-permute-start.12
  59.3 2.7 dispatch.5
  62.1 1.6 collective-permute-start.7
  64.0 5.0 %decode.4 = (bf16[64,4096]{1,0:T(8,128)(2,1)S(1)}, bf16[64,4096]{1,0:T(8,128)(2,1)S(1)}, bf16[64,4096]{1,0:T(8,128)(2,1)S(1)}, bf16[64,4096]{1,0:T(8,128)(2,1)S(1)}) custom-call(f32[16,256]{1,0:T(8,128)S(1)} %get-tuple-element.89.chosen_ref, f32[16,256]{1,0:T(8,128)S(1)} %collective-permute-done.3.added_ref, s32[16,256]{1,0:T(8,128)S(1)} %get-tuple-element.91.picks_ref, ...), custom_call_target="tpu_custom_call" | custom-call | tf_op jit(solution)/shard_map/decode/pallas_call | solution.py:227
  69.0 8.2 %collective-permute-done.7.refs_2_.refs_6_ = bf16[64,4224]{1,0:T(8,128)(2,1)S(1)} collective-permute-done((bf16[64,4224]{1,0:T(8,128)(2,1)S(1)}, bf16[64,4224]{1,0:T(8,128)(2,1)S(1)}, u32[]{:S(2)}, u32[]{:S(2)}) %collective-permute-start.7) | collective-permute-done | bytes 540704 | tf_op jit(solution)/shard_map/out_1_2/ppermute | solution.py:83
  77.2 10.7 %collective-permute-done.8.refs_3_.refs_7_ = bf16[64,4224]{1,0:T(8,128)(2,1)S(1)} collective-permute-done((bf16[64,4224]{1,0:T(8,128)(2,1)S(1)}, bf16[64,4224]{1,0:T(8,128)(2,1)S(1)}, u32[]{:S(2)}, u32[]{:S(2)}) %collective-permute-start.8) | collective-permute-done | bytes 540704 | tf_op jit(solution)/shard_map/out_1_3/ppermute | solution.py:83
  87.9 5.0 %encode.5 = (f32[16,256]{1,0:T(8,128)S(1)}, s32[16,256]{1,0:T(8,128)S(1)}) custom-call(bf16[64,4224]{1,0:T(8,128)(2,1)S(1)} %get-tuple-element.101.refs_0_.refs_4_, bf16[64,4224]{1,0:T(8,128)(2,1)S(1)} %collective-permute-done.6.refs_1_.refs_5_, bf16[64,4224]{1,0:T(8,128)(2,1)S(1)} %collective-permute-done.7.refs_2_.refs_6_, ...), custom_call_target="tpu_custom_call" | custom-call | tf_op jit(solution)/shard_map/encode/pallas_call | solution.py:180
  92.9 1.6 collective-permute-start.9
  94.5 2.2 collective-permute-done.9.added_ref
  96.7 5.0 %decode.5 = bf16[256,4096]{1,0:T(8,128)(2,1)S(1)} custom-call(f32[16,256]{1,0:T(8,128)S(1)} %get-tuple-element.105.chosen_ref, f32[16,256]{1,0:T(8,128)S(1)} %collective-permute-done.9.added_ref, s32[16,256]{1,0:T(8,128)S(1)} %get-tuple-element.106.picks_ref, bf16[1024,4096]{1,0:T(8,128)(2,1)S(1)} %bitcast.9), custom_call_target="tpu_custom_call" | custom-call | tf_op jit(solution)/shard_map/decode/pallas_call | solution.py:227
  101.7 5.5 %collective-permute-done.12.refs_1_ = bf16[256,4224]{1,0:T(8,128)(2,1)S(1)} collective-permute-done((bf16[256,4224]{1,0:T(8,128)(2,1)}, bf16[256,4224]{1,0:T(8,128)(2,1)S(1)}, u32[]{:S(2)}, u32[]{:S(2)}) %collective-permute-start.12) | collective-permute-done | bytes 2162720 | tf_op jit(solution)/shard_map/rows_outward_two/ppermute | solution.py:83
  107.2 1.5 collective-permute-start.13
  108.7 2.8 dispatch.6
  111.5 1.6 collective-permute-start.15
  113.4 6.0 %collective-permute-start.10 = (bf16[256,4096]{1,0:T(8,128)(2,1)S(1)}, bf16[256,4096]{1,0:T(8,128)(2,1)S(1)}, u32[]{:S(2)}, u32[]{:S(2)}) collective-permute-start(bf16[256,4096]{1,0:T(8,128)(2,1)S(1)} %decode.5), channel_id=1, source_target_pairs={{0,4},{1,5},{2,6},{3,7},{12,8},{13,9},{14,10},{15,11},{16,20},{17,... | collective-permute-start | bytes 6291464 | tf_op jit(solution)/shard_map/parts_inward/ppermute | solution.py:83
  119.3 7.3 %collective-permute-done.15.refs_2_.refs_6_ = bf16[64,4224]{1,0:T(8,128)(2,1)S(1)} collective-permute-done((bf16[64,4224]{1,0:T(8,128)(2,1)S(1)}, bf16[64,4224]{1,0:T(8,128)(2,1)S(1)}, u32[]{:S(2)}, u32[]{:S(2)}) %collective-permute-start.15) | collective-permute-done | bytes 540704 | tf_op jit(solution)/shard_map/out_2_2/ppermute | solution.py:83
  126.6 10.7 %collective-permute-done.16.refs_3_.refs_7_ = bf16[64,4224]{1,0:T(8,128)(2,1)S(1)} collective-permute-done((bf16[64,4224]{1,0:T(8,128)(2,1)S(1)}, bf16[64,4224]{1,0:T(8,128)(2,1)S(1)}, u32[]{:S(2)}, u32[]{:S(2)}) %collective-permute-start.16) | collective-permute-done | bytes 540704 | tf_op jit(solution)/shard_map/out_2_3/ppermute | solution.py:83
  137.3 5.0 %encode.6 = (f32[16,256]{1,0:T(8,128)S(1)}, s32[16,256]{1,0:T(8,128)S(1)}) custom-call(bf16[64,4224]{1,0:T(8,128)(2,1)S(1)} %get-tuple-element.110.refs_0_.refs_4_, bf16[64,4224]{1,0:T(8,128)(2,1)S(1)} %collective-permute-done.14.refs_1_.refs_5_, bf16[64,4224]{1,0:T(8,128)(2,1)S(1)} %collective-permute-done.15.refs_2_.refs_6_, ...), custom_call_target="tpu_custom_call" | custom-call | tf_op jit(solution)/shard_map/encode/pallas_call | solution.py:180
  142.3 1.6 collective-permute-start.17
  143.9 2.2 collective-permute-done.17.added_ref
  146.1 5.0 %decode.6 = (bf16[64,4096]{1,0:T(8,128)(2,1)S(1)}, bf16[64,4096]{1,0:T(8,128)(2,1)S(1)}, bf16[64,4096]{1,0:T(8,128)(2,1)S(1)}, bf16[64,4096]{1,0:T(8,128)(2,1)S(1)}) custom-call(f32[16,256]{1,0:T(8,128)S(1)} %get-tuple-element.114.chosen_ref, f32[16,256]{1,0:T(8,128)S(1)} %collective-permute-done.17.added_ref, s32[16,256]{1,0:T(8,128)S(1)} %get-tuple-element.115.picks_ref, ...), custom_call_target="tpu_custom_call" | custom-call | tf_op jit(solution)/shard_map/decode/pallas_call | solution.py:227
  151.2 6.0 %collective-permute-done.13.refs_1_ = bf16[256,4224]{1,0:T(8,128)(2,1)S(1)} collective-permute-done((bf16[256,4224]{1,0:T(8,128)(2,1)S(1)}, bf16[256,4224]{1,0:T(8,128)(2,1)S(1)}, u32[]{:S(2)}, u32[]{:S(2)}) %collective-permute-start.13) | collective-permute-done | bytes 2162720 | tf_op jit(solution)/shard_map/rows_outward_far/ppermute | solution.py:83
  157.2 1.1 dispatch.7
  158.4 1.6 collective-permute-start.19
  159.9 1.3 collective-permute-start.21
  161.9 11.7 %collective-permute-done.19.refs_2_.refs_6_ = bf16[64,4224]{1,0:T(8,128)(2,1)S(1)} collective-permute-done((bf16[64,4224]{1,0:T(8,128)(2,1)S(1)}, bf16[64,4224]{1,0:T(8,128)(2,1)S(1)}, u32[]{:S(2)}, u32[]{:S(2)}) %collective-permute-start.19) | collective-permute-done | bytes 540704 | tf_op jit(solution)/shard_map/out_3_2/ppermute | solution.py:83
  173.6 1.5 collective-permute-start.25
  175.1 9.1 %collective-permute-done.22.refs_3_.refs_7_ = bf16[64,4224]{1,0:T(8,128)(2,1)S(1)} collective-permute-done((bf16[64,4224]{1,0:T(8,128)(2,1)S(1)}, bf16[64,4224]{1,0:T(8,128)(2,1)S(1)}, u32[]{:S(2)}, u32[]{:S(2)}) %collective-permute-start.22) | collective-permute-done | bytes 540704 | tf_op jit(solution)/shard_map/out_3_3/ppermute | solution.py:83
  184.2 4.9 %encode.7 = (f32[16,256]{1,0:T(8,128)S(1)}, s32[16,256]{1,0:T(8,128)S(1)}) custom-call(bf16[64,4224]{1,0:T(8,128)(2,1)S(1)} %get-tuple-element.130.refs_0_.refs_4_, bf16[64,4224]{1,0:T(8,128)(2,1)S(1)} %collective-permute-done.20.refs_1_.refs_5_, bf16[64,4224]{1,0:T(8,128)(2,1)S(1)} %collective-permute-done.19.refs_2_.refs_6_, ...), custom_call_target="tpu_custom_call" | custom-call | tf_op jit(solution)/shard_map/encode/pallas_call | solution.py:180
  189.2 1.6 collective-permute-start.23
  190.8 2.3 collective-permute-done.23.added_ref
  193.0 5.0 %decode.7 = (bf16[64,4096]{1,0:T(8,128)(2,1)S(1)}, bf16[64,4096]{1,0:T(8,128)(2,1)S(1)}, bf16[64,4096]{1,0:T(8,128)(2,1)S(1)}, bf16[64,4096]{1,0:T(8,128)(2,1)S(1)}) custom-call(f32[16,256]{1,0:T(8,128)S(1)} %get-tuple-element.133.chosen_ref, f32[16,256]{1,0:T(8,128)S(1)} %collective-permute-done.23.added_ref, s32[16,256]{1,0:T(8,128)S(1)} %get-tuple-element.134.picks_ref, ...), custom_call_target="tpu_custom_call" | custom-call | tf_op jit(solution)/shard_map/decode/pallas_call | solution.py:227
  198.1 4.7 %collective-permute-done.26.refs_3_ = bf16[64,4096]{1,0:T(8,128)(2,1)S(1)} collective-permute-done((bf16[64,4096]{1,0:T(8,128)(2,1)S(1)}, bf16[64,4096]{1,0:T(8,128)(2,1)S(1)}, u32[]{:S(2)}, u32[]{:S(2)}) %collective-permute-start.26) | collective-permute-done | bytes 524320 | tf_op jit(solution)/shard_map/back_2_3/ppermute | solution.py:83
  203.6 5.0 %collective-permute-start.29 = (bf16[256,2048]{1,0:T(8,128)(2,1)S(1)}, bf16[256,2048]{1,0:T(8,128)(2,1)S(1)}, u32[]{:S(2)}, u32[]{:S(2)}) collective-permute-start(bf16[256,2048]{1,0:T(8,128)(2,1)S(1)} %combine.5), channel_id=1, source_target_pairs={{0,4},{1,5},{2,6},{3,7},{12,8},{13,9},{14,10},{15,11},{16,20},{17,... | collective-permute-start | bytes 3145736 | tf_op jit(solution)/shard_map/sum_inward_two_0/ppermute | solution.py:83
  208.6 1.6 collective-permute-start.24
  211.6 11.8 %collective-permute-done.24.refs_2_ = bf16[64,4096]{1,0:T(8,128)(2,1)S(1)} collective-permute-done((bf16[64,4096]{1,0:T(8,128)(2,1)S(1)}, bf16[64,4096]{1,0:T(8,128)(2,1)S(1)}, u32[]{:S(2)}, u32[]{:S(2)}) %collective-permute-start.24) | collective-permute-done | bytes 524320 | tf_op jit(solution)/shard_map/back_3_2/ppermute | solution.py:83
  223.4 1.6 collective-permute-start.33
  225.8 6.3 %collective-permute-done.29 = bf16[256,2048]{1,0:T(8,128)(2,1)S(1)} collective-permute-done((bf16[256,2048]{1,0:T(8,128)(2,1)S(1)}, bf16[256,2048]{1,0:T(8,128)(2,1)S(1)}, u32[]{:S(2)}, u32[]{:S(2)}) %collective-permute-start.29) | collective-permute-done | bytes 1048608 | tf_op jit(solution)/shard_map/sum_inward_two_0/ppermute | solution.py:83
  232.5 1.0 collective-permute-done.28.refs_3_
  234.3 3.4 %collective-permute-start.35 = (bf16[256,2048]{1,0:T(8,128)(2,1)S(1)}, bf16[256,2048]{1,0:T(8,128)(2,1)S(1)}, u32[]{:S(2)}, u32[]{:S(2)}) collective-permute-start(bf16[256,2048]{1,0:T(8,128)(2,1)S(1)} %combine.8), channel_id=1, source_target_pairs={{0,4},{1,5},{2,6},{3,7},{12,8},{13,9},{14,10},{15,11},{16,20},{17,... | collective-permute-start | bytes 3145736 | tf_op jit(solution)/shard_map/sum_inward_far_0/ppermute | solution.py:83
  238.9 1.6 collective-permute-start.36
  241.3 4.1 %collective-permute-start.31 = (bf16[256,2048]{1,0:T(8,128)(2,1)S(1)}, bf16[256,2048]{1,0:T(8,128)(2,1)S(1)}, u32[]{:S(2)}, u32[]{:S(2)}) collective-permute-start(bf16[256,2048]{1,0:T(8,128)(2,1)S(1)} %combine.7), channel_id=1, source_target_pairs={{0,4},{1,5},{2,6},{3,7},{12,8},{13,9},{14,10},{15,11},{16,20},{17,... | collective-permute-start | bytes 3145736 | tf_op jit(solution)/shard_map/sum_inward_far_1/ppermute | solution.py:83
  245.4 9.2 %collective-permute-done.33 = bf16[256,2048]{1,0:T(8,128)(2,1)S(1)} collective-permute-done((bf16[256,2048]{1,0:T(8,128)(2,1)S(1)}, bf16[256,2048]{1,0:T(8,128)(2,1)S(1)}, u32[]{:S(2)}, u32[]{:S(2)}) %collective-permute-start.33) | collective-permute-done | bytes 1048608 | tf_op jit(solution)/shard_map/sum_inward_two_1/ppermute | solution.py:83
  256.3 20.7 %collective-permute-done.35 = bf16[256,2048]{1,0:T(8,128)(2,1)S(1)} collective-permute-done((bf16[256,2048]{1,0:T(8,128)(2,1)S(1)}, bf16[256,2048]{1,0:T(8,128)(2,1)S(1)}, u32[]{:S(2)}, u32[]{:S(2)}) %collective-permute-start.35) | collective-permute-done | bytes 1048608 | tf_op jit(solution)/shard_map/sum_inward_far_0/ppermute | solution.py:83
  277.4 1.3 collective-permute-start.38
  278.8 5.9 %collective-permute-done.32.refs_3_.refs_7_ = bf16[128,4096]{1,0:T(8,128)(2,1)S(1)} collective-permute-done((bf16[128,4096]{1,0:T(8,128)(2,1)S(1)}, bf16[128,4096]{1,0:T(8,128)(2,1)S(1)}, u32[]{:S(2)}, u32[]{:S(2)}) %collective-permute-start.32) | collective-permute-done | bytes 1048608 | tf_op jit(solution)/shard_map/back_near_3/ppermute | solution.py:83
  284.7 14.5 %collective-permute-done.31 = bf16[256,2048]{1,0:T(8,128)(2,1)S(1)} collective-permute-done((bf16[256,2048]{1,0:T(8,128)(2,1)S(1)}, bf16[256,2048]{1,0:T(8,128)(2,1)S(1)}, u32[]{:S(2)}, u32[]{:S(2)}) %collective-permute-start.31) | collective-permute-done | bytes 1048608 | tf_op jit(solution)/shard_map/sum_inward_far_1/ppermute | solution.py:83
  299.1 8.7 %collective-permute-done.38 = bf16[256,2048]{1,0:T(8,128)(2,1)S(1)} collective-permute-done((bf16[256,2048]{1,0:T(8,128)(2,1)S(1)}, bf16[256,2048]{1,0:T(8,128)(2,1)S(1)}, u32[]{:S(2)}, u32[]{:S(2)}) %collective-permute-start.38) | collective-permute-done | bytes 1048608 | tf_op jit(solution)/shard_map/sum_skip_far_0/ppermute | solution.py:83
  308.2 1.3 collective-permute-start.39
  309.9 2.4 combine.9
  312.3 22.3 %collective-permute-done.39 = bf16[256,2048]{1,0:T(8,128)(2,1)S(1)} collective-permute-done((bf16[256,2048]{1,0:T(8,128)(2,1)S(1)}, bf16[256,2048]{1,0:T(8,128)(2,1)S(1)}, u32[]{:S(2)}, u32[]{:S(2)}) %collective-permute-start.39) | collective-permute-done | bytes 1048608 | tf_op jit(solution)/shard_map/sum_skip_far_1/ppermute | solution.py:83
  334.6 1.8 add_convert_fusion
  (69 shorter events, 14.0 us)
Async XLA Ops:
  1.9 8.4 %copy-start.3 = (f32[4096]{0:T(1024)S(1)}, f32[4096]{0:T(1024)}, u32[]{:S(2)}) copy-start(f32[4096]{0:T(1024)} %param.8) | copy-start | bytes 49156
  3.7 10.8 %copy-start.4 = (f32[1,1024]{1,0:T(1,128)S(1)}, f32[1,1024]{1,0:T(1,128)}, u32[]{:S(2)}) copy-start(f32[1,1024]{1,0:T(1,128)} %param.13) | copy-start | bytes 12292
  3.7 48.5 %collective-permute-start.5 = (bf16[256,4224]{1,0:T(8,128)(2,1)S(1)}, bf16[256,4224]{1,0:T(8,128)(2,1)}, u32[]{:S(2)}, u32[]{:S(2)}) collective-permute-start(bf16[256,4224]{1,0:T(8,128)(2,1)S(1)} %pad_maximum_fusion.refs_0_), channel_id=1, source_target_pairs={{4,8},{5,9},{6,10},{7,11},{8,4},{9,5},{10,6},{11,7},{20,24},{21,25... | collective-permute-start | bytes 6488072 | tf_op jit(solution)/shard_map/rows_middle/ppermute | solution.py:83
  5.8 51.4 %collective-permute-start.4 = (bf16[256,4224]{1,0:T(8,128)(2,1)S(1)}, bf16[256,4224]{1,0:T(8,128)(2,1)}, u32[]{:S(2)}, u32[]{:S(2)}) collective-permute-start(bf16[256,4224]{1,0:T(8,128)(2,1)S(1)} %pad_maximum_fusion.refs_0_), channel_id=1, source_target_pairs={{0,4},{1,5},{2,6},{3,7},{4,0},{5,1},{6,2},{7,3},{8,12},{9,13},{10,... | collective-permute-start | bytes 6488072 | tf_op jit(solution)/shard_map/rows_ends/ppermute | solution.py:83
  12.6 2.1 collective-permute-start
  12.7 15.4 %collective-permute-start.1 = (bf16[64,4224]{1,0:T(8,128)(2,1)}, bf16[64,4224]{1,0:T(8,128)(2,1)}, u32[]{:S(2)}, u32[]{:S(2)}) collective-permute-start(bf16[64,4224]{1,0:T(8,128)(2,1)} %get-tuple-element.87), channel_id=1, source_target_pairs={{0,2},{1,3},{2,0},{3,1},{4,6},{5,7},{6,4},{7,5},{8,10},{9,11},{10,... | collective-permute-start | bytes 1622024 | tf_op jit(solution)/shard_map/out_0_2/ppermute | solution.py:83
  14.1 24.7 %collective-permute-start.2 = (bf16[64,4224]{1,0:T(8,128)(2,1)}, bf16[64,4224]{1,0:T(8,128)(2,1)}, u32[]{:S(2)}, u32[]{:S(2)}) collective-permute-start(bf16[64,4224]{1,0:T(8,128)(2,1)} %get-tuple-element.88), channel_id=1, source_target_pairs={{0,3},{1,2},{2,1},{3,0},{4,7},{5,6},{6,5},{7,4},{8,11},{9,10},{10,... | collective-permute-start | bytes 1622024 | tf_op jit(solution)/shard_map/out_0_3/ppermute | solution.py:83
  38.9 3.4 %copy-start = (bf16[1,4096,1024]{2,1,0:T(8,128)(2,1)S(1)}, bf16[1,4096,1024]{2,1,0:T(8,128)(2,1)}, u32[]{:S(2)}) copy-start(bf16[1,4096,1024]{2,1,0:T(8,128)(2,1)} %param.11) | copy-start | bytes 25165828
  42.2 21.7 %copy-start.2 = (bf16[1,1024,4096]{2,1,0:T(8,128)(2,1)S(1)}, bf16[1,1024,4096]{2,1,0:T(8,128)(2,1)}, u32[]{:S(2)}) copy-start(bf16[1,1024,4096]{2,1,0:T(8,128)(2,1)} %param.12) | copy-start | bytes 25165828
  48.5 3.8 %collective-permute-start.3 = (f32[16,256]{1,0:T(8,128)S(1)}, f32[16,256]{1,0:T(8,128)S(1)}, u32[]{:S(2)}, u32[]{:S(2)}) collective-permute-start(f32[16,256]{1,0:T(8,128)S(1)} %get-tuple-element.89.chosen_ref), channel_id=1, source_target_pairs={{0,16},{16,0},{1,17},{17,1},{2,18},{18,2},{3,19},{19,3},{4,20},{20... | collective-permute-start | bytes 49160 | tf_op jit(solution)/shard_map/sums_0/ppermute | solution.py:340
  57.2 50.0 %collective-permute-start.12 = (bf16[256,4224]{1,0:T(8,128)(2,1)}, bf16[256,4224]{1,0:T(8,128)(2,1)S(1)}, u32[]{:S(2)}, u32[]{:S(2)}) collective-permute-start(bf16[256,4224]{1,0:T(8,128)(2,1)} %collective-permute-done.5.refs_0_), channel_id=1, source_target_pairs={{4,0},{5,1},{6,2},{7,3},{8,12},{9,13},{10,14},{11,15},{20,16},{21,... | collective-permute-start | bytes 6488072 | tf_op jit(solution)/shard_map/rows_outward_two/ppermute | solution.py:83
  58.5 48.7 %collective-permute-start.11 = (bf16[256,4224]{1,0:T(8,128)(2,1)}, bf16[256,4224]{1,0:T(8,128)(2,1)S(1)}, u32[]{:S(2)}, u32[]{:S(2)}) collective-permute-start(bf16[256,4224]{1,0:T(8,128)(2,1)} %collective-permute-done.4.refs_0_), channel_id=1, source_target_pairs={{4,8},{5,9},{6,10},{7,11},{8,4},{9,5},{10,6},{11,7},{20,24},{21,25... | collective-permute-start | bytes 6488072 | tf_op jit(solution)/shard_map/rows_middle_far/ppermute | solution.py:83
  62.0 7.0 %collective-permute-start.6 = (bf16[64,4224]{1,0:T(8,128)(2,1)S(1)}, bf16[64,4224]{1,0:T(8,128)(2,1)S(1)}, u32[]{:S(2)}, u32[]{:S(2)}) collective-permute-start(bf16[64,4224]{1,0:T(8,128)(2,1)S(1)} %get-tuple-element.96), channel_id=1, source_target_pairs={{0,1},{1,0},{2,3},{3,2},{4,5},{5,4},{6,7},{7,6},{8,9},{9,8},{10,11... | collective-permute-start | bytes 1622024 | tf_op jit(solution)/shard_map/out_1_1/ppermute | solution.py:83
  62.1 15.1 %collective-permute-start.7 = (bf16[64,4224]{1,0:T(8,128)(2,1)S(1)}, bf16[64,4224]{1,0:T(8,128)(2,1)S(1)}, u32[]{:S(2)}, u32[]{:S(2)}) collective-permute-start(bf16[64,4224]{1,0:T(8,128)(2,1)S(1)} %get-tuple-element.97), channel_id=1, source_target_pairs={{0,2},{1,3},{2,0},{3,1},{4,6},{5,7},{6,4},{7,5},{8,10},{9,11},{10,... | collective-permute-start | bytes 1622024 | tf_op jit(solution)/shard_map/out_1_2/ppermute | solution.py:83
  63.6 24.3 %collective-permute-start.8 = (bf16[64,4224]{1,0:T(8,128)(2,1)S(1)}, bf16[64,4224]{1,0:T(8,128)(2,1)S(1)}, u32[]{:S(2)}, u32[]{:S(2)}) collective-permute-start(bf16[64,4224]{1,0:T(8,128)(2,1)S(1)} %get-tuple-element.98), channel_id=1, source_target_pairs={{0,3},{1,2},{2,1},{3,0},{4,7},{5,6},{6,5},{7,4},{8,11},{9,10},{10,... | collective-permute-start | bytes 1622024 | tf_op jit(solution)/shard_map/out_1_3/ppermute | solution.py:83
  63.9 24.0 %copy-start.1 = (bf16[1,4096,1024]{2,1,0:T(8,128)(2,1)S(1)}, bf16[1,4096,1024]{2,1,0:T(8,128)(2,1)}, u32[]{:S(2)}) copy-start(bf16[1,4096,1024]{2,1,0:T(8,128)(2,1)} %param.11) | copy-start | bytes 25165828
  92.9 3.8 %collective-permute-start.9 = (f32[16,256]{1,0:T(8,128)S(1)}, f32[16,256]{1,0:T(8,128)S(1)}, u32[]{:S(2)}, u32[]{:S(2)}) collective-permute-start(f32[16,256]{1,0:T(8,128)S(1)} %get-tuple-element.105.chosen_ref), channel_id=1, source_target_pairs={{0,16},{16,0},{1,17},{17,1},{2,18},{18,2},{3,19},{19,3},{4,20},{20... | collective-permute-start | bytes 49160 | tf_op jit(solution)/shard_map/sums_1/ppermute | solution.py:340
  107.2 50.0 %collective-permute-start.13 = (bf16[256,4224]{1,0:T(8,128)(2,1)S(1)}, bf16[256,4224]{1,0:T(8,128)(2,1)S(1)}, u32[]{:S(2)}, u32[]{:S(2)}) collective-permute-start(bf16[256,4224]{1,0:T(8,128)(2,1)S(1)} %collective-permute-done.11.refs_0_), channel_id=1, source_target_pairs={{4,0},{5,1},{6,2},{7,3},{8,12},{9,13},{10,14},{11,15},{20,16},{21,... | collective-permute-start | bytes 6488072 | tf_op jit(solution)/shard_map/rows_outward_far/ppermute | solution.py:83
  111.4 7.9 %collective-permute-start.14 = (bf16[64,4224]{1,0:T(8,128)(2,1)S(1)}, bf16[64,4224]{1,0:T(8,128)(2,1)S(1)}, u32[]{:S(2)}, u32[]{:S(2)}) collective-permute-start(bf16[64,4224]{1,0:T(8,128)(2,1)S(1)} %get-tuple-element.111), channel_id=1, source_target_pairs={{0,1},{1,0},{2,3},{3,2},{4,5},{5,4},{6,7},{7,6},{8,9},{9,8},{10,11... | collective-permute-start | bytes 1622024 | tf_op jit(solution)/shard_map/out_2_1/ppermute | solution.py:83
  111.5 15.1 %collective-permute-start.15 = (bf16[64,4224]{1,0:T(8,128)(2,1)S(1)}, bf16[64,4224]{1,0:T(8,128)(2,1)S(1)}, u32[]{:S(2)}, u32[]{:S(2)}) collective-permute-start(bf16[64,4224]{1,0:T(8,128)(2,1)S(1)} %get-tuple-element.112), channel_id=1, source_target_pairs={{0,2},{1,3},{2,0},{3,1},{4,6},{5,7},{6,4},{7,5},{8,10},{9,11},{10,... | collective-permute-start | bytes 1622024 | tf_op jit(solution)/shard_map/out_2_2/ppermute | solution.py:83
  113.1 24.3 %collective-permute-start.16 = (bf16[64,4224]{1,0:T(8,128)(2,1)S(1)}, bf16[64,4224]{1,0:T(8,128)(2,1)S(1)}, u32[]{:S(2)}, u32[]{:S(2)}) collective-permute-start(bf16[64,4224]{1,0:T(8,128)(2,1)S(1)} %get-tuple-element.113), channel_id=1, source_target_pairs={{0,3},{1,2},{2,1},{3,0},{4,7},{5,6},{6,5},{7,4},{8,11},{9,10},{10,... | collective-permute-start | bytes 1622024 | tf_op jit(solution)/shard_map/out_2_3/ppermute | solution.py:83
  113.4 61.8 %collective-permute-start.10 = (bf16[256,4096]{1,0:T(8,128)(2,1)S(1)}, bf16[256,4096]{1,0:T(8,128)(2,1)S(1)}, u32[]{:S(2)}, u32[]{:S(2)}) collective-permute-start(bf16[256,4096]{1,0:T(8,128)(2,1)S(1)} %decode.5), channel_id=1, source_target_pairs={{0,4},{1,5},{2,6},{3,7},{12,8},{13,9},{14,10},{15,11},{16,20},{17,... | collective-permute-start | bytes 6291464 | tf_op jit(solution)/shard_map/parts_inward/ppermute | solution.py:83
  142.3 3.8 %collective-permute-start.17 = (f32[16,256]{1,0:T(8,128)S(1)}, f32[16,256]{1,0:T(8,128)S(1)}, u32[]{:S(2)}, u32[]{:S(2)}) collective-permute-start(f32[16,256]{1,0:T(8,128)S(1)} %get-tuple-element.114.chosen_ref), channel_id=1, source_target_pairs={{0,16},{16,0},{1,17},{17,1},{2,18},{18,2},{3,19},{19,3},{4,20},{20... | collective-permute-start | bytes 49160 | tf_op jit(solution)/shard_map/sums_2/ppermute | solution.py:340
  151.1 6.1 %collective-permute-start.18 = (bf16[64,4096]{1,0:T(8,128)(2,1)S(1)}, bf16[64,4096]{1,0:T(8,128)(2,1)S(1)}, u32[]{:S(2)}, u32[]{:S(2)}) collective-permute-start(bf16[64,4096]{1,0:T(8,128)(2,1)S(1)} %get-tuple-element.117), channel_id=1, source_target_pairs={{0,1},{1,0},{2,3},{3,2},{4,5},{5,4},{6,7},{7,6},{8,9},{9,8},{10,11... | collective-permute-start | bytes 1572872 | tf_op jit(solution)/shard_map/back_2_1/ppermute | solution.py:83
  158.4 15.3 %collective-permute-start.19 = (bf16[64,4224]{1,0:T(8,128)(2,1)S(1)}, bf16[64,4224]{1,0:T(8,128)(2,1)S(1)}, u32[]{:S(2)}, u32[]{:S(2)}) collective-permute-start(bf16[64,4224]{1,0:T(8,128)(2,1)S(1)} %get-tuple-element.123), channel_id=1, source_target_pairs={{0,2},{1,3},{2,0},{3,1},{4,6},{5,7},{6,4},{7,5},{8,10},{9,11},{10,... | collective-permute-start | bytes 1622024 | tf_op jit(solution)/shard_map/out_3_2/ppermute | solution.py:83
  159.9 15.2 %collective-permute-start.20 = (bf16[64,4224]{1,0:T(8,128)(2,1)S(1)}, bf16[64,4224]{1,0:T(8,128)(2,1)S(1)}, u32[]{:S(2)}, u32[]{:S(2)}) collective-permute-start(bf16[64,4224]{1,0:T(8,128)(2,1)S(1)} %get-tuple-element.124), channel_id=1, source_target_pairs={{0,1},{1,0},{2,3},{3,2},{4,5},{5,4},{6,7},{7,6},{8,9},{9,8},{10,11... | collective-permute-start | bytes 1622024 | tf_op jit(solution)/shard_map/out_3_1/ppermute | solution.py:83
  159.9 65.1 %collective-permute-start.21 = (bf16[256,4096]{1,0:T(8,128)(2,1)S(1)}, bf16[256,4096]{1,0:T(8,128)(2,1)S(1)}, u32[]{:S(2)}, u32[]{:S(2)}) collective-permute-start(bf16[256,4096]{1,0:T(8,128)(2,1)S(1)} %decode.5), channel_id=1, source_target_pairs={{4,0},{5,1},{6,2},{7,3},{8,12},{9,13},{10,14},{11,15},{20,16},{21,... | collective-permute-start | bytes 6291464 | tf_op jit(solution)/shard_map/parts_outward/ppermute | solution.py:83
  161.2 23.0 %collective-permute-start.22 = (bf16[64,4224]{1,0:T(8,128)(2,1)S(1)}, bf16[64,4224]{1,0:T(8,128)(2,1)S(1)}, u32[]{:S(2)}, u32[]{:S(2)}) collective-permute-start(bf16[64,4224]{1,0:T(8,128)(2,1)S(1)} %get-tuple-element.131), channel_id=1, source_target_pairs={{0,3},{1,2},{2,1},{3,0},{4,7},{5,6},{6,5},{7,4},{8,11},{9,10},{10,... | collective-permute-start | bytes 1622024 | tf_op jit(solution)/shard_map/out_3_3/ppermute | solution.py:83
  173.6 24.4 %collective-permute-start.25 = (bf16[64,4096]{1,0:T(8,128)(2,1)S(1)}, bf16[64,4096]{1,0:T(8,128)(2,1)S(1)}, u32[]{:S(2)}, u32[]{:S(2)}) collective-permute-start(bf16[64,4096]{1,0:T(8,128)(2,1)S(1)} %get-tuple-element.118), channel_id=1, source_target_pairs={{0,2},{1,3},{2,0},{3,1},{4,6},{5,7},{6,4},{7,5},{8,10},{9,11},{10,... | collective-permute-start | bytes 1572872 | tf_op jit(solution)/shard_map/back_2_2/ppermute | solution.py:83
  175.1 27.7 %collective-permute-start.26 = (bf16[64,4096]{1,0:T(8,128)(2,1)S(1)}, bf16[64,4096]{1,0:T(8,128)(2,1)S(1)}, u32[]{:S(2)}, u32[]{:S(2)}) collective-permute-start(bf16[64,4096]{1,0:T(8,128)(2,1)S(1)} %get-tuple-element.119), channel_id=1, source_target_pairs={{0,3},{1,2},{2,1},{3,0},{4,7},{5,6},{6,5},{7,4},{8,11},{9,10},{10,... | collective-permute-start | bytes 1572872 | tf_op jit(solution)/shard_map/back_2_3/ppermute | solution.py:83
  189.2 3.8 %collective-permute-start.23 = (f32[16,256]{1,0:T(8,128)S(1)}, f32[16,256]{1,0:T(8,128)S(1)}, u32[]{:S(2)}, u32[]{:S(2)}) collective-permute-start(f32[16,256]{1,0:T(8,128)S(1)} %get-tuple-element.133.chosen_ref), channel_id=1, source_target_pairs={{0,16},{16,0},{1,17},{17,1},{2,18},{18,2},{3,19},{19,3},{4,20},{20... | collective-permute-start | bytes 49160 | tf_op jit(solution)/shard_map/sums_3/ppermute | solution.py:340
  203.6 28.5 %collective-permute-start.29 = (bf16[256,2048]{1,0:T(8,128)(2,1)S(1)}, bf16[256,2048]{1,0:T(8,128)(2,1)S(1)}, u32[]{:S(2)}, u32[]{:S(2)}) collective-permute-start(bf16[256,2048]{1,0:T(8,128)(2,1)S(1)} %combine.5), channel_id=1, source_target_pairs={{0,4},{1,5},{2,6},{3,7},{12,8},{13,9},{14,10},{15,11},{16,20},{17,... | collective-permute-start | bytes 3145736 | tf_op jit(solution)/shard_map/sum_inward_two_0/ppermute | solution.py:83
  208.6 14.8 %collective-permute-start.24 = (bf16[64,4096]{1,0:T(8,128)(2,1)S(1)}, bf16[64,4096]{1,0:T(8,128)(2,1)S(1)}, u32[]{:S(2)}, u32[]{:S(2)}) collective-permute-start(bf16[64,4096]{1,0:T(8,128)(2,1)S(1)} %get-tuple-element.135), channel_id=1, source_target_pairs={{0,2},{1,3},{2,0},{3,1},{4,6},{5,7},{6,4},{7,5},{8,10},{9,11},{10,... | collective-permute-start | bytes 1572872 | tf_op jit(solution)/shard_map/back_3_2/ppermute | solution.py:83
  210.1 22.3 %collective-permute-start.27 = (bf16[64,4096]{1,0:T(8,128)(2,1)S(1)}, bf16[64,4096]{1,0:T(8,128)(2,1)S(1)}, u32[]{:S(2)}, u32[]{:S(2)}) collective-permute-start(bf16[64,4096]{1,0:T(8,128)(2,1)S(1)} %get-tuple-element.138), channel_id=1, source_target_pairs={{0,1},{1,0},{2,3},{3,2},{4,5},{5,4},{6,7},{7,6},{8,9},{9,8},{10,11... | collective-permute-start | bytes 1572872 | tf_op jit(solution)/shard_map/back_3_1/ppermute | solution.py:83
  210.2 23.3 %collective-permute-start.28 = (bf16[64,4096]{1,0:T(8,128)(2,1)S(1)}, bf16[64,4096]{1,0:T(8,128)(2,1)S(1)}, u32[]{:S(2)}, u32[]{:S(2)}) collective-permute-start(bf16[64,4096]{1,0:T(8,128)(2,1)S(1)} %get-tuple-element.139), channel_id=1, source_target_pairs={{0,3},{1,2},{2,1},{3,0},{4,7},{5,6},{6,5},{7,4},{8,11},{9,10},{10,... | collective-permute-start | bytes 1572872 | tf_op jit(solution)/shard_map/back_3_3/ppermute | solution.py:83
  223.4 31.1 %collective-permute-start.33 = (bf16[256,2048]{1,0:T(8,128)(2,1)S(1)}, bf16[256,2048]{1,0:T(8,128)(2,1)S(1)}, u32[]{:S(2)}, u32[]{:S(2)}) collective-permute-start(bf16[256,2048]{1,0:T(8,128)(2,1)S(1)} %combine.6), channel_id=1, source_target_pairs={{0,4},{1,5},{2,6},{3,7},{12,8},{13,9},{14,10},{15,11},{16,20},{17,... | collective-permute-start | bytes 3145736 | tf_op jit(solution)/shard_map/sum_inward_two_1/ppermute | solution.py:83
  234.3 42.7 %collective-permute-start.35 = (bf16[256,2048]{1,0:T(8,128)(2,1)S(1)}, bf16[256,2048]{1,0:T(8,128)(2,1)S(1)}, u32[]{:S(2)}, u32[]{:S(2)}) collective-permute-start(bf16[256,2048]{1,0:T(8,128)(2,1)S(1)} %combine.8), channel_id=1, source_target_pairs={{0,4},{1,5},{2,6},{3,7},{12,8},{13,9},{14,10},{15,11},{16,20},{17,... | collective-permute-start | bytes 3145736 | tf_op jit(solution)/shard_map/sum_inward_far_0/ppermute | solution.py:83
  237.7 17.9 %collective-permute-start.37 = (bf16[256,2048]{1,0:T(8,128)(2,1)S(1)}, bf16[256,2048]{1,0:T(8,128)(2,1)S(1)}, u32[]{:S(2)}, u32[]{:S(2)}) collective-permute-start(bf16[256,2048]{1,0:T(8,128)(2,1)S(1)} %add_convert_fusion.3), channel_id=1, source_target_pairs={{4,8},{5,9},{6,10},{7,11},{8,4},{9,5},{10,6},{11,7},{20,24},{21,25... | collective-permute-start | bytes 3145736 | tf_op jit(solution)/shard_map/sum_middle_two_0/ppermute | solution.py:83
  238.9 38.1 %collective-permute-start.36 = (bf16[128,4096]{1,0:T(8,128)(2,1)S(1)}, bf16[128,4096]{1,0:T(8,128)(2,1)S(1)}, u32[]{:S(2)}, u32[]{:S(2)}) collective-permute-start(bf16[128,4096]{1,0:T(8,128)(2,1)S(1)} %pad_maximum_fusion.2), channel_id=1, source_target_pairs={{0,2},{1,3},{2,0},{3,1},{4,6},{5,7},{6,4},{7,5},{8,10},{9,11},{10,... | collective-permute-start | bytes 3145736 | tf_op jit(solution)/shard_map/back_near_2/ppermute | solution.py:83
  241.3 57.9 %collective-permute-start.31 = (bf16[256,2048]{1,0:T(8,128)(2,1)S(1)}, bf16[256,2048]{1,0:T(8,128)(2,1)S(1)}, u32[]{:S(2)}, u32[]{:S(2)}) collective-permute-start(bf16[256,2048]{1,0:T(8,128)(2,1)S(1)} %combine.7), channel_id=1, source_target_pairs={{0,4},{1,5},{2,6},{3,7},{12,8},{13,9},{14,10},{15,11},{16,20},{17,... | collective-permute-start | bytes 3145736 | tf_op jit(solution)/shard_map/sum_inward_far_1/ppermute | solution.py:83
  254.9 23.9 %collective-permute-start.34 = (bf16[256,2048]{1,0:T(8,128)(2,1)S(1)}, bf16[256,2048]{1,0:T(8,128)(2,1)S(1)}, u32[]{:S(2)}, u32[]{:S(2)}) collective-permute-start(bf16[256,2048]{1,0:T(8,128)(2,1)S(1)} %add_convert_fusion.4), channel_id=1, source_target_pairs={{4,8},{5,9},{6,10},{7,11},{8,4},{9,5},{10,6},{11,7},{20,24},{21,25... | collective-permute-start | bytes 3145736 | tf_op jit(solution)/shard_map/sum_middle_two_1/ppermute | solution.py:83
  255.7 29.0 %collective-permute-start.32 = (bf16[128,4096]{1,0:T(8,128)(2,1)S(1)}, bf16[128,4096]{1,0:T(8,128)(2,1)S(1)}, u32[]{:S(2)}, u32[]{:S(2)}) collective-permute-start(bf16[128,4096]{1,0:T(8,128)(2,1)S(1)} %pad_maximum_fusion.3), channel_id=1, source_target_pairs={{0,3},{1,2},{2,1},{3,0},{4,7},{5,6},{6,5},{7,4},{8,11},{9,10},{10,... | collective-permute-start | bytes 3145736 | tf_op jit(solution)/shard_map/back_near_3/ppermute | solution.py:83
  277.4 30.4 %collective-permute-start.38 = (bf16[256,2048]{1,0:T(8,128)(2,1)S(1)}, bf16[256,2048]{1,0:T(8,128)(2,1)S(1)}, u32[]{:S(2)}, u32[]{:S(2)}) collective-permute-start(bf16[256,2048]{1,0:T(8,128)(2,1)S(1)} %add_convert_fusion.2), channel_id=1, source_target_pairs={{4,12},{5,13},{6,14},{7,15},{8,0},{9,1},{10,2},{11,3},{20,28},{21,... | collective-permute-start | bytes 3145736 | tf_op jit(solution)/shard_map/sum_skip_far_0/ppermute | solution.py:83
  278.7 31.2 %collective-permute-start.30 = (bf16[128,4096]{1,0:T(8,128)(2,1)S(1)}, bf16[128,4096]{1,0:T(8,128)(2,1)S(1)}, u32[]{:S(2)}, u32[]{:S(2)}) collective-permute-start(bf16[128,4096]{1,0:T(8,128)(2,1)S(1)} %pad_maximum_fusion.1), channel_id=1, source_target_pairs={{0,1},{1,0},{2,3},{3,2},{4,5},{5,4},{6,7},{7,6},{8,9},{9,8},{10,11... | collective-permute-start | bytes 3145736 | tf_op jit(solution)/shard_map/back_near_1/ppermute | solution.py:83
  308.2 26.4 %collective-permute-start.39 = (bf16[256,2048]{1,0:T(8,128)(2,1)S(1)}, bf16[256,2048]{1,0:T(8,128)(2,1)S(1)}, u32[]{:S(2)}, u32[]{:S(2)}) collective-permute-start(bf16[256,2048]{1,0:T(8,128)(2,1)S(1)} %add_convert_fusion.1), channel_id=1, source_target_pairs={{4,12},{5,13},{6,14},{7,15},{8,0},{9,1},{10,2},{11,3},{20,28},{21,... | collective-permute-start | bytes 3145736 | tf_op jit(solution)/shard_map/sum_skip_far_1/ppermute | solution.py:83

commit v5 on v4

--- a/solution.py
+++ b/solution.py
@@ -10,7 +10,7 @@
 
 BACK_CHUNKS = (1, 1, 1, 1)
 TWO_SHARES = (1, 1)
-FAR_SHARES = (1, 1)
+FAR_SHARES = (3, 5)
 INNER = 4
 OUTER = 4
 EXTRA = 128

time: 337 us -> 335 us (level)
  no operation moved by 1% of the time
where the time goes in v5:
time: 335 us
  waiting for transfers between devices  209 us (62%)
  starting transfers between devices  56.9 us (17%)
  Pallas kernels  56.5 us (17%)
  other arithmetic  6.91 us (2%)
  local copies, waits for them, and re-layouts  4.58 us (1%)
    ppermute x36, waiting for transfers between devices, move(): return lax.ppermute(value, 'blocks', pairs)  200 us
    ppermute x36, starting transfers between devices, move(): return lax.ppermute(value, 'blocks', pairs)  50.6 us
    pallas_call x4, Pallas kernels, encode(): call(kernel, 'encode', (width // BLOCK,), [pl.BlockSpec((cap, BLOCK), lam...  21.1 us
    pallas_call x4, Pallas kernels, decode(): call(decode_kernel, 'decode', (width // BLOCK,), [pl.BlockSpec((picked, s...  20.1 us
    ppermute x4, waiting for transfers between devices, encoded(): added = lax.ppermute(chosen, 'dp', [(0, 1), (1, 0)])  8.91 us
    pallas_call x4, Pallas kernels, dispatch(): call(functools.partial(dispatch_kernel, cap, len(values)), 'dispatch', ()...  8.85 us
  transfers between devices with their start and end apart: 40, of which 26 were waited for; matrix products, arithmetic and copies ran while one was open for 1% of the time, Pallas kernels for 17%

profile of v5, /device:TPU:0, one launch (start us, length us, event | category | flops | bytes accessed | tf_op | source)
XLA Modules:
  0.0 334.8 jit_solution(10585723317127541568)
XLA Ops:
  2.0 1.8 pad_maximum_fusion.refs_0_
  3.7 2.0 collective-permute-start.5
  5.8 4.5 %collective-permute-start.4 = (bf16[256,4224]{1,0:T(8,128)(2,1)S(1)}, bf16[256,4224]{1,0:T(8,128)(2,1)}, u32[]{:S(2)}, u32[]{:S(2)}) collective-permute-start(bf16[256,4224]{1,0:T(8,128)(2,1)S(1)} %pad_maximum_fusion.refs_0_), channel_id=1, source_target_pairs={{0,4},{1,5},{2,6},{3,7},{4,0},{5,1},{6,2},{7,3},{8,12},{9,13},{10,... | collective-permute-start | bytes 6488072 | tf_op jit(solution)/shard_map/rows_ends/ppermute | solution.py:83
  10.4 2.2 dispatch.4
  12.7 1.5 collective-permute-start.1
  14.8 13.2 %collective-permute-done.1.refs_2_.refs_6_ = bf16[64,4224]{1,0:T(8,128)(2,1)} collective-permute-done((bf16[64,4224]{1,0:T(8,128)(2,1)}, bf16[64,4224]{1,0:T(8,128)(2,1)}, u32[]{:S(2)}, u32[]{:S(2)}) %collective-permute-start.1) | collective-permute-done | bytes 540704 | tf_op jit(solution)/shard_map/out_0_2/ppermute | solution.py:83
  28.0 10.8 %collective-permute-done.2.refs_3_.refs_7_ = bf16[64,4224]{1,0:T(8,128)(2,1)} collective-permute-done((bf16[64,4224]{1,0:T(8,128)(2,1)}, bf16[64,4224]{1,0:T(8,128)(2,1)}, u32[]{:S(2)}, u32[]{:S(2)}) %collective-permute-start.2) | collective-permute-done | bytes 540704 | tf_op jit(solution)/shard_map/out_0_3/ppermute | solution.py:83
  38.9 3.4 %copy-done = bf16[1,4096,1024]{2,1,0:T(8,128)(2,1)S(1)} copy-done((bf16[1,4096,1024]{2,1,0:T(8,128)(2,1)S(1)}, bf16[1,4096,1024]{2,1,0:T(8,128)(2,1)}, u32[]{:S(2)}) %copy-start) | copy-done | bytes 8388632
  42.2 6.2 %encode.4 = (f32[16,256]{1,0:T(8,128)S(1)}, s32[16,256]{1,0:T(8,128)S(1)}) custom-call(bf16[64,4224]{1,0:T(8,128)(2,1)S(1)} %get-tuple-element.85.refs_0_.refs_4_, bf16[64,4224]{1,0:T(8,128)(2,1)S(1)} %collective-permute-done.refs_1_.refs_5_, bf16[64,4224]{1,0:T(8,128)(2,1)} %collective-permute-done.1.refs_2_.refs_6_, ...), custom_call_target="tpu_custom_call" | custom-call | tf_op jit(solution)/shard_map/encode/pallas_call | solution.py:180
  48.5 1.6 collective-permute-start.3
  50.0 2.2 collective-permute-done.3.added_ref
  52.3 4.9 %collective-permute-done.4.refs_0_ = bf16[256,4224]{1,0:T(8,128)(2,1)} collective-permute-done((bf16[256,4224]{1,0:T(8,128)(2,1)S(1)}, bf16[256,4224]{1,0:T(8,128)(2,1)}, u32[]{:S(2)}, u32[]{:S(2)}) %collective-permute-start.4) | collective-permute-done | bytes 2162720 | tf_op jit(solution)/shard_map/rows_ends/ppermute | solution.py:83
  57.2 1.3 collective-permute-start.12
  59.3 2.7 dispatch.5
  62.1 1.6 collective-permute-start.7
  64.0 5.0 %decode.4 = (bf16[64,4096]{1,0:T(8,128)(2,1)S(1)}, bf16[64,4096]{1,0:T(8,128)(2,1)S(1)}, bf16[64,4096]{1,0:T(8,128)(2,1)S(1)}, bf16[64,4096]{1,0:T(8,128)(2,1)S(1)}) custom-call(f32[16,256]{1,0:T(8,128)S(1)} %get-tuple-element.89.chosen_ref, f32[16,256]{1,0:T(8,128)S(1)} %collective-permute-done.3.added_ref, s32[16,256]{1,0:T(8,128)S(1)} %get-tuple-element.91.picks_ref, ...), custom_call_target="tpu_custom_call" | custom-call | tf_op jit(solution)/shard_map/decode/pallas_call | solution.py:227
  69.0 8.2 %collective-permute-done.7.refs_2_.refs_6_ = bf16[64,4224]{1,0:T(8,128)(2,1)S(1)} collective-permute-done((bf16[64,4224]{1,0:T(8,128)(2,1)S(1)}, bf16[64,4224]{1,0:T(8,128)(2,1)S(1)}, u32[]{:S(2)}, u32[]{:S(2)}) %collective-permute-start.7) | collective-permute-done | bytes 540704 | tf_op jit(solution)/shard_map/out_1_2/ppermute | solution.py:83
  77.2 10.7 %collective-permute-done.8.refs_3_.refs_7_ = bf16[64,4224]{1,0:T(8,128)(2,1)S(1)} collective-permute-done((bf16[64,4224]{1,0:T(8,128)(2,1)S(1)}, bf16[64,4224]{1,0:T(8,128)(2,1)S(1)}, u32[]{:S(2)}, u32[]{:S(2)}) %collective-permute-start.8) | collective-permute-done | bytes 540704 | tf_op jit(solution)/shard_map/out_1_3/ppermute | solution.py:83
  87.9 5.0 %encode.5 = (f32[16,256]{1,0:T(8,128)S(1)}, s32[16,256]{1,0:T(8,128)S(1)}) custom-call(bf16[64,4224]{1,0:T(8,128)(2,1)S(1)} %get-tuple-element.101.refs_0_.refs_4_, bf16[64,4224]{1,0:T(8,128)(2,1)S(1)} %collective-permute-done.6.refs_1_.refs_5_, bf16[64,4224]{1,0:T(8,128)(2,1)S(1)} %collective-permute-done.7.refs_2_.refs_6_, ...), custom_call_target="tpu_custom_call" | custom-call | tf_op jit(solution)/shard_map/encode/pallas_call | solution.py:180
  92.9 1.6 collective-permute-start.9
  94.5 2.2 collective-permute-done.9.added_ref
  96.7 5.0 %decode.5 = bf16[256,4096]{1,0:T(8,128)(2,1)S(1)} custom-call(f32[16,256]{1,0:T(8,128)S(1)} %get-tuple-element.105.chosen_ref, f32[16,256]{1,0:T(8,128)S(1)} %collective-permute-done.9.added_ref, s32[16,256]{1,0:T(8,128)S(1)} %get-tuple-element.106.picks_ref, bf16[1024,4096]{1,0:T(8,128)(2,1)S(1)} %bitcast.9), custom_call_target="tpu_custom_call" | custom-call | tf_op jit(solution)/shard_map/decode/pallas_call | solution.py:227
  101.7 5.5 %collective-permute-done.12.refs_1_ = bf16[256,4224]{1,0:T(8,128)(2,1)S(1)} collective-permute-done((bf16[256,4224]{1,0:T(8,128)(2,1)}, bf16[256,4224]{1,0:T(8,128)(2,1)S(1)}, u32[]{:S(2)}, u32[]{:S(2)}) %collective-permute-start.12) | collective-permute-done | bytes 2162720 | tf_op jit(solution)/shard_map/rows_outward_two/ppermute | solution.py:83
  107.2 1.5 collective-permute-start.13
  108.7 2.8 dispatch.6
  111.5 1.6 collective-permute-start.15
  113.4 6.0 %collective-permute-start.10 = (bf16[256,4096]{1,0:T(8,128)(2,1)S(1)}, bf16[256,4096]{1,0:T(8,128)(2,1)S(1)}, u32[]{:S(2)}, u32[]{:S(2)}) collective-permute-start(bf16[256,4096]{1,0:T(8,128)(2,1)S(1)} %decode.5), channel_id=1, source_target_pairs={{0,4},{1,5},{2,6},{3,7},{12,8},{13,9},{14,10},{15,11},{16,20},{17,... | collective-permute-start | bytes 6291464 | tf_op jit(solution)/shard_map/parts_inward/ppermute | solution.py:83
  119.3 7.3 %collective-permute-done.15.refs_2_.refs_6_ = bf16[64,4224]{1,0:T(8,128)(2,1)S(1)} collective-permute-done((bf16[64,4224]{1,0:T(8,128)(2,1)S(1)}, bf16[64,4224]{1,0:T(8,128)(2,1)S(1)}, u32[]{:S(2)}, u32[]{:S(2)}) %collective-permute-start.15) | collective-permute-done | bytes 540704 | tf_op jit(solution)/shard_map/out_2_2/ppermute | solution.py:83
  126.6 10.7 %collective-permute-done.16.refs_3_.refs_7_ = bf16[64,4224]{1,0:T(8,128)(2,1)S(1)} collective-permute-done((bf16[64,4224]{1,0:T(8,128)(2,1)S(1)}, bf16[64,4224]{1,0:T(8,128)(2,1)S(1)}, u32[]{:S(2)}, u32[]{:S(2)}) %collective-permute-start.16) | collective-permute-done | bytes 540704 | tf_op jit(solution)/shard_map/out_2_3/ppermute | solution.py:83
  137.3 5.0 %encode.6 = (f32[16,256]{1,0:T(8,128)S(1)}, s32[16,256]{1,0:T(8,128)S(1)}) custom-call(bf16[64,4224]{1,0:T(8,128)(2,1)S(1)} %get-tuple-element.110.refs_0_.refs_4_, bf16[64,4224]{1,0:T(8,128)(2,1)S(1)} %collective-permute-done.14.refs_1_.refs_5_, bf16[64,4224]{1,0:T(8,128)(2,1)S(1)} %collective-permute-done.15.refs_2_.refs_6_, ...), custom_call_target="tpu_custom_call" | custom-call | tf_op jit(solution)/shard_map/encode/pallas_call | solution.py:180
  142.3 1.6 collective-permute-start.17
  143.9 2.2 collective-permute-done.17.added_ref
  146.1 5.0 %decode.6 = (bf16[64,4096]{1,0:T(8,128)(2,1)S(1)}, bf16[64,4096]{1,0:T(8,128)(2,1)S(1)}, bf16[64,4096]{1,0:T(8,128)(2,1)S(1)}, bf16[64,4096]{1,0:T(8,128)(2,1)S(1)}) custom-call(f32[16,256]{1,0:T(8,128)S(1)} %get-tuple-element.114.chosen_ref, f32[16,256]{1,0:T(8,128)S(1)} %collective-permute-done.17.added_ref, s32[16,256]{1,0:T(8,128)S(1)} %get-tuple-element.115.picks_ref, ...), custom_call_target="tpu_custom_call" | custom-call | tf_op jit(solution)/shard_map/decode/pallas_call | solution.py:227
  151.2 6.0 %collective-permute-done.13.refs_1_ = bf16[256,4224]{1,0:T(8,128)(2,1)S(1)} collective-permute-done((bf16[256,4224]{1,0:T(8,128)(2,1)S(1)}, bf16[256,4224]{1,0:T(8,128)(2,1)S(1)}, u32[]{:S(2)}, u32[]{:S(2)}) %collective-permute-start.13) | collective-permute-done | bytes 2162720 | tf_op jit(solution)/shard_map/rows_outward_far/ppermute | solution.py:83
  157.2 1.1 dispatch.7
  158.4 1.6 collective-permute-start.19
  159.9 1.3 collective-permute-start.21
  161.9 11.7 %collective-permute-done.19.refs_2_.refs_6_ = bf16[64,4224]{1,0:T(8,128)(2,1)S(1)} collective-permute-done((bf16[64,4224]{1,0:T(8,128)(2,1)S(1)}, bf16[64,4224]{1,0:T(8,128)(2,1)S(1)}, u32[]{:S(2)}, u32[]{:S(2)}) %collective-permute-start.19) | collective-permute-done | bytes 540704 | tf_op jit(solution)/shard_map/out_3_2/ppermute | solution.py:83
  173.6 1.5 collective-permute-start.25
  175.1 9.1 %collective-permute-done.22.refs_3_.refs_7_ = bf16[64,4224]{1,0:T(8,128)(2,1)S(1)} collective-permute-done((bf16[64,4224]{1,0:T(8,128)(2,1)S(1)}, bf16[64,4224]{1,0:T(8,128)(2,1)S(1)}, u32[]{:S(2)}, u32[]{:S(2)}) %collective-permute-start.22) | collective-permute-done | bytes 540704 | tf_op jit(solution)/shard_map/out_3_3/ppermute | solution.py:83
  184.2 4.9 %encode.7 = (f32[16,256]{1,0:T(8,128)S(1)}, s32[16,256]{1,0:T(8,128)S(1)}) custom-call(bf16[64,4224]{1,0:T(8,128)(2,1)S(1)} %get-tuple-element.130.refs_0_.refs_4_, bf16[64,4224]{1,0:T(8,128)(2,1)S(1)} %collective-permute-done.20.refs_1_.refs_5_, bf16[64,4224]{1,0:T(8,128)(2,1)S(1)} %collective-permute-done.19.refs_2_.refs_6_, ...), custom_call_target="tpu_custom_call" | custom-call | tf_op jit(solution)/shard_map/encode/pallas_call | solution.py:180
  189.2 1.6 collective-permute-start.23
  190.8 2.3 collective-permute-done.23.added_ref
  193.0 5.0 %decode.7 = (bf16[64,4096]{1,0:T(8,128)(2,1)S(1)}, bf16[64,4096]{1,0:T(8,128)(2,1)S(1)}, bf16[64,4096]{1,0:T(8,128)(2,1)S(1)}, bf16[64,4096]{1,0:T(8,128)(2,1)S(1)}) custom-call(f32[16,256]{1,0:T(8,128)S(1)} %get-tuple-element.133.chosen_ref, f32[16,256]{1,0:T(8,128)S(1)} %collective-permute-done.23.added_ref, s32[16,256]{1,0:T(8,128)S(1)} %get-tuple-element.134.picks_ref, ...), custom_call_target="tpu_custom_call" | custom-call | tf_op jit(solution)/shard_map/decode/pallas_call | solution.py:227
  198.1 4.7 %collective-permute-done.26.refs_3_ = bf16[64,4096]{1,0:T(8,128)(2,1)S(1)} collective-permute-done((bf16[64,4096]{1,0:T(8,128)(2,1)S(1)}, bf16[64,4096]{1,0:T(8,128)(2,1)S(1)}, u32[]{:S(2)}, u32[]{:S(2)}) %collective-permute-start.26) | collective-permute-done | bytes 524320 | tf_op jit(solution)/shard_map/back_2_3/ppermute | solution.py:83
  203.6 5.0 %collective-permute-start.29 = (bf16[256,2048]{1,0:T(8,128)(2,1)S(1)}, bf16[256,2048]{1,0:T(8,128)(2,1)S(1)}, u32[]{:S(2)}, u32[]{:S(2)}) collective-permute-start(bf16[256,2048]{1,0:T(8,128)(2,1)S(1)} %combine.5), channel_id=1, source_target_pairs={{0,4},{1,5},{2,6},{3,7},{12,8},{13,9},{14,10},{15,11},{16,20},{17,... | collective-permute-start | bytes 3145736 | tf_op jit(solution)/shard_map/sum_inward_two_0/ppermute | solution.py:83
  208.6 1.6 collective-permute-start.24
  211.6 11.8 %collective-permute-done.24.refs_2_ = bf16[64,4096]{1,0:T(8,128)(2,1)S(1)} collective-permute-done((bf16[64,4096]{1,0:T(8,128)(2,1)S(1)}, bf16[64,4096]{1,0:T(8,128)(2,1)S(1)}, u32[]{:S(2)}, u32[]{:S(2)}) %collective-permute-start.24) | collective-permute-done | bytes 524320 | tf_op jit(solution)/shard_map/back_3_2/ppermute | solution.py:83
  223.4 1.6 collective-permute-start.33
  225.8 6.3 %collective-permute-done.29 = bf16[256,2048]{1,0:T(8,128)(2,1)S(1)} collective-permute-done((bf16[256,2048]{1,0:T(8,128)(2,1)S(1)}, bf16[256,2048]{1,0:T(8,128)(2,1)S(1)}, u32[]{:S(2)}, u32[]{:S(2)}) %collective-permute-start.29) | collective-permute-done | bytes 1048608 | tf_op jit(solution)/shard_map/sum_inward_two_0/ppermute | solution.py:83
  233.7 1.6 collective-permute-start.36
  236.0 7.3 %collective-permute-start.35 = (bf16[256,1536]{1,0:T(8,128)(2,1)S(1)}, bf16[256,1536]{1,0:T(8,128)(2,1)S(1)}, u32[]{:S(2)}, u32[]{:S(2)}) collective-permute-start(bf16[256,1536]{1,0:T(8,128)(2,1)S(1)} %combine.8), channel_id=1, source_target_pairs={{0,4},{1,5},{2,6},{3,7},{12,8},{13,9},{14,10},{15,11},{16,20},{17,... | collective-permute-start | bytes 2359304 | tf_op jit(solution)/shard_map/sum_inward_far_0/ppermute | solution.py:83
  243.3 1.4 combine.7
  244.7 1.4 collective-permute-start.31
  246.1 8.5 %collective-permute-done.33 = bf16[256,2048]{1,0:T(8,128)(2,1)S(1)} collective-permute-done((bf16[256,2048]{1,0:T(8,128)(2,1)S(1)}, bf16[256,2048]{1,0:T(8,128)(2,1)S(1)}, u32[]{:S(2)}, u32[]{:S(2)}) %collective-permute-start.33) | collective-permute-done | bytes 1048608 | tf_op jit(solution)/shard_map/sum_inward_two_1/ppermute | solution.py:83
  256.3 15.1 %collective-permute-done.35 = bf16[256,1536]{1,0:T(8,128)(2,1)S(1)} collective-permute-done((bf16[256,1536]{1,0:T(8,128)(2,1)S(1)}, bf16[256,1536]{1,0:T(8,128)(2,1)S(1)}, u32[]{:S(2)}, u32[]{:S(2)}) %collective-permute-start.35) | collective-permute-done | bytes 786464 | tf_op jit(solution)/shard_map/sum_inward_far_0/ppermute | solution.py:83
  271.6 1.3 collective-permute-start.38
  272.9 8.4 %collective-permute-done.32.refs_3_.refs_7_ = bf16[128,4096]{1,0:T(8,128)(2,1)S(1)} collective-permute-done((bf16[128,4096]{1,0:T(8,128)(2,1)S(1)}, bf16[128,4096]{1,0:T(8,128)(2,1)S(1)}, u32[]{:S(2)}, u32[]{:S(2)}) %collective-permute-start.32) | collective-permute-done | bytes 1048608 | tf_op jit(solution)/shard_map/back_near_3/ppermute | solution.py:83
  281.2 17.9 %collective-permute-done.31 = bf16[256,2560]{1,0:T(8,128)(2,1)S(1)} collective-permute-done((bf16[256,2560]{1,0:T(8,128)(2,1)S(1)}, bf16[256,2560]{1,0:T(8,128)(2,1)S(1)}, u32[]{:S(2)}, u32[]{:S(2)}) %collective-permute-start.31) | collective-permute-done | bytes 1310752 | tf_op jit(solution)/shard_map/sum_inward_far_1/ppermute | solution.py:83
  300.4 1.3 collective-permute-start.39
  302.1 2.3 collective-permute-done.30.refs_1_.refs_5_
  304.4 2.4 combine.9
  306.8 26.2 %collective-permute-done.39 = bf16[256,2560]{1,0:T(8,128)(2,1)S(1)} collective-permute-done((bf16[256,2560]{1,0:T(8,128)(2,1)S(1)}, bf16[256,2560]{1,0:T(8,128)(2,1)S(1)}, u32[]{:S(2)}, u32[]{:S(2)}) %collective-permute-start.39) | collective-permute-done | bytes 1310752 | tf_op jit(solution)/shard_map/sum_skip_far_1/ppermute | solution.py:83
  333.0 1.8 add_convert_fusion
  (69 shorter events, 13.9 us)
Async XLA Ops:
  1.9 8.4 %copy-start.3 = (f32[4096]{0:T(1024)S(1)}, f32[4096]{0:T(1024)}, u32[]{:S(2)}) copy-start(f32[4096]{0:T(1024)} %param.8) | copy-start | bytes 49156
  3.7 10.8 %copy-start.4 = (f32[1,1024]{1,0:T(1,128)S(1)}, f32[1,1024]{1,0:T(1,128)}, u32[]{:S(2)}) copy-start(f32[1,1024]{1,0:T(1,128)} %param.13) | copy-start | bytes 12292
  3.7 48.5 %collective-permute-start.5 = (bf16[256,4224]{1,0:T(8,128)(2,1)S(1)}, bf16[256,4224]{1,0:T(8,128)(2,1)}, u32[]{:S(2)}, u32[]{:S(2)}) collective-permute-start(bf16[256,4224]{1,0:T(8,128)(2,1)S(1)} %pad_maximum_fusion.refs_0_), channel_id=1, source_target_pairs={{4,8},{5,9},{6,10},{7,11},{8,4},{9,5},{10,6},{11,7},{20,24},{21,25... | collective-permute-start | bytes 6488072 | tf_op jit(solution)/shard_map/rows_middle/ppermute | solution.py:83
  5.8 51.4 %collective-permute-start.4 = (bf16[256,4224]{1,0:T(8,128)(2,1)S(1)}, bf16[256,4224]{1,0:T(8,128)(2,1)}, u32[]{:S(2)}, u32[]{:S(2)}) collective-permute-start(bf16[256,4224]{1,0:T(8,128)(2,1)S(1)} %pad_maximum_fusion.refs_0_), channel_id=1, source_target_pairs={{0,4},{1,5},{2,6},{3,7},{4,0},{5,1},{6,2},{7,3},{8,12},{9,13},{10,... | collective-permute-start | bytes 6488072 | tf_op jit(solution)/shard_map/rows_ends/ppermute | solution.py:83
  12.6 2.1 collective-permute-start
  12.7 15.4 %collective-permute-start.1 = (bf16[64,4224]{1,0:T(8,128)(2,1)}, bf16[64,4224]{1,0:T(8,128)(2,1)}, u32[]{:S(2)}, u32[]{:S(2)}) collective-permute-start(bf16[64,4224]{1,0:T(8,128)(2,1)} %get-tuple-element.87), channel_id=1, source_target_pairs={{0,2},{1,3},{2,0},{3,1},{4,6},{5,7},{6,4},{7,5},{8,10},{9,11},{10,... | collective-permute-start | bytes 1622024 | tf_op jit(solution)/shard_map/out_0_2/ppermute | solution.py:83
  14.1 24.7 %collective-permute-start.2 = (bf16[64,4224]{1,0:T(8,128)(2,1)}, bf16[64,4224]{1,0:T(8,128)(2,1)}, u32[]{:S(2)}, u32[]{:S(2)}) collective-permute-start(bf16[64,4224]{1,0:T(8,128)(2,1)} %get-tuple-element.88), channel_id=1, source_target_pairs={{0,3},{1,2},{2,1},{3,0},{4,7},{5,6},{6,5},{7,4},{8,11},{9,10},{10,... | collective-permute-start | bytes 1622024 | tf_op jit(solution)/shard_map/out_0_3/ppermute | solution.py:83
  38.9 3.4 %copy-start = (bf16[1,4096,1024]{2,1,0:T(8,128)(2,1)S(1)}, bf16[1,4096,1024]{2,1,0:T(8,128)(2,1)}, u32[]{:S(2)}) copy-start(bf16[1,4096,1024]{2,1,0:T(8,128)(2,1)} %param.11) | copy-start | bytes 25165828
  42.2 21.7 %copy-start.2 = (bf16[1,1024,4096]{2,1,0:T(8,128)(2,1)S(1)}, bf16[1,1024,4096]{2,1,0:T(8,128)(2,1)}, u32[]{:S(2)}) copy-start(bf16[1,1024,4096]{2,1,0:T(8,128)(2,1)} %param.12) | copy-start | bytes 25165828
  48.5 3.8 %collective-permute-start.3 = (f32[16,256]{1,0:T(8,128)S(1)}, f32[16,256]{1,0:T(8,128)S(1)}, u32[]{:S(2)}, u32[]{:S(2)}) collective-permute-start(f32[16,256]{1,0:T(8,128)S(1)} %get-tuple-element.89.chosen_ref), channel_id=1, source_target_pairs={{0,16},{16,0},{1,17},{17,1},{2,18},{18,2},{3,19},{19,3},{4,20},{20... | collective-permute-start | bytes 49160 | tf_op jit(solution)/shard_map/sums_0/ppermute | solution.py:340
  57.2 50.0 %collective-permute-start.12 = (bf16[256,4224]{1,0:T(8,128)(2,1)}, bf16[256,4224]{1,0:T(8,128)(2,1)S(1)}, u32[]{:S(2)}, u32[]{:S(2)}) collective-permute-start(bf16[256,4224]{1,0:T(8,128)(2,1)} %collective-permute-done.5.refs_0_), channel_id=1, source_target_pairs={{4,0},{5,1},{6,2},{7,3},{8,12},{9,13},{10,14},{11,15},{20,16},{21,... | collective-permute-start | bytes 6488072 | tf_op jit(solution)/shard_map/rows_outward_two/ppermute | solution.py:83
  58.5 48.7 %collective-permute-start.11 = (bf16[256,4224]{1,0:T(8,128)(2,1)}, bf16[256,4224]{1,0:T(8,128)(2,1)S(1)}, u32[]{:S(2)}, u32[]{:S(2)}) collective-permute-start(bf16[256,4224]{1,0:T(8,128)(2,1)} %collective-permute-done.4.refs_0_), channel_id=1, source_target_pairs={{4,8},{5,9},{6,10},{7,11},{8,4},{9,5},{10,6},{11,7},{20,24},{21,25... | collective-permute-start | bytes 6488072 | tf_op jit(solution)/shard_map/rows_middle_far/ppermute | solution.py:83
  62.0 7.0 %collective-permute-start.6 = (bf16[64,4224]{1,0:T(8,128)(2,1)S(1)}, bf16[64,4224]{1,0:T(8,128)(2,1)S(1)}, u32[]{:S(2)}, u32[]{:S(2)}) collective-permute-start(bf16[64,4224]{1,0:T(8,128)(2,1)S(1)} %get-tuple-element.96), channel_id=1, source_target_pairs={{0,1},{1,0},{2,3},{3,2},{4,5},{5,4},{6,7},{7,6},{8,9},{9,8},{10,11... | collective-permute-start | bytes 1622024 | tf_op jit(solution)/shard_map/out_1_1/ppermute | solution.py:83
  62.1 15.1 %collective-permute-start.7 = (bf16[64,4224]{1,0:T(8,128)(2,1)S(1)}, bf16[64,4224]{1,0:T(8,128)(2,1)S(1)}, u32[]{:S(2)}, u32[]{:S(2)}) collective-permute-start(bf16[64,4224]{1,0:T(8,128)(2,1)S(1)} %get-tuple-element.97), channel_id=1, source_target_pairs={{0,2},{1,3},{2,0},{3,1},{4,6},{5,7},{6,4},{7,5},{8,10},{9,11},{10,... | collective-permute-start | bytes 1622024 | tf_op jit(solution)/shard_map/out_1_2/ppermute | solution.py:83
  63.6 24.3 %collective-permute-start.8 = (bf16[64,4224]{1,0:T(8,128)(2,1)S(1)}, bf16[64,4224]{1,0:T(8,128)(2,1)S(1)}, u32[]{:S(2)}, u32[]{:S(2)}) collective-permute-start(bf16[64,4224]{1,0:T(8,128)(2,1)S(1)} %get-tuple-element.98), channel_id=1, source_target_pairs={{0,3},{1,2},{2,1},{3,0},{4,7},{5,6},{6,5},{7,4},{8,11},{9,10},{10,... | collective-permute-start | bytes 1622024 | tf_op jit(solution)/shard_map/out_1_3/ppermute | solution.py:83
  63.9 24.0 %copy-start.1 = (bf16[1,4096,1024]{2,1,0:T(8,128)(2,1)S(1)}, bf16[1,4096,1024]{2,1,0:T(8,128)(2,1)}, u32[]{:S(2)}) copy-start(bf16[1,4096,1024]{2,1,0:T(8,128)(2,1)} %param.11) | copy-start | bytes 25165828
  92.9 3.8 %collective-permute-start.9 = (f32[16,256]{1,0:T(8,128)S(1)}, f32[16,256]{1,0:T(8,128)S(1)}, u32[]{:S(2)}, u32[]{:S(2)}) collective-permute-start(f32[16,256]{1,0:T(8,128)S(1)} %get-tuple-element.105.chosen_ref), channel_id=1, source_target_pairs={{0,16},{16,0},{1,17},{17,1},{2,18},{18,2},{3,19},{19,3},{4,20},{20... | collective-permute-start | bytes 49160 | tf_op jit(solution)/shard_map/sums_1/ppermute | solution.py:340
  107.2 50.0 %collective-permute-start.13 = (bf16[256,4224]{1,0:T(8,128)(2,1)S(1)}, bf16[256,4224]{1,0:T(8,128)(2,1)S(1)}, u32[]{:S(2)}, u32[]{:S(2)}) collective-permute-start(bf16[256,4224]{1,0:T(8,128)(2,1)S(1)} %collective-permute-done.11.refs_0_), channel_id=1, source_target_pairs={{4,0},{5,1},{6,2},{7,3},{8,12},{9,13},{10,14},{11,15},{20,16},{21,... | collective-permute-start | bytes 6488072 | tf_op jit(solution)/shard_map/rows_outward_far/ppermute | solution.py:83
  111.4 7.9 %collective-permute-start.14 = (bf16[64,4224]{1,0:T(8,128)(2,1)S(1)}, bf16[64,4224]{1,0:T(8,128)(2,1)S(1)}, u32[]{:S(2)}, u32[]{:S(2)}) collective-permute-start(bf16[64,4224]{1,0:T(8,128)(2,1)S(1)} %get-tuple-element.111), channel_id=1, source_target_pairs={{0,1},{1,0},{2,3},{3,2},{4,5},{5,4},{6,7},{7,6},{8,9},{9,8},{10,11... | collective-permute-start | bytes 1622024 | tf_op jit(solution)/shard_map/out_2_1/ppermute | solution.py:83
  111.5 15.1 %collective-permute-start.15 = (bf16[64,4224]{1,0:T(8,128)(2,1)S(1)}, bf16[64,4224]{1,0:T(8,128)(2,1)S(1)}, u32[]{:S(2)}, u32[]{:S(2)}) collective-permute-start(bf16[64,4224]{1,0:T(8,128)(2,1)S(1)} %get-tuple-element.112), channel_id=1, source_target_pairs={{0,2},{1,3},{2,0},{3,1},{4,6},{5,7},{6,4},{7,5},{8,10},{9,11},{10,... | collective-permute-start | bytes 1622024 | tf_op jit(solution)/shard_map/out_2_2/ppermute | solution.py:83
  113.1 24.3 %collective-permute-start.16 = (bf16[64,4224]{1,0:T(8,128)(2,1)S(1)}, bf16[64,4224]{1,0:T(8,128)(2,1)S(1)}, u32[]{:S(2)}, u32[]{:S(2)}) collective-permute-start(bf16[64,4224]{1,0:T(8,128)(2,1)S(1)} %get-tuple-element.113), channel_id=1, source_target_pairs={{0,3},{1,2},{2,1},{3,0},{4,7},{5,6},{6,5},{7,4},{8,11},{9,10},{10,... | collective-permute-start | bytes 1622024 | tf_op jit(solution)/shard_map/out_2_3/ppermute | solution.py:83
  113.4 61.8 %collective-permute-start.10 = (bf16[256,4096]{1,0:T(8,128)(2,1)S(1)}, bf16[256,4096]{1,0:T(8,128)(2,1)S(1)}, u32[]{:S(2)}, u32[]{:S(2)}) collective-permute-start(bf16[256,4096]{1,0:T(8,128)(2,1)S(1)} %decode.5), channel_id=1, source_target_pairs={{0,4},{1,5},{2,6},{3,7},{12,8},{13,9},{14,10},{15,11},{16,20},{17,... | collective-permute-start | bytes 6291464 | tf_op jit(solution)/shard_map/parts_inward/ppermute | solution.py:83
  142.3 3.8 %collective-permute-start.17 = (f32[16,256]{1,0:T(8,128)S(1)}, f32[16,256]{1,0:T(8,128)S(1)}, u32[]{:S(2)}, u32[]{:S(2)}) collective-permute-start(f32[16,256]{1,0:T(8,128)S(1)} %get-tuple-element.114.chosen_ref), channel_id=1, source_target_pairs={{0,16},{16,0},{1,17},{17,1},{2,18},{18,2},{3,19},{19,3},{4,20},{20... | collective-permute-start | bytes 49160 | tf_op jit(solution)/shard_map/sums_2/ppermute | solution.py:340
  151.1 6.1 %collective-permute-start.18 = (bf16[64,4096]{1,0:T(8,128)(2,1)S(1)}, bf16[64,4096]{1,0:T(8,128)(2,1)S(1)}, u32[]{:S(2)}, u32[]{:S(2)}) collective-permute-start(bf16[64,4096]{1,0:T(8,128)(2,1)S(1)} %get-tuple-element.117), channel_id=1, source_target_pairs={{0,1},{1,0},{2,3},{3,2},{4,5},{5,4},{6,7},{7,6},{8,9},{9,8},{10,11... | collective-permute-start | bytes 1572872 | tf_op jit(solution)/shard_map/back_2_1/ppermute | solution.py:83
  158.4 15.3 %collective-permute-start.19 = (bf16[64,4224]{1,0:T(8,128)(2,1)S(1)}, bf16[64,4224]{1,0:T(8,128)(2,1)S(1)}, u32[]{:S(2)}, u32[]{:S(2)}) collective-permute-start(bf16[64,4224]{1,0:T(8,128)(2,1)S(1)} %get-tuple-element.123), channel_id=1, source_target_pairs={{0,2},{1,3},{2,0},{3,1},{4,6},{5,7},{6,4},{7,5},{8,10},{9,11},{10,... | collective-permute-start | bytes 1622024 | tf_op jit(solution)/shard_map/out_3_2/ppermute | solution.py:83
  159.9 15.2 %collective-permute-start.20 = (bf16[64,4224]{1,0:T(8,128)(2,1)S(1)}, bf16[64,4224]{1,0:T(8,128)(2,1)S(1)}, u32[]{:S(2)}, u32[]{:S(2)}) collective-permute-start(bf16[64,4224]{1,0:T(8,128)(2,1)S(1)} %get-tuple-element.124), channel_id=1, source_target_pairs={{0,1},{1,0},{2,3},{3,2},{4,5},{5,4},{6,7},{7,6},{8,9},{9,8},{10,11... | collective-permute-start | bytes 1622024 | tf_op jit(solution)/shard_map/out_3_1/ppermute | solution.py:83
  159.9 65.1 %collective-permute-start.21 = (bf16[256,4096]{1,0:T(8,128)(2,1)S(1)}, bf16[256,4096]{1,0:T(8,128)(2,1)S(1)}, u32[]{:S(2)}, u32[]{:S(2)}) collective-permute-start(bf16[256,4096]{1,0:T(8,128)(2,1)S(1)} %decode.5), channel_id=1, source_target_pairs={{4,0},{5,1},{6,2},{7,3},{8,12},{9,13},{10,14},{11,15},{20,16},{21,... | collective-permute-start | bytes 6291464 | tf_op jit(solution)/shard_map/parts_outward/ppermute | solution.py:83
  161.2 23.0 %collective-permute-start.22 = (bf16[64,4224]{1,0:T(8,128)(2,1)S(1)}, bf16[64,4224]{1,0:T(8,128)(2,1)S(1)}, u32[]{:S(2)}, u32[]{:S(2)}) collective-permute-start(bf16[64,4224]{1,0:T(8,128)(2,1)S(1)} %get-tuple-element.131), channel_id=1, source_target_pairs={{0,3},{1,2},{2,1},{3,0},{4,7},{5,6},{6,5},{7,4},{8,11},{9,10},{10,... | collective-permute-start | bytes 1622024 | tf_op jit(solution)/shard_map/out_3_3/ppermute | solution.py:83
  173.6 24.4 %collective-permute-start.25 = (bf16[64,4096]{1,0:T(8,128)(2,1)S(1)}, bf16[64,4096]{1,0:T(8,128)(2,1)S(1)}, u32[]{:S(2)}, u32[]{:S(2)}) collective-permute-start(bf16[64,4096]{1,0:T(8,128)(2,1)S(1)} %get-tuple-element.118), channel_id=1, source_target_pairs={{0,2},{1,3},{2,0},{3,1},{4,6},{5,7},{6,4},{7,5},{8,10},{9,11},{10,... | collective-permute-start | bytes 1572872 | tf_op jit(solution)/shard_map/back_2_2/ppermute | solution.py:83
  175.1 27.7 %collective-permute-start.26 = (bf16[64,4096]{1,0:T(8,128)(2,1)S(1)}, bf16[64,4096]{1,0:T(8,128)(2,1)S(1)}, u32[]{:S(2)}, u32[]{:S(2)}) collective-permute-start(bf16[64,4096]{1,0:T(8,128)(2,1)S(1)} %get-tuple-element.119), channel_id=1, source_target_pairs={{0,3},{1,2},{2,1},{3,0},{4,7},{5,6},{6,5},{7,4},{8,11},{9,10},{10,... | collective-permute-start | bytes 1572872 | tf_op jit(solution)/shard_map/back_2_3/ppermute | solution.py:83
  189.2 3.8 %collective-permute-start.23 = (f32[16,256]{1,0:T(8,128)S(1)}, f32[16,256]{1,0:T(8,128)S(1)}, u32[]{:S(2)}, u32[]{:S(2)}) collective-permute-start(f32[16,256]{1,0:T(8,128)S(1)} %get-tuple-element.133.chosen_ref), channel_id=1, source_target_pairs={{0,16},{16,0},{1,17},{17,1},{2,18},{18,2},{3,19},{19,3},{4,20},{20... | collective-permute-start | bytes 49160 | tf_op jit(solution)/shard_map/sums_3/ppermute | solution.py:340
  203.6 28.5 %collective-permute-start.29 = (bf16[256,2048]{1,0:T(8,128)(2,1)S(1)}, bf16[256,2048]{1,0:T(8,128)(2,1)S(1)}, u32[]{:S(2)}, u32[]{:S(2)}) collective-permute-start(bf16[256,2048]{1,0:T(8,128)(2,1)S(1)} %combine.5), channel_id=1, source_target_pairs={{0,4},{1,5},{2,6},{3,7},{12,8},{13,9},{14,10},{15,11},{16,20},{17,... | collective-permute-start | bytes 3145736 | tf_op jit(solution)/shard_map/sum_inward_two_0/ppermute | solution.py:83
  208.6 14.8 %collective-permute-start.24 = (bf16[64,4096]{1,0:T(8,128)(2,1)S(1)}, bf16[64,4096]{1,0:T(8,128)(2,1)S(1)}, u32[]{:S(2)}, u32[]{:S(2)}) collective-permute-start(bf16[64,4096]{1,0:T(8,128)(2,1)S(1)} %get-tuple-element.135), channel_id=1, source_target_pairs={{0,2},{1,3},{2,0},{3,1},{4,6},{5,7},{6,4},{7,5},{8,10},{9,11},{10,... | collective-permute-start | bytes 1572872 | tf_op jit(solution)/shard_map/back_3_2/ppermute | solution.py:83
  210.1 23.4 %collective-permute-start.27 = (bf16[64,4096]{1,0:T(8,128)(2,1)S(1)}, bf16[64,4096]{1,0:T(8,128)(2,1)S(1)}, u32[]{:S(2)}, u32[]{:S(2)}) collective-permute-start(bf16[64,4096]{1,0:T(8,128)(2,1)S(1)} %get-tuple-element.138), channel_id=1, source_target_pairs={{0,1},{1,0},{2,3},{3,2},{4,5},{5,4},{6,7},{7,6},{8,9},{9,8},{10,11... | collective-permute-start | bytes 1572872 | tf_op jit(solution)/shard_map/back_3_1/ppermute | solution.py:83
  210.2 23.3 %collective-permute-start.28 = (bf16[64,4096]{1,0:T(8,128)(2,1)S(1)}, bf16[64,4096]{1,0:T(8,128)(2,1)S(1)}, u32[]{:S(2)}, u32[]{:S(2)}) collective-permute-start(bf16[64,4096]{1,0:T(8,128)(2,1)S(1)} %get-tuple-element.139), channel_id=1, source_target_pairs={{0,3},{1,2},{2,1},{3,0},{4,7},{5,6},{6,5},{7,4},{8,11},{9,10},{10,... | collective-permute-start | bytes 1572872 | tf_op jit(solution)/shard_map/back_3_3/ppermute | solution.py:83
  223.4 31.1 %collective-permute-start.33 = (bf16[256,2048]{1,0:T(8,128)(2,1)S(1)}, bf16[256,2048]{1,0:T(8,128)(2,1)S(1)}, u32[]{:S(2)}, u32[]{:S(2)}) collective-permute-start(bf16[256,2048]{1,0:T(8,128)(2,1)S(1)} %combine.6), channel_id=1, source_target_pairs={{0,4},{1,5},{2,6},{3,7},{12,8},{13,9},{14,10},{15,11},{16,20},{17,... | collective-permute-start | bytes 3145736 | tf_op jit(solution)/shard_map/sum_inward_two_1/ppermute | solution.py:83
  232.4 23.2 %collective-permute-start.37 = (bf16[256,2048]{1,0:T(8,128)(2,1)S(1)}, bf16[256,2048]{1,0:T(8,128)(2,1)S(1)}, u32[]{:S(2)}, u32[]{:S(2)}) collective-permute-start(bf16[256,2048]{1,0:T(8,128)(2,1)S(1)} %add_convert_fusion.2), channel_id=1, source_target_pairs={{4,8},{5,9},{6,10},{7,11},{8,4},{9,5},{10,6},{11,7},{20,24},{21,25... | collective-permute-start | bytes 3145736 | tf_op jit(solution)/shard_map/sum_middle_two_0/ppermute | solution.py:83
  233.7 37.7 %collective-permute-start.36 = (bf16[128,4096]{1,0:T(8,128)(2,1)S(1)}, bf16[128,4096]{1,0:T(8,128)(2,1)S(1)}, u32[]{:S(2)}, u32[]{:S(2)}) collective-permute-start(bf16[128,4096]{1,0:T(8,128)(2,1)S(1)} %pad_maximum_fusion.2), channel_id=1, source_target_pairs={{0,2},{1,3},{2,0},{3,1},{4,6},{5,7},{6,4},{7,5},{8,10},{9,11},{10,... | collective-permute-start | bytes 3145736 | tf_op jit(solution)/shard_map/back_near_2/ppermute | solution.py:83
  236.0 35.3 %collective-permute-start.35 = (bf16[256,1536]{1,0:T(8,128)(2,1)S(1)}, bf16[256,1536]{1,0:T(8,128)(2,1)S(1)}, u32[]{:S(2)}, u32[]{:S(2)}) collective-permute-start(bf16[256,1536]{1,0:T(8,128)(2,1)S(1)} %combine.8), channel_id=1, source_target_pairs={{0,4},{1,5},{2,6},{3,7},{12,8},{13,9},{14,10},{15,11},{16,20},{17,... | collective-permute-start | bytes 2359304 | tf_op jit(solution)/shard_map/sum_inward_far_0/ppermute | solution.py:83
  244.7 54.4 %collective-permute-start.31 = (bf16[256,2560]{1,0:T(8,128)(2,1)S(1)}, bf16[256,2560]{1,0:T(8,128)(2,1)S(1)}, u32[]{:S(2)}, u32[]{:S(2)}) collective-permute-start(bf16[256,2560]{1,0:T(8,128)(2,1)S(1)} %combine.7), channel_id=1, source_target_pairs={{0,4},{1,5},{2,6},{3,7},{12,8},{13,9},{14,10},{15,11},{16,20},{17,... | collective-permute-start | bytes 3932168 | tf_op jit(solution)/shard_map/sum_inward_far_1/ppermute | solution.py:83
  254.9 18.0 %collective-permute-start.34 = (bf16[256,2048]{1,0:T(8,128)(2,1)S(1)}, bf16[256,2048]{1,0:T(8,128)(2,1)S(1)}, u32[]{:S(2)}, u32[]{:S(2)}) collective-permute-start(bf16[256,2048]{1,0:T(8,128)(2,1)S(1)} %add_convert_fusion.3), channel_id=1, source_target_pairs={{4,8},{5,9},{6,10},{7,11},{8,4},{9,5},{10,6},{11,7},{20,24},{21,25... | collective-permute-start | bytes 3145736 | tf_op jit(solution)/shard_map/sum_middle_two_1/ppermute | solution.py:83
  255.7 25.6 %collective-permute-start.32 = (bf16[128,4096]{1,0:T(8,128)(2,1)S(1)}, bf16[128,4096]{1,0:T(8,128)(2,1)S(1)}, u32[]{:S(2)}, u32[]{:S(2)}) collective-permute-start(bf16[128,4096]{1,0:T(8,128)(2,1)S(1)} %pad_maximum_fusion.3), channel_id=1, source_target_pairs={{0,3},{1,2},{2,1},{3,0},{4,7},{5,6},{6,5},{7,4},{8,11},{9,10},{10,... | collective-permute-start | bytes 3145736 | tf_op jit(solution)/shard_map/back_near_3/ppermute | solution.py:83
  271.6 28.5 %collective-permute-start.38 = (bf16[256,1536]{1,0:T(8,128)(2,1)S(1)}, bf16[256,1536]{1,0:T(8,128)(2,1)S(1)}, u32[]{:S(2)}, u32[]{:S(2)}) collective-permute-start(bf16[256,1536]{1,0:T(8,128)(2,1)S(1)} %add_convert_fusion.4), channel_id=1, source_target_pairs={{4,12},{5,13},{6,14},{7,15},{8,0},{9,1},{10,2},{11,3},{20,28},{21,... | collective-permute-start | bytes 2359304 | tf_op jit(solution)/shard_map/sum_skip_far_0/ppermute | solution.py:83
  300.4 32.6 %collective-permute-start.39 = (bf16[256,2560]{1,0:T(8,128)(2,1)S(1)}, bf16[256,2560]{1,0:T(8,128)(2,1)S(1)}, u32[]{:S(2)}, u32[]{:S(2)}) collective-permute-start(bf16[256,2560]{1,0:T(8,128)(2,1)S(1)} %add_convert_fusion.1), channel_id=1, source_target_pairs={{4,12},{5,13},{6,14},{7,15},{8,0},{9,1},{10,2},{11,3},{20,28},{21,... | collective-permute-start | bytes 3932168 | tf_op jit(solution)/shard_map/sum_skip_far_1/ppermute | solution.py:83
  301.7 2.7 collective-permute-start.30

commit v6 on v5

--- a/solution.py
+++ b/solution.py
@@ -14,7 +14,7 @@
 INNER = 4
 OUTER = 4
 EXTRA = 128
-BLOCK = 1024
+BLOCK = 2048
 VMEM = 24 * 1024 * 1024
 F32 = jnp.float32
 BF16 = jnp.bfloat16

time: 335 us -> 334 us (level)
  waiting for transfers between devices: 209 us -> 216 us
  Pallas kernels: 56.5 us -> 51.5 us
    ppermute x36, waiting for transfers between devices: 200 us -> 207 us  [move(): return lax.ppermute(value, 'blocks', pairs)]
    pallas_call x4, Pallas kernels: 21.1 us -> 17.5 us  [encode(): call(kernel, 'encode', (width // BLOCK,), [pl.BlockSpec((cap, BLOCK), lam...]
  transfers between devices with their start and end apart: 40 -> 40, of which waited for: 26 -> 27; matrix products, arithmetic and copies ran while one was open for 1% -> 1% of each run, Pallas kernels for 17% -> 15%
where the time goes in v6:
time: 334 us
  waiting for transfers between devices  216 us (65%)
  starting transfers between devices  54.1 us (16%)
  Pallas kernels  51.5 us (15%)
  other arithmetic  6.91 us (2%)
  local copies, waits for them, and re-layouts  4.58 us (1%)
    ppermute x36, waiting for transfers between devices, move(): return lax.ppermute(value, 'blocks', pairs)  207 us
    ppermute x36, starting transfers between devices, move(): return lax.ppermute(value, 'blocks', pairs)  47.8 us
    pallas_call x4, Pallas kernels, decode(): call(decode_kernel, 'decode', (width // BLOCK,), [pl.BlockSpec((picked, s...  18.7 us
    pallas_call x4, Pallas kernels, encode(): call(kernel, 'encode', (width // BLOCK,), [pl.BlockSpec((cap, BLOCK), lam...  17.5 us
    ppermute x4, waiting for transfers between devices, encoded(): added = lax.ppermute(chosen, 'dp', [(0, 1), (1, 0)])  8.91 us
    pallas_call x4, Pallas kernels, dispatch(): call(functools.partial(dispatch_kernel, cap, len(values)), 'dispatch', ()...  8.85 us
  transfers between devices with their start and end apart: 40, of which 27 were waited for; matrix products, arithmetic and copies ran while one was open for 1% of the time, Pallas kernels for 15%

profile of v6, /device:TPU:0, one launch (start us, length us, event | category | flops | bytes accessed | tf_op | source)
XLA Modules:
  0.0 333.7 jit_solution(14288651853725924969)
XLA Ops:
  2.0 1.8 pad_maximum_fusion.refs_0_
  3.7 2.0 collective-permute-start.5
  5.8 4.5 %collective-permute-start.4 = (bf16[256,4224]{1,0:T(8,128)(2,1)S(1)}, bf16[256,4224]{1,0:T(8,128)(2,1)}, u32[]{:S(2)}, u32[]{:S(2)}) collective-permute-start(bf16[256,4224]{1,0:T(8,128)(2,1)S(1)} %pad_maximum_fusion.refs_0_), channel_id=1, source_target_pairs={{0,4},{1,5},{2,6},{3,7},{4,0},{5,1},{6,2},{7,3},{8,12},{9,13},{10,... | collective-permute-start | bytes 6488072 | tf_op jit(solution)/shard_map/rows_ends/ppermute | solution.py:83
  10.4 2.2 dispatch.4
  12.7 1.5 collective-permute-start.1
  14.8 13.2 %collective-permute-done.1.refs_2_.refs_6_ = bf16[64,4224]{1,0:T(8,128)(2,1)} collective-permute-done((bf16[64,4224]{1,0:T(8,128)(2,1)}, bf16[64,4224]{1,0:T(8,128)(2,1)}, u32[]{:S(2)}, u32[]{:S(2)}) %collective-permute-start.1) | collective-permute-done | bytes 540704 | tf_op jit(solution)/shard_map/out_0_2/ppermute | solution.py:83
  28.0 10.8 %collective-permute-done.2.refs_3_.refs_7_ = bf16[64,4224]{1,0:T(8,128)(2,1)} collective-permute-done((bf16[64,4224]{1,0:T(8,128)(2,1)}, bf16[64,4224]{1,0:T(8,128)(2,1)}, u32[]{:S(2)}, u32[]{:S(2)}) %collective-permute-start.2) | collective-permute-done | bytes 540704 | tf_op jit(solution)/shard_map/out_0_3/ppermute | solution.py:83
  38.9 3.4 %copy-done = bf16[1,4096,1024]{2,1,0:T(8,128)(2,1)S(1)} copy-done((bf16[1,4096,1024]{2,1,0:T(8,128)(2,1)S(1)}, bf16[1,4096,1024]{2,1,0:T(8,128)(2,1)}, u32[]{:S(2)}) %copy-start) | copy-done | bytes 8388632
  42.2 5.0 %encode.4 = (f32[16,256]{1,0:T(8,128)S(1)}, s32[16,256]{1,0:T(8,128)S(1)}) custom-call(bf16[64,4224]{1,0:T(8,128)(2,1)S(1)} %get-tuple-element.85.refs_0_.refs_4_, bf16[64,4224]{1,0:T(8,128)(2,1)S(1)} %collective-permute-done.refs_1_.refs_5_, bf16[64,4224]{1,0:T(8,128)(2,1)} %collective-permute-done.1.refs_2_.refs_6_, ...), custom_call_target="tpu_custom_call" | custom-call | tf_op jit(solution)/shard_map/encode/pallas_call | solution.py:180
  47.3 1.6 collective-permute-start.3
  48.9 2.2 collective-permute-done.3.added_ref
  51.1 6.1 %collective-permute-done.4.refs_0_ = bf16[256,4224]{1,0:T(8,128)(2,1)} collective-permute-done((bf16[256,4224]{1,0:T(8,128)(2,1)S(1)}, bf16[256,4224]{1,0:T(8,128)(2,1)}, u32[]{:S(2)}, u32[]{:S(2)}) %collective-permute-start.4) | collective-permute-done | bytes 2162720 | tf_op jit(solution)/shard_map/rows_ends/ppermute | solution.py:83
  57.2 1.3 collective-permute-start.12
  59.5 2.7 dispatch.5
  62.3 1.6 collective-permute-start.7
  64.1 4.7 %decode.4 = (bf16[64,4096]{1,0:T(8,128)(2,1)S(1)}, bf16[64,4096]{1,0:T(8,128)(2,1)S(1)}, bf16[64,4096]{1,0:T(8,128)(2,1)S(1)}, bf16[64,4096]{1,0:T(8,128)(2,1)S(1)}) custom-call(f32[16,256]{1,0:T(8,128)S(1)} %get-tuple-element.89.chosen_ref, f32[16,256]{1,0:T(8,128)S(1)} %collective-permute-done.3.added_ref, s32[16,256]{1,0:T(8,128)S(1)} %get-tuple-element.91.picks_ref, ...), custom_call_target="tpu_custom_call" | custom-call | tf_op jit(solution)/shard_map/decode/pallas_call | solution.py:227
  68.8 8.6 %collective-permute-done.7.refs_2_.refs_6_ = bf16[64,4224]{1,0:T(8,128)(2,1)S(1)} collective-permute-done((bf16[64,4224]{1,0:T(8,128)(2,1)S(1)}, bf16[64,4224]{1,0:T(8,128)(2,1)S(1)}, u32[]{:S(2)}, u32[]{:S(2)}) %collective-permute-start.7) | collective-permute-done | bytes 540704 | tf_op jit(solution)/shard_map/out_1_2/ppermute | solution.py:83
  77.4 10.7 %collective-permute-done.8.refs_3_.refs_7_ = bf16[64,4224]{1,0:T(8,128)(2,1)S(1)} collective-permute-done((bf16[64,4224]{1,0:T(8,128)(2,1)S(1)}, bf16[64,4224]{1,0:T(8,128)(2,1)S(1)}, u32[]{:S(2)}, u32[]{:S(2)}) %collective-permute-start.8) | collective-permute-done | bytes 540704 | tf_op jit(solution)/shard_map/out_1_3/ppermute | solution.py:83
  88.1 4.2 %encode.5 = (f32[16,256]{1,0:T(8,128)S(1)}, s32[16,256]{1,0:T(8,128)S(1)}) custom-call(bf16[64,4224]{1,0:T(8,128)(2,1)S(1)} %get-tuple-element.101.refs_0_.refs_4_, bf16[64,4224]{1,0:T(8,128)(2,1)S(1)} %collective-permute-done.6.refs_1_.refs_5_, bf16[64,4224]{1,0:T(8,128)(2,1)S(1)} %collective-permute-done.7.refs_2_.refs_6_, ...), custom_call_target="tpu_custom_call" | custom-call | tf_op jit(solution)/shard_map/encode/pallas_call | solution.py:180
  92.3 1.6 collective-permute-start.9
  93.8 2.2 collective-permute-done.9.added_ref
  96.1 4.7 %decode.5 = bf16[256,4096]{1,0:T(8,128)(2,1)S(1)} custom-call(f32[16,256]{1,0:T(8,128)S(1)} %get-tuple-element.105.chosen_ref, f32[16,256]{1,0:T(8,128)S(1)} %collective-permute-done.9.added_ref, s32[16,256]{1,0:T(8,128)S(1)} %get-tuple-element.106.picks_ref, bf16[1024,4096]{1,0:T(8,128)(2,1)S(1)} %bitcast.9), custom_call_target="tpu_custom_call" | custom-call | tf_op jit(solution)/shard_map/decode/pallas_call | solution.py:227
  100.7 6.4 %collective-permute-done.12.refs_1_ = bf16[256,4224]{1,0:T(8,128)(2,1)S(1)} collective-permute-done((bf16[256,4224]{1,0:T(8,128)(2,1)}, bf16[256,4224]{1,0:T(8,128)(2,1)S(1)}, u32[]{:S(2)}, u32[]{:S(2)}) %collective-permute-start.12) | collective-permute-done | bytes 2162720 | tf_op jit(solution)/shard_map/rows_outward_two/ppermute | solution.py:83
  107.2 1.3 collective-permute-start.13
  108.5 2.8 dispatch.6
  111.3 1.6 collective-permute-start.15
  113.2 6.2 %collective-permute-start.10 = (bf16[256,4096]{1,0:T(8,128)(2,1)S(1)}, bf16[256,4096]{1,0:T(8,128)(2,1)S(1)}, u32[]{:S(2)}, u32[]{:S(2)}) collective-permute-start(bf16[256,4096]{1,0:T(8,128)(2,1)S(1)} %decode.5), channel_id=1, source_target_pairs={{0,4},{1,5},{2,6},{3,7},{12,8},{13,9},{14,10},{15,11},{16,20},{17,... | collective-permute-start | bytes 6291464 | tf_op jit(solution)/shard_map/parts_inward/ppermute | solution.py:83
  119.4 7.1 %collective-permute-done.15.refs_2_.refs_6_ = bf16[64,4224]{1,0:T(8,128)(2,1)S(1)} collective-permute-done((bf16[64,4224]{1,0:T(8,128)(2,1)S(1)}, bf16[64,4224]{1,0:T(8,128)(2,1)S(1)}, u32[]{:S(2)}, u32[]{:S(2)}) %collective-permute-start.15) | collective-permute-done | bytes 540704 | tf_op jit(solution)/shard_map/out_2_2/ppermute | solution.py:83
  126.5 10.7 %collective-permute-done.16.refs_3_.refs_7_ = bf16[64,4224]{1,0:T(8,128)(2,1)S(1)} collective-permute-done((bf16[64,4224]{1,0:T(8,128)(2,1)S(1)}, bf16[64,4224]{1,0:T(8,128)(2,1)S(1)}, u32[]{:S(2)}, u32[]{:S(2)}) %collective-permute-start.16) | collective-permute-done | bytes 540704 | tf_op jit(solution)/shard_map/out_2_3/ppermute | solution.py:83
  137.1 4.2 %encode.6 = (f32[16,256]{1,0:T(8,128)S(1)}, s32[16,256]{1,0:T(8,128)S(1)}) custom-call(bf16[64,4224]{1,0:T(8,128)(2,1)S(1)} %get-tuple-element.110.refs_0_.refs_4_, bf16[64,4224]{1,0:T(8,128)(2,1)S(1)} %collective-permute-done.14.refs_1_.refs_5_, bf16[64,4224]{1,0:T(8,128)(2,1)S(1)} %collective-permute-done.15.refs_2_.refs_6_, ...), custom_call_target="tpu_custom_call" | custom-call | tf_op jit(solution)/shard_map/encode/pallas_call | solution.py:180
  141.3 1.6 collective-permute-start.17
  142.9 2.2 collective-permute-done.17.added_ref
  145.1 4.7 %decode.6 = (bf16[64,4096]{1,0:T(8,128)(2,1)S(1)}, bf16[64,4096]{1,0:T(8,128)(2,1)S(1)}, bf16[64,4096]{1,0:T(8,128)(2,1)S(1)}, bf16[64,4096]{1,0:T(8,128)(2,1)S(1)}) custom-call(f32[16,256]{1,0:T(8,128)S(1)} %get-tuple-element.114.chosen_ref, f32[16,256]{1,0:T(8,128)S(1)} %collective-permute-done.17.added_ref, s32[16,256]{1,0:T(8,128)S(1)} %get-tuple-element.115.picks_ref, ...), custom_call_target="tpu_custom_call" | custom-call | tf_op jit(solution)/shard_map/decode/pallas_call | solution.py:227
  149.9 7.3 %collective-permute-done.13.refs_1_ = bf16[256,4224]{1,0:T(8,128)(2,1)S(1)} collective-permute-done((bf16[256,4224]{1,0:T(8,128)(2,1)S(1)}, bf16[256,4224]{1,0:T(8,128)(2,1)S(1)}, u32[]{:S(2)}, u32[]{:S(2)}) %collective-permute-start.13) | collective-permute-done | bytes 2162720 | tf_op jit(solution)/shard_map/rows_outward_far/ppermute | solution.py:83
  157.2 1.1 dispatch.7
  158.4 1.6 collective-permute-start.19
  159.9 1.3 collective-permute-start.21
  161.9 11.7 %collective-permute-done.19.refs_2_.refs_6_ = bf16[64,4224]{1,0:T(8,128)(2,1)S(1)} collective-permute-done((bf16[64,4224]{1,0:T(8,128)(2,1)S(1)}, bf16[64,4224]{1,0:T(8,128)(2,1)S(1)}, u32[]{:S(2)}, u32[]{:S(2)}) %collective-permute-start.19) | collective-permute-done | bytes 540704 | tf_op jit(solution)/shard_map/out_3_2/ppermute | solution.py:83
  173.6 1.5 collective-permute-start.25
  175.1 9.1 %collective-permute-done.22.refs_3_.refs_7_ = bf16[64,4224]{1,0:T(8,128)(2,1)S(1)} collective-permute-done((bf16[64,4224]{1,0:T(8,128)(2,1)S(1)}, bf16[64,4224]{1,0:T(8,128)(2,1)S(1)}, u32[]{:S(2)}, u32[]{:S(2)}) %collective-permute-start.22) | collective-permute-done | bytes 540704 | tf_op jit(solution)/shard_map/out_3_3/ppermute | solution.py:83
  184.2 4.2 %encode.7 = (f32[16,256]{1,0:T(8,128)S(1)}, s32[16,256]{1,0:T(8,128)S(1)}) custom-call(bf16[64,4224]{1,0:T(8,128)(2,1)S(1)} %get-tuple-element.130.refs_0_.refs_4_, bf16[64,4224]{1,0:T(8,128)(2,1)S(1)} %collective-permute-done.20.refs_1_.refs_5_, bf16[64,4224]{1,0:T(8,128)(2,1)S(1)} %collective-permute-done.19.refs_2_.refs_6_, ...), custom_call_target="tpu_custom_call" | custom-call | tf_op jit(solution)/shard_map/encode/pallas_call | solution.py:180
  188.4 1.6 collective-permute-start.23
  190.0 2.3 collective-permute-done.23.added_ref
  192.2 4.7 %decode.7 = (bf16[64,4096]{1,0:T(8,128)(2,1)S(1)}, bf16[64,4096]{1,0:T(8,128)(2,1)S(1)}, bf16[64,4096]{1,0:T(8,128)(2,1)S(1)}, bf16[64,4096]{1,0:T(8,128)(2,1)S(1)}) custom-call(f32[16,256]{1,0:T(8,128)S(1)} %get-tuple-element.133.chosen_ref, f32[16,256]{1,0:T(8,128)S(1)} %collective-permute-done.23.added_ref, s32[16,256]{1,0:T(8,128)S(1)} %get-tuple-element.134.picks_ref, ...), custom_call_target="tpu_custom_call" | custom-call | tf_op jit(solution)/shard_map/decode/pallas_call | solution.py:227
  196.9 5.9 %collective-permute-done.26.refs_3_ = bf16[64,4096]{1,0:T(8,128)(2,1)S(1)} collective-permute-done((bf16[64,4096]{1,0:T(8,128)(2,1)S(1)}, bf16[64,4096]{1,0:T(8,128)(2,1)S(1)}, u32[]{:S(2)}, u32[]{:S(2)}) %collective-permute-start.26) | collective-permute-done | bytes 524320 | tf_op jit(solution)/shard_map/back_2_3/ppermute | solution.py:83
  203.6 3.7 %collective-permute-start.29 = (bf16[256,2048]{1,0:T(8,128)(2,1)S(1)}, bf16[256,2048]{1,0:T(8,128)(2,1)S(1)}, u32[]{:S(2)}, u32[]{:S(2)}) collective-permute-start(bf16[256,2048]{1,0:T(8,128)(2,1)S(1)} %combine.5), channel_id=1, source_target_pairs={{0,4},{1,5},{2,6},{3,7},{12,8},{13,9},{14,10},{15,11},{16,20},{17,... | collective-permute-start | bytes 3145736 | tf_op jit(solution)/shard_map/sum_inward_two_0/ppermute | solution.py:83
  207.9 1.2 collective-permute-start.27
  210.3 11.8 %collective-permute-done.24.refs_2_ = bf16[64,4096]{1,0:T(8,128)(2,1)S(1)} collective-permute-done((bf16[64,4096]{1,0:T(8,128)(2,1)S(1)}, bf16[64,4096]{1,0:T(8,128)(2,1)S(1)}, u32[]{:S(2)}, u32[]{:S(2)}) %collective-permute-start.24) | collective-permute-done | bytes 524320 | tf_op jit(solution)/shard_map/back_3_2/ppermute | solution.py:83
  222.1 1.4 collective-permute-start.33
  224.3 6.3 %collective-permute-done.29 = bf16[256,2048]{1,0:T(8,128)(2,1)S(1)} collective-permute-done((bf16[256,2048]{1,0:T(8,128)(2,1)S(1)}, bf16[256,2048]{1,0:T(8,128)(2,1)S(1)}, u32[]{:S(2)}, u32[]{:S(2)}) %collective-permute-start.29) | collective-permute-done | bytes 1048608 | tf_op jit(solution)/shard_map/sum_inward_two_0/ppermute | solution.py:83
  232.7 1.4 collective-permute-start.36
  234.9 5.4 %collective-permute-start.35 = (bf16[256,1536]{1,0:T(8,128)(2,1)S(1)}, bf16[256,1536]{1,0:T(8,128)(2,1)S(1)}, u32[]{:S(2)}, u32[]{:S(2)}) collective-permute-start(bf16[256,1536]{1,0:T(8,128)(2,1)S(1)} %combine.8), channel_id=1, source_target_pairs={{0,4},{1,5},{2,6},{3,7},{12,8},{13,9},{14,10},{15,11},{16,20},{17,... | collective-permute-start | bytes 2359304 | tf_op jit(solution)/shard_map/sum_inward_far_0/ppermute | solution.py:83
  240.3 1.4 combine.7
  241.7 1.4 collective-permute-start.31
  243.1 9.9 %collective-permute-done.33 = bf16[256,2048]{1,0:T(8,128)(2,1)S(1)} collective-permute-done((bf16[256,2048]{1,0:T(8,128)(2,1)S(1)}, bf16[256,2048]{1,0:T(8,128)(2,1)S(1)}, u32[]{:S(2)}, u32[]{:S(2)}) %collective-permute-start.33) | collective-permute-done | bytes 1048608 | tf_op jit(solution)/shard_map/sum_inward_two_1/ppermute | solution.py:83
  255.2 14.6 %collective-permute-done.35 = bf16[256,1536]{1,0:T(8,128)(2,1)S(1)} collective-permute-done((bf16[256,1536]{1,0:T(8,128)(2,1)S(1)}, bf16[256,1536]{1,0:T(8,128)(2,1)S(1)}, u32[]{:S(2)}, u32[]{:S(2)}) %collective-permute-start.35) | collective-permute-done | bytes 786464 | tf_op jit(solution)/shard_map/sum_inward_far_0/ppermute | solution.py:83
  270.0 1.3 collective-permute-start.38
  271.4 8.4 %collective-permute-done.32.refs_3_.refs_7_ = bf16[128,4096]{1,0:T(8,128)(2,1)S(1)} collective-permute-done((bf16[128,4096]{1,0:T(8,128)(2,1)S(1)}, bf16[128,4096]{1,0:T(8,128)(2,1)S(1)}, u32[]{:S(2)}, u32[]{:S(2)}) %collective-permute-start.32) | collective-permute-done | bytes 1048608 | tf_op jit(solution)/shard_map/back_near_3/ppermute | solution.py:83
  279.7 18.0 %collective-permute-done.31 = bf16[256,2560]{1,0:T(8,128)(2,1)S(1)} collective-permute-done((bf16[256,2560]{1,0:T(8,128)(2,1)S(1)}, bf16[256,2560]{1,0:T(8,128)(2,1)S(1)}, u32[]{:S(2)}, u32[]{:S(2)}) %collective-permute-start.31) | collective-permute-done | bytes 1310752 | tf_op jit(solution)/shard_map/sum_inward_far_1/ppermute | solution.py:83
  299.2 1.3 collective-permute-start.39
  301.0 2.3 collective-permute-done.30.refs_1_.refs_5_
  303.3 2.4 combine.9
  305.6 26.2 %collective-permute-done.39 = bf16[256,2560]{1,0:T(8,128)(2,1)S(1)} collective-permute-done((bf16[256,2560]{1,0:T(8,128)(2,1)S(1)}, bf16[256,2560]{1,0:T(8,128)(2,1)S(1)}, u32[]{:S(2)}, u32[]{:S(2)}) %collective-permute-start.39) | collective-permute-done | bytes 1310752 | tf_op jit(solution)/shard_map/sum_skip_far_1/ppermute | solution.py:83
  331.8 1.8 add_convert_fusion
  (69 shorter events, 15.7 us)
Async XLA Ops:
  1.9 8.4 %copy-start.3 = (f32[4096]{0:T(1024)S(1)}, f32[4096]{0:T(1024)}, u32[]{:S(2)}) copy-start(f32[4096]{0:T(1024)} %param.8) | copy-start | bytes 49156
  3.7 10.8 %copy-start.4 = (f32[1,1024]{1,0:T(1,128)S(1)}, f32[1,1024]{1,0:T(1,128)}, u32[]{:S(2)}) copy-start(f32[1,1024]{1,0:T(1,128)} %param.13) | copy-start | bytes 12292
  3.7 47.3 %collective-permute-start.5 = (bf16[256,4224]{1,0:T(8,128)(2,1)S(1)}, bf16[256,4224]{1,0:T(8,128)(2,1)}, u32[]{:S(2)}, u32[]{:S(2)}) collective-permute-start(bf16[256,4224]{1,0:T(8,128)(2,1)S(1)} %pad_maximum_fusion.refs_0_), channel_id=1, source_target_pairs={{4,8},{5,9},{6,10},{7,11},{8,4},{9,5},{10,6},{11,7},{20,24},{21,25... | collective-permute-start | bytes 6488072 | tf_op jit(solution)/shard_map/rows_middle/ppermute | solution.py:83
  5.8 51.4 %collective-permute-start.4 = (bf16[256,4224]{1,0:T(8,128)(2,1)S(1)}, bf16[256,4224]{1,0:T(8,128)(2,1)}, u32[]{:S(2)}, u32[]{:S(2)}) collective-permute-start(bf16[256,4224]{1,0:T(8,128)(2,1)S(1)} %pad_maximum_fusion.refs_0_), channel_id=1, source_target_pairs={{0,4},{1,5},{2,6},{3,7},{4,0},{5,1},{6,2},{7,3},{8,12},{9,13},{10,... | collective-permute-start | bytes 6488072 | tf_op jit(solution)/shard_map/rows_ends/ppermute | solution.py:83
  12.6 2.1 collective-permute-start
  12.7 15.4 %collective-permute-start.1 = (bf16[64,4224]{1,0:T(8,128)(2,1)}, bf16[64,4224]{1,0:T(8,128)(2,1)}, u32[]{:S(2)}, u32[]{:S(2)}) collective-permute-start(bf16[64,4224]{1,0:T(8,128)(2,1)} %get-tuple-element.87), channel_id=1, source_target_pairs={{0,2},{1,3},{2,0},{3,1},{4,6},{5,7},{6,4},{7,5},{8,10},{9,11},{10,... | collective-permute-start | bytes 1622024 | tf_op jit(solution)/shard_map/out_0_2/ppermute | solution.py:83
  14.1 24.7 %collective-permute-start.2 = (bf16[64,4224]{1,0:T(8,128)(2,1)}, bf16[64,4224]{1,0:T(8,128)(2,1)}, u32[]{:S(2)}, u32[]{:S(2)}) collective-permute-start(bf16[64,4224]{1,0:T(8,128)(2,1)} %get-tuple-element.88), channel_id=1, source_target_pairs={{0,3},{1,2},{2,1},{3,0},{4,7},{5,6},{6,5},{7,4},{8,11},{9,10},{10,... | collective-permute-start | bytes 1622024 | tf_op jit(solution)/shard_map/out_0_3/ppermute | solution.py:83
  38.9 3.4 %copy-start = (bf16[1,4096,1024]{2,1,0:T(8,128)(2,1)S(1)}, bf16[1,4096,1024]{2,1,0:T(8,128)(2,1)}, u32[]{:S(2)}) copy-start(bf16[1,4096,1024]{2,1,0:T(8,128)(2,1)} %param.11) | copy-start | bytes 25165828
  42.2 21.9 %copy-start.2 = (bf16[1,1024,4096]{2,1,0:T(8,128)(2,1)S(1)}, bf16[1,1024,4096]{2,1,0:T(8,128)(2,1)}, u32[]{:S(2)}) copy-start(bf16[1,1024,4096]{2,1,0:T(8,128)(2,1)} %param.12) | copy-start | bytes 25165828
  47.3 3.8 %collective-permute-start.3 = (f32[16,256]{1,0:T(8,128)S(1)}, f32[16,256]{1,0:T(8,128)S(1)}, u32[]{:S(2)}, u32[]{:S(2)}) collective-permute-start(f32[16,256]{1,0:T(8,128)S(1)} %get-tuple-element.89.chosen_ref), channel_id=1, source_target_pairs={{0,16},{16,0},{1,17},{17,1},{2,18},{18,2},{3,19},{19,3},{4,20},{20... | collective-permute-start | bytes 49160 | tf_op jit(solution)/shard_map/sums_0/ppermute | solution.py:340
  57.2 50.0 %collective-permute-start.12 = (bf16[256,4224]{1,0:T(8,128)(2,1)}, bf16[256,4224]{1,0:T(8,128)(2,1)S(1)}, u32[]{:S(2)}, u32[]{:S(2)}) collective-permute-start(bf16[256,4224]{1,0:T(8,128)(2,1)} %collective-permute-done.5.refs_0_), channel_id=1, source_target_pairs={{4,0},{5,1},{6,2},{7,3},{8,12},{9,13},{10,14},{11,15},{20,16},{21,... | collective-permute-start | bytes 6488072 | tf_op jit(solution)/shard_map/rows_outward_two/ppermute | solution.py:83
  58.5 48.7 %collective-permute-start.11 = (bf16[256,4224]{1,0:T(8,128)(2,1)}, bf16[256,4224]{1,0:T(8,128)(2,1)S(1)}, u32[]{:S(2)}, u32[]{:S(2)}) collective-permute-start(bf16[256,4224]{1,0:T(8,128)(2,1)} %collective-permute-done.4.refs_0_), channel_id=1, source_target_pairs={{4,8},{5,9},{6,10},{7,11},{8,4},{9,5},{10,6},{11,7},{20,24},{21,25... | collective-permute-start | bytes 6488072 | tf_op jit(solution)/shard_map/rows_middle_far/ppermute | solution.py:83
  62.2 6.6 %collective-permute-start.6 = (bf16[64,4224]{1,0:T(8,128)(2,1)S(1)}, bf16[64,4224]{1,0:T(8,128)(2,1)S(1)}, u32[]{:S(2)}, u32[]{:S(2)}) collective-permute-start(bf16[64,4224]{1,0:T(8,128)(2,1)S(1)} %get-tuple-element.96), channel_id=1, source_target_pairs={{0,1},{1,0},{2,3},{3,2},{4,5},{5,4},{6,7},{7,6},{8,9},{9,8},{10,11... | collective-permute-start | bytes 1622024 | tf_op jit(solution)/shard_map/out_1_1/ppermute | solution.py:83
  62.3 15.1 %collective-permute-start.7 = (bf16[64,4224]{1,0:T(8,128)(2,1)S(1)}, bf16[64,4224]{1,0:T(8,128)(2,1)S(1)}, u32[]{:S(2)}, u32[]{:S(2)}) collective-permute-start(bf16[64,4224]{1,0:T(8,128)(2,1)S(1)} %get-tuple-element.97), channel_id=1, source_target_pairs={{0,2},{1,3},{2,0},{3,1},{4,6},{5,7},{6,4},{7,5},{8,10},{9,11},{10,... | collective-permute-start | bytes 1622024 | tf_op jit(solution)/shard_map/out_1_2/ppermute | solution.py:83
  63.8 24.3 %collective-permute-start.8 = (bf16[64,4224]{1,0:T(8,128)(2,1)S(1)}, bf16[64,4224]{1,0:T(8,128)(2,1)S(1)}, u32[]{:S(2)}, u32[]{:S(2)}) collective-permute-start(bf16[64,4224]{1,0:T(8,128)(2,1)S(1)} %get-tuple-element.98), channel_id=1, source_target_pairs={{0,3},{1,2},{2,1},{3,0},{4,7},{5,6},{6,5},{7,4},{8,11},{9,10},{10,... | collective-permute-start | bytes 1622024 | tf_op jit(solution)/shard_map/out_1_3/ppermute | solution.py:83
  64.1 24.0 %copy-start.1 = (bf16[1,4096,1024]{2,1,0:T(8,128)(2,1)S(1)}, bf16[1,4096,1024]{2,1,0:T(8,128)(2,1)}, u32[]{:S(2)}) copy-start(bf16[1,4096,1024]{2,1,0:T(8,128)(2,1)} %param.11) | copy-start | bytes 25165828
  92.3 3.8 %collective-permute-start.9 = (f32[16,256]{1,0:T(8,128)S(1)}, f32[16,256]{1,0:T(8,128)S(1)}, u32[]{:S(2)}, u32[]{:S(2)}) collective-permute-start(f32[16,256]{1,0:T(8,128)S(1)} %get-tuple-element.105.chosen_ref), channel_id=1, source_target_pairs={{0,16},{16,0},{1,17},{17,1},{2,18},{18,2},{3,19},{19,3},{4,20},{20... | collective-permute-start | bytes 49160 | tf_op jit(solution)/shard_map/sums_1/ppermute | solution.py:340
  107.2 50.0 %collective-permute-start.13 = (bf16[256,4224]{1,0:T(8,128)(2,1)S(1)}, bf16[256,4224]{1,0:T(8,128)(2,1)S(1)}, u32[]{:S(2)}, u32[]{:S(2)}) collective-permute-start(bf16[256,4224]{1,0:T(8,128)(2,1)S(1)} %collective-permute-done.11.refs_0_), channel_id=1, source_target_pairs={{4,0},{5,1},{6,2},{7,3},{8,12},{9,13},{10,14},{11,15},{20,16},{21,... | collective-permute-start | bytes 6488072 | tf_op jit(solution)/shard_map/rows_outward_far/ppermute | solution.py:83
  111.2 8.1 %collective-permute-start.14 = (bf16[64,4224]{1,0:T(8,128)(2,1)S(1)}, bf16[64,4224]{1,0:T(8,128)(2,1)S(1)}, u32[]{:S(2)}, u32[]{:S(2)}) collective-permute-start(bf16[64,4224]{1,0:T(8,128)(2,1)S(1)} %get-tuple-element.111), channel_id=1, source_target_pairs={{0,1},{1,0},{2,3},{3,2},{4,5},{5,4},{6,7},{7,6},{8,9},{9,8},{10,11... | collective-permute-start | bytes 1622024 | tf_op jit(solution)/shard_map/out_2_1/ppermute | solution.py:83
  111.3 15.1 %collective-permute-start.15 = (bf16[64,4224]{1,0:T(8,128)(2,1)S(1)}, bf16[64,4224]{1,0:T(8,128)(2,1)S(1)}, u32[]{:S(2)}, u32[]{:S(2)}) collective-permute-start(bf16[64,4224]{1,0:T(8,128)(2,1)S(1)} %get-tuple-element.112), channel_id=1, source_target_pairs={{0,2},{1,3},{2,0},{3,1},{4,6},{5,7},{6,4},{7,5},{8,10},{9,11},{10,... | collective-permute-start | bytes 1622024 | tf_op jit(solution)/shard_map/out_2_2/ppermute | solution.py:83
  112.9 24.3 %collective-permute-start.16 = (bf16[64,4224]{1,0:T(8,128)(2,1)S(1)}, bf16[64,4224]{1,0:T(8,128)(2,1)S(1)}, u32[]{:S(2)}, u32[]{:S(2)}) collective-permute-start(bf16[64,4224]{1,0:T(8,128)(2,1)S(1)} %get-tuple-element.113), channel_id=1, source_target_pairs={{0,3},{1,2},{2,1},{3,0},{4,7},{5,6},{6,5},{7,4},{8,11},{9,10},{10,... | collective-permute-start | bytes 1622024 | tf_op jit(solution)/shard_map/out_2_3/ppermute | solution.py:83
  113.2 62.0 %collective-permute-start.10 = (bf16[256,4096]{1,0:T(8,128)(2,1)S(1)}, bf16[256,4096]{1,0:T(8,128)(2,1)S(1)}, u32[]{:S(2)}, u32[]{:S(2)}) collective-permute-start(bf16[256,4096]{1,0:T(8,128)(2,1)S(1)} %decode.5), channel_id=1, source_target_pairs={{0,4},{1,5},{2,6},{3,7},{12,8},{13,9},{14,10},{15,11},{16,20},{17,... | collective-permute-start | bytes 6291464 | tf_op jit(solution)/shard_map/parts_inward/ppermute | solution.py:83
  141.3 3.8 %collective-permute-start.17 = (f32[16,256]{1,0:T(8,128)S(1)}, f32[16,256]{1,0:T(8,128)S(1)}, u32[]{:S(2)}, u32[]{:S(2)}) collective-permute-start(f32[16,256]{1,0:T(8,128)S(1)} %get-tuple-element.114.chosen_ref), channel_id=1, source_target_pairs={{0,16},{16,0},{1,17},{17,1},{2,18},{18,2},{3,19},{19,3},{4,20},{20... | collective-permute-start | bytes 49160 | tf_op jit(solution)/shard_map/sums_2/ppermute | solution.py:340
  149.8 7.4 %collective-permute-start.18 = (bf16[64,4096]{1,0:T(8,128)(2,1)S(1)}, bf16[64,4096]{1,0:T(8,128)(2,1)S(1)}, u32[]{:S(2)}, u32[]{:S(2)}) collective-permute-start(bf16[64,4096]{1,0:T(8,128)(2,1)S(1)} %get-tuple-element.117), channel_id=1, source_target_pairs={{0,1},{1,0},{2,3},{3,2},{4,5},{5,4},{6,7},{7,6},{8,9},{9,8},{10,11... | collective-permute-start | bytes 1572872 | tf_op jit(solution)/shard_map/back_2_1/ppermute | solution.py:83
  158.4 15.3 %collective-permute-start.19 = (bf16[64,4224]{1,0:T(8,128)(2,1)S(1)}, bf16[64,4224]{1,0:T(8,128)(2,1)S(1)}, u32[]{:S(2)}, u32[]{:S(2)}) collective-permute-start(bf16[64,4224]{1,0:T(8,128)(2,1)S(1)} %get-tuple-element.123), channel_id=1, source_target_pairs={{0,2},{1,3},{2,0},{3,1},{4,6},{5,7},{6,4},{7,5},{8,10},{9,11},{10,... | collective-permute-start | bytes 1622024 | tf_op jit(solution)/shard_map/out_3_2/ppermute | solution.py:83
  159.9 15.2 %collective-permute-start.20 = (bf16[64,4224]{1,0:T(8,128)(2,1)S(1)}, bf16[64,4224]{1,0:T(8,128)(2,1)S(1)}, u32[]{:S(2)}, u32[]{:S(2)}) collective-permute-start(bf16[64,4224]{1,0:T(8,128)(2,1)S(1)} %get-tuple-element.124), channel_id=1, source_target_pairs={{0,1},{1,0},{2,3},{3,2},{4,5},{5,4},{6,7},{7,6},{8,9},{9,8},{10,11... | collective-permute-start | bytes 1622024 | tf_op jit(solution)/shard_map/out_3_1/ppermute | solution.py:83
  159.9 63.6 %collective-permute-start.21 = (bf16[256,4096]{1,0:T(8,128)(2,1)S(1)}, bf16[256,4096]{1,0:T(8,128)(2,1)S(1)}, u32[]{:S(2)}, u32[]{:S(2)}) collective-permute-start(bf16[256,4096]{1,0:T(8,128)(2,1)S(1)} %decode.5), channel_id=1, source_target_pairs={{4,0},{5,1},{6,2},{7,3},{8,12},{9,13},{10,14},{11,15},{20,16},{21,... | collective-permute-start | bytes 6291464 | tf_op jit(solution)/shard_map/parts_outward/ppermute | solution.py:83
  161.2 23.0 %collective-permute-start.22 = (bf16[64,4224]{1,0:T(8,128)(2,1)S(1)}, bf16[64,4224]{1,0:T(8,128)(2,1)S(1)}, u32[]{:S(2)}, u32[]{:S(2)}) collective-permute-start(bf16[64,4224]{1,0:T(8,128)(2,1)S(1)} %get-tuple-element.131), channel_id=1, source_target_pairs={{0,3},{1,2},{2,1},{3,0},{4,7},{5,6},{6,5},{7,4},{8,11},{9,10},{10,... | collective-permute-start | bytes 1622024 | tf_op jit(solution)/shard_map/out_3_3/ppermute | solution.py:83
  173.6 23.3 %collective-permute-start.25 = (bf16[64,4096]{1,0:T(8,128)(2,1)S(1)}, bf16[64,4096]{1,0:T(8,128)(2,1)S(1)}, u32[]{:S(2)}, u32[]{:S(2)}) collective-permute-start(bf16[64,4096]{1,0:T(8,128)(2,1)S(1)} %get-tuple-element.118), channel_id=1, source_target_pairs={{0,2},{1,3},{2,0},{3,1},{4,6},{5,7},{6,4},{7,5},{8,10},{9,11},{10,... | collective-permute-start | bytes 1572872 | tf_op jit(solution)/shard_map/back_2_2/ppermute | solution.py:83
  175.1 27.7 %collective-permute-start.26 = (bf16[64,4096]{1,0:T(8,128)(2,1)S(1)}, bf16[64,4096]{1,0:T(8,128)(2,1)S(1)}, u32[]{:S(2)}, u32[]{:S(2)}) collective-permute-start(bf16[64,4096]{1,0:T(8,128)(2,1)S(1)} %get-tuple-element.119), channel_id=1, source_target_pairs={{0,3},{1,2},{2,1},{3,0},{4,7},{5,6},{6,5},{7,4},{8,11},{9,10},{10,... | collective-permute-start | bytes 1572872 | tf_op jit(solution)/shard_map/back_2_3/ppermute | solution.py:83
  188.4 3.8 %collective-permute-start.23 = (f32[16,256]{1,0:T(8,128)S(1)}, f32[16,256]{1,0:T(8,128)S(1)}, u32[]{:S(2)}, u32[]{:S(2)}) collective-permute-start(f32[16,256]{1,0:T(8,128)S(1)} %get-tuple-element.133.chosen_ref), channel_id=1, source_target_pairs={{0,16},{16,0},{1,17},{17,1},{2,18},{18,2},{3,19},{19,3},{4,20},{20... | collective-permute-start | bytes 49160 | tf_op jit(solution)/shard_map/sums_3/ppermute | solution.py:340
  203.6 27.0 %collective-permute-start.29 = (bf16[256,2048]{1,0:T(8,128)(2,1)S(1)}, bf16[256,2048]{1,0:T(8,128)(2,1)S(1)}, u32[]{:S(2)}, u32[]{:S(2)}) collective-permute-start(bf16[256,2048]{1,0:T(8,128)(2,1)S(1)} %combine.5), channel_id=1, source_target_pairs={{0,4},{1,5},{2,6},{3,7},{12,8},{13,9},{14,10},{15,11},{16,20},{17,... | collective-permute-start | bytes 3145736 | tf_op jit(solution)/shard_map/sum_inward_two_0/ppermute | solution.py:83
  207.3 14.8 %collective-permute-start.24 = (bf16[64,4096]{1,0:T(8,128)(2,1)S(1)}, bf16[64,4096]{1,0:T(8,128)(2,1)S(1)}, u32[]{:S(2)}, u32[]{:S(2)}) collective-permute-start(bf16[64,4096]{1,0:T(8,128)(2,1)S(1)} %get-tuple-element.135), channel_id=1, source_target_pairs={{0,2},{1,3},{2,0},{3,1},{4,6},{5,7},{6,4},{7,5},{8,10},{9,11},{10,... | collective-permute-start | bytes 1572872 | tf_op jit(solution)/shard_map/back_3_2/ppermute | solution.py:83
  207.9 24.1 %collective-permute-start.27 = (bf16[64,4096]{1,0:T(8,128)(2,1)S(1)}, bf16[64,4096]{1,0:T(8,128)(2,1)S(1)}, u32[]{:S(2)}, u32[]{:S(2)}) collective-permute-start(bf16[64,4096]{1,0:T(8,128)(2,1)S(1)} %get-tuple-element.138), channel_id=1, source_target_pairs={{0,1},{1,0},{2,3},{3,2},{4,5},{5,4},{6,7},{7,6},{8,9},{9,8},{10,11... | collective-permute-start | bytes 1572872 | tf_op jit(solution)/shard_map/back_3_1/ppermute | solution.py:83
  209.1 23.5 %collective-permute-start.28 = (bf16[64,4096]{1,0:T(8,128)(2,1)S(1)}, bf16[64,4096]{1,0:T(8,128)(2,1)S(1)}, u32[]{:S(2)}, u32[]{:S(2)}) collective-permute-start(bf16[64,4096]{1,0:T(8,128)(2,1)S(1)} %get-tuple-element.139), channel_id=1, source_target_pairs={{0,3},{1,2},{2,1},{3,0},{4,7},{5,6},{6,5},{7,4},{8,11},{9,10},{10,... | collective-permute-start | bytes 1572872 | tf_op jit(solution)/shard_map/back_3_3/ppermute | solution.py:83
  222.1 30.9 %collective-permute-start.33 = (bf16[256,2048]{1,0:T(8,128)(2,1)S(1)}, bf16[256,2048]{1,0:T(8,128)(2,1)S(1)}, u32[]{:S(2)}, u32[]{:S(2)}) collective-permute-start(bf16[256,2048]{1,0:T(8,128)(2,1)S(1)} %combine.6), channel_id=1, source_target_pairs={{0,4},{1,5},{2,6},{3,7},{12,8},{13,9},{14,10},{15,11},{16,20},{17,... | collective-permute-start | bytes 3145736 | tf_op jit(solution)/shard_map/sum_inward_two_1/ppermute | solution.py:83
  230.9 23.2 %collective-permute-start.37 = (bf16[256,2048]{1,0:T(8,128)(2,1)S(1)}, bf16[256,2048]{1,0:T(8,128)(2,1)S(1)}, u32[]{:S(2)}, u32[]{:S(2)}) collective-permute-start(bf16[256,2048]{1,0:T(8,128)(2,1)S(1)} %add_convert_fusion.2), channel_id=1, source_target_pairs={{4,8},{5,9},{6,10},{7,11},{8,4},{9,5},{10,6},{11,7},{20,24},{21,25... | collective-permute-start | bytes 3145736 | tf_op jit(solution)/shard_map/sum_middle_two_0/ppermute | solution.py:83
  232.7 37.1 %collective-permute-start.36 = (bf16[128,4096]{1,0:T(8,128)(2,1)S(1)}, bf16[128,4096]{1,0:T(8,128)(2,1)S(1)}, u32[]{:S(2)}, u32[]{:S(2)}) collective-permute-start(bf16[128,4096]{1,0:T(8,128)(2,1)S(1)} %pad_maximum_fusion.2), channel_id=1, source_target_pairs={{0,2},{1,3},{2,0},{3,1},{4,6},{5,7},{6,4},{7,5},{8,10},{9,11},{10,... | collective-permute-start | bytes 3145736 | tf_op jit(solution)/shard_map/back_near_2/ppermute | solution.py:83
  234.9 34.9 %collective-permute-start.35 = (bf16[256,1536]{1,0:T(8,128)(2,1)S(1)}, bf16[256,1536]{1,0:T(8,128)(2,1)S(1)}, u32[]{:S(2)}, u32[]{:S(2)}) collective-permute-start(bf16[256,1536]{1,0:T(8,128)(2,1)S(1)} %combine.8), channel_id=1, source_target_pairs={{0,4},{1,5},{2,6},{3,7},{12,8},{13,9},{14,10},{15,11},{16,20},{17,... | collective-permute-start | bytes 2359304 | tf_op jit(solution)/shard_map/sum_inward_far_0/ppermute | solution.py:83
  241.7 56.1 %collective-permute-start.31 = (bf16[256,2560]{1,0:T(8,128)(2,1)S(1)}, bf16[256,2560]{1,0:T(8,128)(2,1)S(1)}, u32[]{:S(2)}, u32[]{:S(2)}) collective-permute-start(bf16[256,2560]{1,0:T(8,128)(2,1)S(1)} %combine.7), channel_id=1, source_target_pairs={{0,4},{1,5},{2,6},{3,7},{12,8},{13,9},{14,10},{15,11},{16,20},{17,... | collective-permute-start | bytes 3932168 | tf_op jit(solution)/shard_map/sum_inward_far_1/ppermute | solution.py:83
  253.4 18.0 %collective-permute-start.34 = (bf16[256,2048]{1,0:T(8,128)(2,1)S(1)}, bf16[256,2048]{1,0:T(8,128)(2,1)S(1)}, u32[]{:S(2)}, u32[]{:S(2)}) collective-permute-start(bf16[256,2048]{1,0:T(8,128)(2,1)S(1)} %add_convert_fusion.3), channel_id=1, source_target_pairs={{4,8},{5,9},{6,10},{7,11},{8,4},{9,5},{10,6},{11,7},{20,24},{21,25... | collective-permute-start | bytes 3145736 | tf_op jit(solution)/shard_map/sum_middle_two_1/ppermute | solution.py:83
  254.1 25.6 %collective-permute-start.32 = (bf16[128,4096]{1,0:T(8,128)(2,1)S(1)}, bf16[128,4096]{1,0:T(8,128)(2,1)S(1)}, u32[]{:S(2)}, u32[]{:S(2)}) collective-permute-start(bf16[128,4096]{1,0:T(8,128)(2,1)S(1)} %pad_maximum_fusion.3), channel_id=1, source_target_pairs={{0,3},{1,2},{2,1},{3,0},{4,7},{5,6},{6,5},{7,4},{8,11},{9,10},{10,... | collective-permute-start | bytes 3145736 | tf_op jit(solution)/shard_map/back_near_3/ppermute | solution.py:83
  270.0 28.9 %collective-permute-start.38 = (bf16[256,1536]{1,0:T(8,128)(2,1)S(1)}, bf16[256,1536]{1,0:T(8,128)(2,1)S(1)}, u32[]{:S(2)}, u32[]{:S(2)}) collective-permute-start(bf16[256,1536]{1,0:T(8,128)(2,1)S(1)} %add_convert_fusion.4), channel_id=1, source_target_pairs={{4,12},{5,13},{6,14},{7,15},{8,0},{9,1},{10,2},{11,3},{20,28},{21,... | collective-permute-start | bytes 2359304 | tf_op jit(solution)/shard_map/sum_skip_far_0/ppermute | solution.py:83
  299.2 32.6 %collective-permute-start.39 = (bf16[256,2560]{1,0:T(8,128)(2,1)S(1)}, bf16[256,2560]{1,0:T(8,128)(2,1)S(1)}, u32[]{:S(2)}, u32[]{:S(2)}) collective-permute-start(bf16[256,2560]{1,0:T(8,128)(2,1)S(1)} %add_convert_fusion.1), channel_id=1, source_target_pairs={{4,12},{5,13},{6,14},{7,15},{8,0},{9,1},{10,2},{11,3},{20,28},{21,... | collective-permute-start | bytes 3932168 | tf_op jit(solution)/shard_map/sum_skip_far_1/ppermute | solution.py:83
  300.5 2.7 collective-permute-start.30
